TPU v7x, 128 devices: a whole 4x4x4 slice. The times are simulated.
128 devices in a mesh: sx: 8 (over x, z_lo), sy: 16 (over y, z_hi, core).
Axes of the slice: x: 4, y: 4, z: 4 (z_hi: 2, z_lo: 2; z = z_hi * 2 + z_lo), core: 2. Of those that a mesh axis runs over, the one named last changes fastest.
Arguments:
- text_tokens: bfloat16 [16, 32, 4096], P('sy', 'sx'), may hold values from -2.5 to 2.5
- latent: bfloat16 [16, 16, 512], P('sy', 'sx'), may hold values from -6 to 6
- image_offset: int32 [16], P('sy'), may hold values from 0 to 32
- norm_gain: bfloat16 [4096], replicated, may hold values from 0.099609375 to 1.8984375
- w_query: bfloat16 [4096, 4096], P(None, 'sx')
- w_key: bfloat16 [4096, 4096], P(None, 'sx')
- w_value: bfloat16 [4096, 4096], P(None, 'sx'), may hold values from -0.09375 to 0.09375
- w_out: bfloat16 [4096, 4096], P('sx'), may hold values from -0.09375 to 0.09375
- w_down_conv: bfloat16 [288, 128], replicated, may hold values from -0.375 to 0.375
- w_down_proj: bfloat16 [128, 4096], replicated, may hold values from -0.5 to 0.5
- w_up_proj: bfloat16 [4096, 128], replicated, may hold values from -0.09375 to 0.09375
- w_up_out: bfloat16 [128, 32], replicated, may hold values from -0.5 to 0.5
- pred_grad: bfloat16 [16, 16, 512], P('sy', 'sx'), may hold values from -0.8984375 to 0.8984375
- text_grad: bfloat16 [16, 32, 4096], P('sy', 'sx'), may hold values from -0.29882812 to 0.29882812
Outputs:
- prediction: bfloat16 [16, 16, 512], P('sy', 'sx')
- text_out: bfloat16 [16, 32, 4096], P('sy', 'sx')
- grad_down_conv: float32 [288, 128], replicated
- grad_down_proj: float32 [128, 4096], replicated
- grad_up_proj: float32 [4096, 128], replicated
- grad_up_out: float32 [128, 32], replicated
All inputs are finite; a program needn't handle non-finite values.
Results may differ from a plain program's by a relative error of at most 0.028.
Values may be sent and summed in bfloat16 or wider, within the bound.
A program may use at most 192 MiB of HBM per device.

v0:
```python
import math

import jax
import jax.numpy as jnp
from jax import lax
from jax.sharding import PartitionSpec as P

HD = 128


epsilon = 1e-05
NEG_SCORE = -1e30
rope_base = 500000.0


def with_halo(block, sides, width):
    for axis, dim in sides:
        count = lax.axis_size(axis)
        forward = [(i, i + 1) for i in range(count - 1)]
        backward = [(target, source) for source, target in forward]
        low = lax.ppermute(
            lax.slice_in_dim(block, block.shape[dim] - width, None, axis=dim), axis, forward
        )
        high = lax.ppermute(lax.slice_in_dim(block, 0, width, axis=dim), axis, backward)
        block = jnp.concatenate([low, block, high], axis=dim)
    return block


def silu_slope(values):
    sigma = jax.nn.sigmoid(values)
    return sigma * (1.0 + values * (1.0 - sigma))


def neighbour_cells(padded, rows, cols):
    wide = jnp.pad(padded, ((0, 0), (1, 1), (0, 0)))
    parts = [wide[r : r + rows, c : c + cols, :] for r in range(3) for c in range(3)]
    return jnp.concatenate(parts, axis=-1)


def rope_tables(positions, head_size):
    half = head_size // 2
    freq = jnp.exp(-(2.0 * jnp.arange(half, dtype=jnp.float32) / head_size) * math.log(rope_base))
    angle = positions.astype(jnp.float32)[:, None] * freq[None, :]
    return (jnp.cos(angle)[:, None, :], jnp.sin(angle)[:, None, :])


def rotate(values, cosine, sine):
    half = values.shape[-1] // 2
    first = values[..., :half]
    second = values[..., half:]
    return jnp.concatenate(
        [first * cosine - second * sine, second * cosine + first * sine], axis=-1
    )


def shards(
    text_tokens,
    latent,
    image_offset,
    norm_gain,
    w_query,
    w_key,
    w_value,
    w_out,
    w_down_conv,
    w_down_proj,
    w_up_proj,
    w_up_out,
    pred_grad,
    text_grad,
):
    wide_type = jnp.float32
    text_local = text_tokens[0]
    latent_tile = latent[0]
    offset = image_offset[0]
    lat_chan = w_up_out.shape[1]
    text_rows = text_local.shape[0]
    tile_rows = latent_tile.shape[0]
    tile_cols = latent_tile.shape[1] // lat_chan
    image_rows = tile_rows * tile_cols
    share_rows = text_rows + image_rows
    row_groups = lax.axis_size("sx")
    seq_blocks = lax.axis_size("sy")
    block_len = share_rows * row_groups
    image_len = image_rows * row_groups
    total_len = block_len * seq_blocks
    own_block = lax.axis_index("sy")
    head_width = w_query.shape[1]
    heads_here = head_width // HD
    score_scale = HD ** (-0.5)
    rimmed = with_halo(latent_tile, (("sx", 0),), 1)
    grid_cells = rimmed.reshape(tile_rows + 2, tile_cols, lat_chan)
    patches = neighbour_cells(grid_cells, tile_rows, tile_cols).reshape(image_rows, 9 * lat_chan)
    pre_down = jnp.dot(patches, w_down_conv, preferred_element_type=wide_type)
    down_act = jax.nn.silu(pre_down).astype(jnp.bfloat16)
    embedded = jnp.dot(down_act, w_down_proj, preferred_element_type=wide_type).astype(jnp.bfloat16)
    local_rows = jnp.concatenate([text_local, embedded], axis=0)
    gain = norm_gain.astype(wide_type)
    w_project = jnp.concatenate([w_query, w_key, w_value], axis=1)
    inputs = lax.all_gather(local_rows, "sx", axis=0, tiled=True).astype(wide_type)
    inverse = lax.rsqrt(jnp.mean(inputs * inputs, axis=-1, keepdims=True) + epsilon)
    normed = (inputs * inverse * gain).astype(jnp.bfloat16)
    projected = jnp.dot(normed, w_project, preferred_element_type=wide_type)

    def layout(row_ids):
        part_index = row_ids // share_rows
        inner_row = row_ids % share_rows
        is_image = inner_row >= text_rows
        text_index = part_index * text_rows + inner_row
        text_pos = text_index + jnp.where(text_index >= offset, image_len, 0)
        image_pos = offset + part_index * image_rows + (inner_row - text_rows)
        return (jnp.where(is_image, image_pos, text_pos), is_image)

    query_pos, query_image = layout(jnp.arange(block_len, dtype=jnp.int32))
    cosine, sine = rope_tables(own_block * block_len + query_pos, HD)
    queries = rotate(
        projected[:, :head_width].reshape(block_len, heads_here, HD), cosine, sine
    ).astype(jnp.bfloat16)
    keys_turned = (
        rotate(
            projected[:, head_width : 2 * head_width].reshape(block_len, heads_here, HD),
            cosine,
            sine,
        )
        .astype(jnp.bfloat16)
        .reshape(block_len, head_width)
    )
    keys_values = jnp.concatenate(
        [keys_turned, projected[:, 2 * head_width :].astype(jnp.bfloat16)], axis=1
    )

    def visible(key_ids):
        key_block = key_ids // block_len
        key_pos, key_image = layout(key_ids % block_len)
        same = (key_block == own_block)[None, :] & (
            (key_pos[None, :] <= query_pos[:, None]) | key_image[None, :] & query_image[:, None]
        )
        return (key_block < own_block)[None, :] | same

    def stats_keys(running, shard_piece, first_row):
        peak, total = running
        count_rows = shard_piece.shape[0]
        key_heads = shard_piece[:, :head_width].reshape(count_rows, heads_here, HD)
        allowed = visible(first_row + jnp.arange(count_rows, dtype=jnp.int32))
        scores = (
            jnp.einsum("qhd,khd->hqk", queries, key_heads, preferred_element_type=wide_type)
            * score_scale
        )
        scores = jnp.where(allowed[None], scores, NEG_SCORE)
        new_peak = jnp.maximum(peak, jnp.max(scores, axis=-1))
        raised = jnp.where(allowed[None], jnp.exp(scores - new_peak[:, :, None]), 0.0)
        total = total * jnp.exp(peak - new_peak) + jnp.sum(raised, axis=-1)
        return (new_peak, total)

    def stats_visible(running, shard_piece, first_row):
        return stats_keys(running, shard_piece, first_row)

    key_step = math.gcd(total_len, 512)
    slab_count = total_len // key_step
    start_state = (
        jnp.full((heads_here, block_len), NEG_SCORE, wide_type),
        jnp.zeros((heads_here, block_len), wide_type),
    )
    every_key = lax.all_gather(keys_values, "sy", axis=0, tiled=True)

    def stats_turn(index, running):
        first_row = index * key_step
        return stats_visible(
            running, lax.dynamic_slice_in_dim(every_key, first_row, key_step, 0), first_row
        )

    peak, total = lax.fori_loop(0, slab_count, stats_turn, start_state)
    log_total = peak + jnp.log(total)

    def mix_keys(accum, shard_piece, first_row):
        key_heads = shard_piece[:, :head_width].reshape(key_step, heads_here, HD)
        value_heads = shard_piece[:, head_width:].reshape(key_step, heads_here, HD)
        allowed = visible(first_row + jnp.arange(key_step, dtype=jnp.int32))
        scores = (
            jnp.einsum("qhd,khd->hqk", queries, key_heads, preferred_element_type=wide_type)
            * score_scale
        )
        scores = jnp.where(allowed[None], scores, NEG_SCORE)
        probs = jnp.where(allowed[None], jnp.exp(scores - log_total[:, :, None]), 0.0)
        return accum + jnp.einsum(
            "hqk,khd->qhd",
            probs.astype(jnp.bfloat16),
            value_heads,
            preferred_element_type=wide_type,
        )

    def mix_turn(index, accum):
        first_row = index * key_step
        shard_piece = lax.dynamic_slice_in_dim(every_key, first_row, key_step, 0)
        return mix_keys(accum, shard_piece, first_row)

    accum = lax.fori_loop(
        0, slab_count, mix_turn, jnp.zeros((block_len, heads_here, HD), wide_type)
    )
    attended = accum.astype(jnp.bfloat16).reshape(block_len, head_width)
    rows_here = attended
    mixed_rows = lax.psum_scatter(
        jnp.dot(rows_here, w_out, preferred_element_type=wide_type).astype(jnp.bfloat16),
        "sx",
        scatter_dimension=0,
        tiled=True,
    ).astype(jnp.float32)
    layer_out = (local_rows.astype(wide_type) + mixed_rows).astype(jnp.bfloat16)
    text_out = layer_out[:text_rows]
    image_out = layer_out[text_rows:]
    pre_up = jnp.dot(image_out, w_up_proj, preferred_element_type=wide_type)
    up_act = jax.nn.silu(pre_up).astype(jnp.bfloat16)
    prediction = (
        jnp.dot(up_act, w_up_out, preferred_element_type=wide_type)
        .astype(jnp.bfloat16)
        .reshape(tile_rows, tile_cols * lat_chan)
    )
    out_grad = pred_grad[0].reshape(image_rows, lat_chan)
    grad_up_out = jnp.einsum("ru,rc->uc", up_act, out_grad, preferred_element_type=wide_type)
    grad_pre_up = (
        jnp.einsum("rc,uc->ru", out_grad, w_up_out, preferred_element_type=wide_type)
        * silu_slope(pre_up)
    ).astype(jnp.bfloat16)
    grad_up_proj = jnp.einsum("rd,ru->du", image_out, grad_pre_up, preferred_element_type=wide_type)
    grad_image = jnp.einsum("ru,du->rd", grad_pre_up, w_up_proj, preferred_element_type=wide_type)
    grad_rows = jnp.concatenate([text_grad[0].astype(wide_type), grad_image], axis=0).astype(
        jnp.bfloat16
    )
    grad_attended = jnp.einsum(
        "rd,hd->rh",
        lax.all_gather(grad_rows, "sx", axis=0, tiled=True),
        w_out,
        preferred_element_type=wide_type,
    ).astype(jnp.bfloat16)
    grad_heads = grad_attended.reshape(block_len, heads_here, HD)
    delta = jnp.einsum(
        "qhd,qhd->hq",
        grad_heads,
        attended.reshape(block_len, heads_here, HD),
        preferred_element_type=wide_type,
    )

    def back_keys(query_sum, shard_piece, first_row):
        key_heads = shard_piece[:, :head_width].reshape(key_step, heads_here, HD)
        value_heads = shard_piece[:, head_width:].reshape(key_step, heads_here, HD)
        allowed = visible(first_row + jnp.arange(key_step, dtype=jnp.int32))
        scores = (
            jnp.einsum("qhd,khd->hqk", queries, key_heads, preferred_element_type=wide_type)
            * score_scale
        )
        scores = jnp.where(allowed[None], scores, NEG_SCORE)
        probs = jnp.where(allowed[None], jnp.exp(scores - log_total[:, :, None]), 0.0)
        weights = probs.astype(jnp.bfloat16)
        grad_prob = jnp.einsum(
            "qhd,khd->hqk", grad_heads, value_heads, preferred_element_type=wide_type
        )
        grad_score = (probs * (grad_prob - delta[:, :, None]) * score_scale).astype(jnp.bfloat16)
        query_sum = query_sum + jnp.einsum(
            "hqk,khd->qhd", grad_score, key_heads, preferred_element_type=wide_type
        )
        key_part = jnp.einsum(
            "hqk,qhd->khd", grad_score, queries, preferred_element_type=wide_type
        ).astype(jnp.bfloat16)
        value_part = jnp.einsum(
            "hqk,qhd->khd", weights, grad_heads, preferred_element_type=wide_type
        ).astype(jnp.bfloat16)
        return (
            query_sum,
            jnp.concatenate(
                [key_part.reshape(key_step, head_width), value_part.reshape(key_step, head_width)],
                axis=1,
            ),
        )

    def back_turn(query_sum, index):
        first_row = index * key_step
        shard_piece = lax.dynamic_slice_in_dim(every_key, first_row, key_step, 0)
        return back_keys(query_sum, shard_piece, first_row)

    query_sum, key_pieces = lax.scan(
        back_turn,
        jnp.zeros((block_len, heads_here, HD), wide_type),
        jnp.arange(slab_count, dtype=jnp.int32),
    )
    grads_term = key_pieces.reshape(total_len, 2 * head_width)
    own_sums = lax.psum_scatter(
        grads_term.astype(wide_type).astype(jnp.bfloat16), "sy", scatter_dimension=0, tiled=True
    ).astype(jnp.float32)
    grad_query = (
        rotate(query_sum, cosine, -sine).astype(jnp.bfloat16).reshape(block_len, head_width)
    )
    grad_key = (
        rotate(own_sums[:, :head_width].reshape(block_len, heads_here, HD), cosine, -sine)
        .astype(jnp.bfloat16)
        .reshape(block_len, head_width)
    )
    grad_value = own_sums[:, head_width:].astype(jnp.bfloat16)
    head_grads = jnp.concatenate([grad_query, grad_key, grad_value], axis=1)
    rows_here = head_grads
    grad_normed = lax.psum_scatter(
        jnp.einsum("rh,dh->rd", rows_here, w_project, preferred_element_type=wide_type).astype(
            jnp.bfloat16
        ),
        "sx",
        scatter_dimension=0,
        tiled=True,
    ).astype(jnp.float32)
    inputs = local_rows.astype(wide_type)
    inverse = lax.rsqrt(jnp.mean(inputs * inputs, axis=-1, keepdims=True) + epsilon)
    scaled = grad_normed * gain
    grad_in = (
        grad_rows.astype(wide_type)
        + inverse * scaled
        - inputs * inverse**3 * jnp.mean(inputs * scaled, axis=-1, keepdims=True)
    )
    grad_embedded = grad_in[text_rows:].astype(jnp.bfloat16)
    grad_down_proj = jnp.einsum(
        "ru,rd->ud", down_act, grad_embedded, preferred_element_type=wide_type
    )
    grad_pre_down = (
        jnp.einsum("rd,ud->ru", grad_embedded, w_down_proj, preferred_element_type=wide_type)
        * silu_slope(pre_down)
    ).astype(jnp.bfloat16)
    grad_down_conv = jnp.einsum(
        "rc,ru->cu", patches, grad_pre_down, preferred_element_type=wide_type
    )
    weight_sums = lax.psum(
        (grad_down_conv, grad_down_proj, grad_up_proj, grad_up_out), ("sx", "sy")
    )
    return (
        prediction[None],
        text_out[None],
        weight_sums[0],
        weight_sums[1],
        weight_sums[2],
        weight_sums[3],
    )


def solution(mesh):
    placed = (
        P("sy", "sx", None),
        P("sy", "sx", None),
        P("sy"),
        P(),
        P(None, "sx"),
        P(None, "sx"),
        P(None, "sx"),
        P("sx", None),
        P(),
        P(),
        P(),
        P(),
        P("sy", "sx", None),
        P("sy", "sx", None),
    )
    return jax.shard_map(
        shards,
        mesh=mesh,
        in_specs=placed,
        out_specs=(P("sy", "sx", None), P("sy", "sx", None), P(), P(), P(), P()),
        check_vma=False,
    )
```

profile of v0, /device:TPU:1, one launch (start us, length us, event | category | flops | bytes accessed | tf_op | source)
XLA Modules:
  0.0 917.8 jit_solution(17023266584406782388)
XLA Ops:
  8.0 4.4 collective-permute-start
  19.0 1.8 fusion.123
  22.9 4.7 constant_dynamic-update-slice_fusion.3
  27.6 2.4 constant_dynamic-update-slice_fusion.2
  31.3 2.4 constant_dynamic-update-slice_fusion.1
  33.7 50.8 %all-gather.8.cloned.1.call-done = bf16[8,36,4096]{2,1,0:T(8,128)(2,1)} async-done(((bf16[1,36,4096]{2,1,0:T(8,128)(2,1)}), bf16[8,36,4096]{2,1,0:T(8,128)(2,1)}) %all-gather.8.cloned.1.call-update) | async-done | bytes 2359312 | tf_op jit(solution)/shard_map/all_gather | solution.py:100
  84.5 4.5 reshape.707
  89.0 2.9 multiply_reduce_fusion
  92.7 7.2 fusion.77
  100.5 2.5 subtract_convert_fusion.2
  105.6 78.3 %all-gather.6.cloned.1.call-done = bf16[4608,1024]{1,0:T(8,128)(2,1)} async-done(((bf16[288,1024]{1,0:T(8,128)(2,1)}), bf16[4608,1024]{1,0:T(8,128)(2,1)}) %all-gather.6.cloned.1.call-update) | async-done | bytes 9437200 | tf_op jit(solution)/shard_map/all_gather | solution.py:164
  183.9 12.7 %copy.66 = bf16[4608,1024]{0,1:T(8,128)(2,1)} copy(bf16[4608,1024]{1,0:T(8,128)(2,1)} %all-gather.6.cloned.1.call-done) | data formatting | bytes 18874368
  196.6 47.8 %while.58 = (s32[]{:T(128)}, f32[4,288]{1,0:T(4,128)S(1)}, f32[4,288]{1,0:T(4,128)S(1)}, s32[]{:T(128)}, s32[]{:T(128)}, /*index=5*/bf16[4608,1024]{0,1:T(8,128)...) while((s32[]{:T(128)}, f32[4,288]{1,0:T(4,128)S(1)}, ...), condition=%wide.region_4.5_spmd.clone.clone.clone, body=%wide.region_1.4_spmd.clone.clone.clone.sunk | while | flops 156493376 | bytes 7098890 | solution.py:172
  209.9 1.6 fusion.195
  215.2 1.6 fusion.195
  220.5 1.6 fusion.195
  225.9 1.6 fusion.195
  241.8 1.6 fusion.195
  244.4 45.8 %while.59 = (s32[]{:T(128)}, f32[288,4,128]{2,0,1:T(8,128)S(1)}, bf16[4608,1024]{0,1:T(8,128)(2,1)}, s32[]{:T(128)}, s32[]{:T(128)}, /*index=5*/bf16[288,4,128]{...) while((s32[]{:T(128)}, f32[288,4,128]{2,0,1:T(8,128)S(1)}, ...), condition=%wide.region_6.7_spmd.clone.clone.clone, body=%wide.region_5.6_spmd.clone.clone.clone.sunk | while | flops 306008000 | bytes 4930081 | solution.py:197
  247.3 2.1 fusion.202
  252.4 2.1 fusion.202
  257.5 2.1 fusion.202
  262.6 2.1 fusion.202
  267.7 2.1 fusion.202
  272.8 2.1 fusion.202
  277.8 2.1 fusion.202
  282.9 2.1 fusion.202
  288.0 2.1 fusion.202
  291.0 3.8 convolution_convert_fusion.3
  294.8 55.9 %fusion.12 = bf16[40,4096]{1,0:T(8,128)(2,1)} fusion(bf16[288,4096]{1,0:T(8,128)(2,1)S(1)} %convolution_convert_fusion.3), kind=kCustom, calls=%all-reduce-scatter | all-reduce-scatter fusion | flops 1310721 | bytes 2687488
  351.8 1.7 collective-permute-start.2
  354.8 1.9 collective-permute-done.2
  356.8 2.1 concatenate.105
  363.0 66.7 %all-gather.10.cloned.1.call-done = bf16[8,36,4096]{2,1,0:T(8,128)(2,1)} async-done(((bf16[1,36,4096]{2,1,0:T(8,128)(2,1)}), bf16[8,36,4096]{2,1,0:T(8,128)(2,1)}) %all-gather.10.cloned.1.call-update) | async-done | bytes 2359312 | tf_op jit(solution)/shard_map/all_gather | solution.py:231
  429.6 2.7 reshape.706
  432.3 3.6 convolution_convert_fusion.6
  438.2 110.9 %while.60 = (s32[]{:T(128)}, f32[288,4,128]{2,0,1:T(8,128)}, bf16[9,512,1024]{2,1,0:T(8,128)(2,1)}, s32[9]{0:T(128)S(1)}, bf16[4608,1024]{0,1:T(8,128)(2,1)}, /*...) while((s32[]{:T(128)}, f32[288,4,128]{2,0,1:T(8,128)}, ...), condition=%wide.region_10.11_spmd.clone.clone.clone, body=%wide.region_9.10_spmd.clone.clone.clone.sunk | while | flops 763973568 | bytes 24300624 | solution.py:280
  442.3 1.7 fusion.216
  453.7 1.8 fusion.216
  456.4 2.4 fusion.218
  466.1 1.7 fusion.216
  468.8 2.4 fusion.218
  478.6 1.8 fusion.216
  481.4 2.4 fusion.218
  491.1 1.8 fusion.216
  493.8 2.4 fusion.218
  503.5 1.8 fusion.216
  506.2 2.4 fusion.218
  515.9 1.8 fusion.216
  518.6 2.4 fusion.218
  528.4 1.8 fusion.216
  531.1 2.4 fusion.218
  540.8 1.7 fusion.216
  543.5 2.4 fusion.218
  550.7 106.8 %reduce-scatter.6.cloned.1.call-done = bf16[288,1024]{1,0:T(8,128)(2,1)} async-done(((bf16[4608,1024]{1,0:T(8,128)(2,1)}), bf16[288,1024]{1,0:T(8,128)(2,1)}) %reduce-scatter.6.cloned.1.call-update) | async-done | bytes 589840 | tf_op jit(solution)/shard_map/reduce_scatter | solution.py:286
  660.6 14.0 %convolution_convert_fusion.2 = bf16[288,4096]{1,0:T(8,128)(2,1)} fusion(bf16[4096,1536]{1,0:T(8,128)(2,1)} %constant_dynamic-update-slice_fusion.1, bf16[288,512]{1,0:T(8,128)(2,1)S(1)} %get-tuple-element.1170, bf16[288,512]{1,0:T(8,128)(2,1)S(1)} %bitcast.222, bf16[288,512]{1,0:T(8,128)(2,1)S(1)} %bitcast.221), kind=kOutput, calls=%fused_computation.144 | convolution fusion | flops 3627712512 | bytes 15826944 | tf_op jit(solution)/shard_map/rh,dh->rd/dot_general | solution.py:301
  674.6 55.6 %fusion.13 = bf16[40,4096]{1,0:T(8,128)(2,1)S(1)} fusion(bf16[288,4096]{1,0:T(8,128)(2,1)} %convolution_convert_fusion.2), kind=kCustom, calls=%all-reduce-scatter.1 | all-reduce-scatter fusion | flops 1310721 | bytes 2687488
  730.2 2.8 collective-permute-start.3
  733.0 1.8 fusion.96
  741.0 1.8 fusion.120
  744.5 71.2 %psum.31 = f32[128,32]{0,1:T(8,128)} all-reduce(f32[128,32]{0,1:T(8,128)S(1)} %fusion.121), channel_id=1, replica_groups=mesh['sx'=8,'sy'=16] {'sx','sy'}, use_global_device_ids=true, to_apply=%region_17.18 | all-reduce | flops 4096 | bytes 32768 | tf_op jit(solution)/shard_map/psum | solution.py:327
  816.3 88.8 %all-reduce.8.cloned.1.call-done = (f32[288,128]{1,0:T(8,128)}, f32[128,4096]{1,0:T(8,128)}, f32[4096,128]{1,0:T(8,128)}) async-done(((f32[288,128]{1,0:T(8,128)}, f32[128,4096]{1,0:T(8,128)}, f32[4096,128]{1,0:T(8,128)}), (f32[288,128]{1,0:T(8,128)}, f32[128,4096]{1,0:T(8,128)}, f32[4096,128]{1,0:T(8,128)})) %all-reduce.8.cloned.1.call-update) | async-done | bytes 4341776 | tf_op jit(solution)/shard_map/psum | solution.py:327
  905.2 1.7 copy.140
  906.9 3.1 copy.141
  (443 shorter events, 171.9 us)
Async XLA Ops:
  7.2 10.9 %copy-start = (bf16[128,4096]{1,0:T(8,128)(2,1)S(1)}, bf16[128,4096]{1,0:T(8,128)(2,1)}, u32[]{:S(2)}) copy-start(bf16[128,4096]{1,0:T(8,128)(2,1)} %param.29) | copy-start | bytes 3145732
  7.2 14.4 %copy-start.27 = (bf16[4096]{0:T(1024)(128)(2,1)S(1)}, bf16[4096]{0:T(1024)(128)(2,1)}, u32[]{:S(2)}) copy-start(bf16[4096]{0:T(1024)(128)(2,1)} %param.23) | copy-start | bytes 24580
  7.2 77.3 %all-gather.8.cloned.1.call-start = ((), (), s32[]{:S(2)}) async-start(), calls=%async_computation.3 | async-start | bytes 2949120 | tf_op jit(solution)/shard_map/all_gather | solution.py:100
  8.0 7.2 collective-permute-start
  12.4 4.3 collective-permute-start.1
  17.0 10.6 %copy-start.23 = (bf16[32,288]{1,0:T(8,128)(2,1)}, bf16[32,288]{1,0:T(8,128)(2,1)S(1)}, u32[]{:S(2)}) copy-start(bf16[32,288]{1,0:T(8,128)(2,1)S(1)} %concatenate.92) | copy-start | bytes 55300
  18.0 2.8 copy-start.21
  18.3 0.7 copy-start.4
  20.8 163.0 %all-gather.6.cloned.1.call-start = ((), (), s32[]{:S(2)}) async-start(), calls=%async_computation.1 | async-start | bytes 10027008 | tf_op jit(solution)/shard_map/all_gather | solution.py:164
  21.6 70.3 %copy-start.26 = (f32[4096]{0:T(1024)}, f32[4096]{0:T(1024)S(1)}, u32[]{:S(2)}) copy-start(f32[4096]{0:T(1024)S(1)} %convert_element_type.140) | copy-start | bytes 49156
  22.9 77.5 %copy-start.12 = (f32[288,64]{1,0:T(8,128)}, f32[288,64]{1,0:T(8,128)S(1)}, u32[]{:S(2)}) copy-start(f32[288,64]{1,0:T(8,128)S(1)} %get-tuple-element.1187) | copy-start | bytes 221188
  22.9 4.7 copy-start.2
  27.6 3.7 copy-start.3
  89.0 3.8 copy-start.1
  102.9 1.5 copy-start.17
  104.3 325.3 %all-gather.10.cloned.1.call-start = ((), (), s32[]{:S(2)}) async-start(), calls=%async_computation.4 | async-start | bytes 2949120 | tf_op jit(solution)/shard_map/all_gather | solution.py:231
  290.2 0.8 copy-start.6
  294.8 58.7 %copy-start.28 = (bf16[1,2,512]{2,1,0:T(2,128)(2,1)S(1)}, bf16[1,2,512]{2,1,0:T(2,128)(2,1)}, u32[]{:S(2)}) copy-start(bf16[1,2,512]{2,1,0:T(2,128)(2,1)} %param.32) | copy-start | bytes 6148
  294.8 58.8 %copy-start.29 = (u32[128]{0:T(128)S(1)}, u32[128]{0:T(128)}, u32[]{:S(2)}) copy-start(u32[128]{0:T(128)} %constant.505) | copy-start | bytes 1540
  294.8 64.1 %copy-start.20 = (bf16[1,4,4096]{2,1,0:T(4,128)(2,1)S(1)}, bf16[1,4,4096]{2,1,0:T(4,128)(2,1)}, u32[]{:S(2)}) copy-start(bf16[1,4,4096]{2,1,0:T(4,128)(2,1)} %param.20) | copy-start | bytes 98308
  350.7 9.3 %copy-start.18 = (bf16[4096,128]{1,0:T(8,128)(2,1)S(1)}, bf16[4096,128]{1,0:T(8,128)(2,1)}, u32[]{:S(2)}) copy-start(bf16[4096,128]{1,0:T(8,128)(2,1)} %param.30) | copy-start | bytes 3145732
  350.7 10.1 %copy-start.30 = (bf16[128,32]{0,1:T(8,128)(2,1)S(1)}, bf16[128,32]{0,1:T(8,128)(2,1)}, u32[]{:S(2)}) copy-start(bf16[128,32]{0,1:T(8,128)(2,1)} %param.31) | copy-start | bytes 24580
  351.8 5.0 collective-permute-start.2
  354.8 7.2 copy-start.25
  360.0 0.7 copy-start.14
  360.8 71.5 %copy-start.32 = (f32[32,128]{1,0:T(8,128)}, f32[32,128]{1,0:T(8,128)S(1)}, u32[]{:S(2)}) copy-start(f32[32,128]{1,0:T(8,128)S(1)} %fusion.98) | copy-start | bytes 49156
  361.4 0.7 copy-start.8
  362.9 294.6 %reduce-scatter.6.cloned.1.call-start = ((), (), s32[]{:S(2)}) async-start(), calls=%async_computation.2 | async-start | bytes 10027008 | tf_op jit(solution)/shard_map/reduce_scatter | solution.py:286
  435.9 0.7 copy-start.16
  436.6 1.2 copy-start.7
  549.1 109.7 %copy-start.13 = (f32[288,64]{1,0:T(8,128)S(1)}, f32[288,64]{1,0:T(8,128)}, u32[]{:S(2)}) copy-start(f32[288,64]{1,0:T(8,128)} %copy-done.12) | copy-start | bytes 221188
  549.1 109.7 %copy-start.19 = (f32[288,64]{1,0:T(8,128)S(1)}, f32[288,64]{1,0:T(8,128)}, u32[]{:S(2)}) copy-start(f32[288,64]{1,0:T(8,128)} %get-tuple-element.1185) | copy-start | bytes 221188
  549.1 356.1 %all-reduce.8.cloned.1.call-start = ((), (), s32[]{:S(2)}) async-start(), calls=%async_computation.5 | async-start | bytes 8683520 | tf_op jit(solution)/shard_map/psum | solution.py:327
  674.6 58.5 %copy-start.15 = (bf16[36,4096]{1,0:T(8,128)(2,1)S(1)}, bf16[36,4096]{1,0:T(8,128)(2,1)}, u32[]{:S(2)}) copy-start(bf16[36,4096]{1,0:T(8,128)(2,1)} %copy-done.14) | copy-start | bytes 884740
  730.1 7.2 copy-start.5
  730.2 8.4 copy-start.9
  730.2 8.4 copy-start.10
  730.2 5.7 collective-permute-start.3
  734.8 4.8 copy-start.22
  734.8 4.8 copy-start.24
  742.8 0.7 copy-start.31
  742.8 0.7 copy-start.33
  905.2 4.8 copy-start.11
Sparse Core Ops, SparseCore 0:
  21.0 63.4 all-gather.7
  104.4 79.3 all-gather.5
  363.0 66.5 all-gather.9
  549.2 108.2 reduce-scatter.5
  742.9 162.1 all-reduce.7
where the time goes:
time: 922 us; the launch traced here: 918 us
  waiting for transfers between devices  396 us (43%)
  blocking collectives  183 us (20%)
  matrix products  127 us (14%)
  local copies, waits for them, and re-layouts  108 us (12%)
  other arithmetic  70.2 us (8%)
  between operations  15.7 us (2%)
  starting transfers between devices  10.3 us (1%)
    unnamed x2, blocking collectives  111 us
    reduce_scatter x1, waiting for transfers between devices, shards(): lax.psum_scatter(grads_term.astype(wide_type).astype(jnp.bfloat16), 'sy',...  107 us
    psum x1, waiting for transfers between devices, shards(): lax.psum((grad_down_conv, grad_down_proj, grad_up_proj, grad_up_out), ('s...  88.8 us
    all_gather x1, waiting for transfers between devices, shards(): every_key = lax.all_gather(keys_values, 'sy', axis=0, tiled=True)  78.3 us
    psum x1, blocking collectives, shards(): lax.psum((grad_down_conv, grad_down_proj, grad_up_proj, grad_up_out), ('s...  71.2 us
    all_gather x1, waiting for transfers between devices, shards(): lax.all_gather(grad_rows, 'sx', axis=0, tiled=True)  66.7 us
    all_gather x1, waiting for transfers between devices, shards(): lax.all_gather(local_rows, 'sx', axis=0, tiled=True).astype(wide_type)  50.8 us
    unnamed x85, local copies, waits for them, and re-layouts  41.2 us
  transfers between devices with their start and end apart: 9, of which 8 were waited for; matrix products, arithmetic and copies ran while one was open for 2% of the time, Pallas kernels for 0%

commit v1 on v0

v1 whole, which is shorter than its diff:
```python
import functools
import math

import jax
import jax.numpy as jnp
import numpy as np
from jax import lax
from jax.experimental import pallas as pl
from jax.experimental.pallas import tpu as pltpu
from jax.sharding import PartitionSpec as P

MESH = pl.DeviceIdType.MESH
F32 = jnp.float32
BF16 = jnp.bfloat16
HD = 128
N_SX = 8
N_SY = 16
SB = 288
TXT = 32
IMG = 256
PH = 16
PW = 16
CH = 32
D = 4096
EPS = 1e-05
NEG = -1e30
LOG2E = math.log2(math.e)
SCALE = HD ** (-0.5)
ROPE_BASE = 500000.0
SIZES = {"sx": 8, "sy": 16, "group": 4, "head": 4, "team": 32, "syhead": 16}
NT = (((1,), (1,)), ((), ()))
TN = (((0,), (0,)), ((), ()))


def dot(a, b, dims=(((1,), (0,)), ((), ()))):
    return lax.dot_general(a, b, dims, preferred_element_type=F32)


def sy_of(g, i):
    return jnp.where(i < 2, 2 * g + i, 12 - 2 * g + i)


def split_sy(sy):
    low = sy < 8
    g = jnp.where(low, sy // 2, (15 - sy) // 2)
    i = sy % 2 + jnp.where(low, 0, 2)
    return g, i


def ring(kind):
    sx = lax.axis_index("sx")
    sy = lax.axis_index("sy")
    g, i = split_sy(sy)
    if kind == "sx":
        return sx, lambda o: ((sx + o) % 8, sy, (sx + o) % 8)
    if kind == "sy":
        return sy, lambda o: (sx, (sy + o) % 16, (sy + o) % 16)
    if kind == "syhead":
        return sy, lambda o: (sx, (sy + o) % 16, split_sy((sy + o) % 16)[1])
    if kind == "group":
        return i, lambda o: (sx, sy_of(g, (i + o) % 4), (i + o) % 4)
    if kind == "head":
        return g, lambda o: (sx, sy_of((g + o) % 4, i), (g + o) % 4)
    e = i * 8 + sx

    def peer(o):
        f = (e + o) % 32
        return f % 8, sy_of(g, f // 8), f

    return e, peer


def greet(kinds):
    barrier = pltpu.get_barrier_semaphore()
    total = 0
    for kind in kinds:
        _, peer = ring(kind)
        for o in range(1, SIZES[kind]):
            tx, ty, _ = peer(o)
            pl.semaphore_signal(barrier, inc=1, device_id=(tx, ty), device_id_type=MESH)
        total += SIZES[kind] - 1
    pl.semaphore_wait(barrier, total)


def exchange_kernel(items, count, *refs):
    ins = refs[:count]
    outs = refs[count : 2 * count]
    local, send, recv = refs[2 * count :]
    kinds = {("sy" if kind == "syhead" else kind): 0 for kind, _ in items}
    greet(kinds)
    copies = []
    at = 0
    for idx, (kind, mode) in enumerate(items):
        slot, peer = ring(kind)
        own_slot = split_sy(lax.axis_index("sy"))[1] if kind == "syhead" else slot
        src = ins[idx] if mode == "gather" else ins[idx].at[own_slot]
        own = pltpu.make_async_copy(src, outs[idx].at[slot], local.at[idx])
        own.start()
        copies.append(own)
        for o in range(1, SIZES[kind]):
            tx, ty, to = peer(o)
            copy = pltpu.make_async_remote_copy(
                src_ref=ins[idx] if mode == "gather" else ins[idx].at[to],
                dst_ref=outs[idx].at[slot],
                send_sem=send.at[at],
                recv_sem=recv.at[at],
                device_id=(tx, ty),
                device_id_type=MESH,
            )
            copy.start()
            copies.append(copy)
            at += 1
    for copy in copies:
        copy.wait()


def exchange(arrays, items, cid):
    shapes = []
    sems = 0
    for array, (kind, mode) in zip(arrays, items):
        sems += SIZES[kind] - 1
        tail = array.shape if mode == "gather" else array.shape[1:]
        shapes.append(jax.ShapeDtypeStruct((SIZES[kind],) + tail, array.dtype))
    return pl.pallas_call(
        functools.partial(exchange_kernel, items, len(arrays)),
        out_shape=shapes,
        in_specs=[pl.BlockSpec(memory_space=pl.ANY)] * len(arrays),
        out_specs=[pl.BlockSpec(memory_space=pl.ANY)] * len(arrays),
        scratch_shapes=[
            pltpu.SemaphoreType.DMA((len(arrays),)),
            pltpu.SemaphoreType.DMA((sems,)),
            pltpu.SemaphoreType.DMA((sems,)),
        ],
        compiler_params=pltpu.CompilerParams(collective_id=cid, has_side_effects=True),
    )(*arrays)


def sigmoid(v):
    return 1.0 / (1.0 + jnp.exp(-v))


def turn(v, cosine, sine):
    return v * cosine + pltpu.roll(v, 64, 1) * sine


def tables(j, phase_ref, base_ref):
    pc = phase_ref[0, pl.ds(j, 1), :]
    ps = phase_ref[1, pl.ds(j, 1), :]
    bc = base_ref[0]
    bs = base_ref[1]
    return pc * bc - ps * bs, ps * bc + pc * bs


def row_scale(da, wd):
    both = dot(da, wd)
    dawd = both[:, :HD] + both[:, HD:]
    mean = jnp.sum(dawd * da.astype(F32), axis=1, keepdims=True) * (1.0 / D)
    return dawd, lax.rsqrt(mean + EPS)


def forward_kernel(
    info,
    lat,
    wconv,
    wd,
    mix,
    wu,
    nt,
    phase,
    base,
    kvt,
    qdt,
    bias_it,
    vis_q,
    bias_tt,
    patches,
    da_ref,
    sp_ref,
    k_ref,
    v_ref,
    q_ref,
    att_ref,
    lse_ref,
    part_ref,
    wide,
    wpad,
    reorder,
):
    g = info[0]
    wpad[...] = jnp.zeros_like(wpad)
    for tap in range(3):
        wpad[tap * 128 : tap * 128 + 96, :] = wconv[tap * 96 : tap * 96 + 96, :].astype(F32)
    mid = lat[...].astype(F32)
    row = lax.broadcasted_iota(jnp.int32, mid.shape, 0) % PH
    wide[0] = jnp.where(row == 0, 0.0, pltpu.roll(mid, 1, 0))
    wide[1] = mid
    wide[2] = jnp.where(row == PH - 1, 0.0, pltpu.roll(mid, 16 * PH - 1, 0))
    weight = wpad[...].astype(BF16)
    for c in range(PW):
        for tap in range(3):
            patches[c, :, tap * 128 : tap * 128 + 128] = wide[
                tap, :, c * CH : c * CH + 128
            ].astype(BF16)
        pre = dot(patches[c], weight)
        sig = sigmoid(pre)
        da_ref[:, c * PH : c * PH + PH, :] = (pre * sig).astype(BF16).reshape(16, PH, HD)
        sp_ref[:, c * PH : c * PH + PH, :] = (
            (sig * (1.0 + pre * (1.0 - sig))).astype(BF16).reshape(16, PH, HD)
        )
    mix_kv = mix[:, HD:]
    mix_q = mix[:, :HD]
    wd_val = wd[...]

    @pl.loop(0, 16)
    def _(j):
        da = da_ref[j]
        _, inv = row_scale(da, wd_val)
        kv = dot(da, mix_kv) * inv
        cosine, sine = tables(j, phase, base)
        rows = pl.ds(pl.multiple_of(j * IMG, IMG), IMG)
        k_ref[rows, :] = turn(kv[:, :HD], cosine, sine).astype(BF16)
        v_ref[rows, :] = kv[:, HD:].astype(BF16)

    for m in range(4):
        j = info[1 + m]
        da = da_ref[j]
        _, inv = row_scale(da, wd_val)
        cosine, sine = tables(j, phase, base)
        q_ref[m * IMG : (m + 1) * IMG, :] = (
            turn(dot(da, mix_q) * inv, cosine, sine) * (SCALE * LOG2E)
        ).astype(BF16)
    q_ref[1024:, :] = qdt[:, :HD]
    k_txt = kvt[:, :HD]
    v_txt = kvt[:, HD:]

    def finish(rows, peak, total, acc):
        att_ref[rows, :] = (acc / total).astype(BF16)
        lse_ref[rows, :] = jnp.broadcast_to(peak + jnp.log2(total), acc.shape)

    def step(q, scores_of):
        def body(j, state):
            peak, total, acc = state
            at = pl.ds(pl.multiple_of(j * 512, 512), 512)
            scores = scores_of(dot(q, k_ref[at, :], NT), j)
            new = jnp.maximum(peak, jnp.max(scores, axis=1, keepdims=True))
            raised = jnp.exp2(scores - new)
            old = jnp.exp2(peak - new)
            total = total * old + jnp.sum(raised, axis=1, keepdims=True)
            acc = acc * old + dot(raised.astype(BF16), v_ref[at, :])
            return new, total, acc

        return body

    def first(scores):
        peak = jnp.max(scores, axis=1, keepdims=True)
        raised = jnp.exp2(scores - peak)
        return (
            peak,
            jnp.sum(raised, axis=1, keepdims=True),
            dot(raised.astype(BF16), v_txt),
        )

    for p in range(2):
        diagonal = g if p == 0 else 7 - g
        q = q_ref[p * 512 : p * 512 + 512, :]
        bias = jnp.concatenate(
            [
                jnp.broadcast_to(bias_it[2 * p : 2 * p + 1, :], (IMG, 512)),
                jnp.broadcast_to(bias_it[2 * p + 1 : 2 * p + 2, :], (IMG, 512)),
            ],
            axis=0,
        )
        scores = jnp.where(bias < 0.0, NEG, dot(q, k_txt, NT))
        state = first(scores)

        def masked(scores, j):
            top = lax.broadcasted_iota(jnp.int32, scores.shape, 0) < IMG
            right = lax.broadcasted_iota(jnp.int32, scores.shape, 1) >= IMG
            return jnp.where(top & right, NEG, scores)

        state = step(q, masked)(diagonal, state)
        state = lax.fori_loop(0, diagonal, step(q, lambda s, j: s), state)
        finish(pl.ds(p * 512, 512), *state)

    q = q_ref[1024:, :]
    vis = vis_q[:, :1]

    def before(scores, j):
        block = 2 * j + (lax.broadcasted_iota(jnp.int32, scores.shape, 1) >= IMG).astype(jnp.int32)
        return jnp.where(block.astype(F32) < vis, scores, NEG)

    state = first(jnp.where(bias_tt[...] < 0.0, NEG, dot(q, k_txt, NT)))
    state = lax.fori_loop(0, 8 - g, step(q, before), state)
    finish(pl.ds(1024, 128), *state)

    for m in range(4):
        rows = slice(m * IMG, (m + 1) * IMG)
        reorder[...] = dot(att_ref[rows, :], nt[...], NT) + dot(
            da_ref[info[1 + m]], wu[...]
        ) * (1.0 / 32.0)
        for r in range(PH):
            part_ref[m * IMG + r * PW : m * IMG + r * PW + PW, :] = reorder[
                pl.ds(r, PW, stride=PH), :
            ].astype(BF16)


def vmem(count):
    return [pl.BlockSpec(memory_space=pltpu.VMEM)] * count


def forward(info, *args):
    sds = jax.ShapeDtypeStruct
    return pl.pallas_call(
        forward_kernel,
        out_shape=[
            sds((16, 256, 384), BF16),
            sds((16, 256, HD), BF16),
            sds((16, 256, HD), BF16),
            sds((4096, HD), BF16),
            sds((4096, HD), BF16),
            sds((1152, HD), BF16),
            sds((1152, HD), BF16),
            sds((1152, HD), F32),
            sds((1024, HD), BF16),
        ],
        in_specs=[pl.BlockSpec(memory_space=pltpu.SMEM)] + vmem(len(args)),
        out_specs=vmem(9),
        scratch_shapes=[
            pltpu.VMEM((3, 256, 640), F32),
            pltpu.VMEM((384, HD), F32),
            pltpu.VMEM((IMG, HD), F32),
        ],
        compiler_params=pltpu.CompilerParams(vmem_limit_bytes=50 * 2**20),
        cost_estimate=pl.CostEstimate(flops=8 * 10**9, bytes_accessed=2**24, transcendentals=2**22),
    )(info, *args)


def middle_kernel(
    part, pgrad, w_uo, att_txt, gall, pred, gup, atx, recv, send_a, recv_a, send_b, recv_b, send_c, recv_c
):
    e, peer = ring("team")
    i, mate = ring("group")
    greet(["team"])
    copies = []
    for o in range(1, 32):
        tx, ty, to = peer(o)
        copy = pltpu.make_async_remote_copy(
            src_ref=part.at[to],
            dst_ref=recv.at[e],
            send_sem=send_a.at[o],
            recv_sem=recv_a.at[o],
            device_id=(tx, ty),
            device_id_type=MESH,
        )
        copy.start()
        copies.append(copy)
    others = []
    for o in range(1, 4):
        tx, ty, to = mate(o)
        copy = pltpu.make_async_remote_copy(
            src_ref=att_txt.at[to],
            dst_ref=atx.at[i],
            send_sem=send_c.at[o],
            recv_sem=recv_c.at[o],
            device_id=(tx, ty),
            device_id_type=MESH,
        )
        copy.start()
        others.append(copy)
    recv[e] = part[e]
    atx[i] = att_txt[i]
    for copy in copies:
        copy.wait()
    pre = jnp.sum(recv[...].astype(F32), axis=0)
    sig = sigmoid(pre)
    act = (pre * sig).astype(BF16)
    grad = (dot(pgrad[...], w_uo[...], NT) * (sig * (1.0 + pre * (1.0 - sig)))).astype(BF16)
    gall[e] = grad
    copies = []
    for o in range(1, 32):
        tx, ty, _ = peer(o)
        copy = pltpu.make_async_remote_copy(
            src_ref=gall.at[e],
            dst_ref=gall.at[e],
            send_sem=send_b.at[o],
            recv_sem=recv_b.at[o],
            device_id=(tx, ty),
            device_id_type=MESH,
        )
        copy.start()
        copies.append(copy)
    pred[...] = dot(act, w_uo[...]).astype(BF16)
    gup[...] = dot(pgrad[...], act, TN)
    for copy in copies + others:
        copy.wait()


def middle(part, pgrad, w_uo, att_txt, cid):
    sds = jax.ShapeDtypeStruct
    return pl.pallas_call(
        middle_kernel,
        out_shape=[
            sds((32, 32, HD), BF16),
            sds((32, CH), BF16),
            sds((CH, HD), F32),
            sds((4, TXT, HD), BF16),
        ],
        in_specs=vmem(4),
        out_specs=vmem(4),
        scratch_shapes=[pltpu.VMEM((32, 32, HD), BF16)]
        + [pltpu.SemaphoreType.DMA((32,))] * 4
        + [pltpu.SemaphoreType.DMA((4,))] * 2,
        compiler_params=pltpu.CompilerParams(collective_id=cid, has_side_effects=True),
    )(part, pgrad, w_uo, att_txt)


def backward_kernel(
    info,
    patches,
    da_ref,
    sp_ref,
    k_ref,
    v_ref,
    q_ref,
    att_ref,
    lse_ref,
    gall,
    wd,
    mix,
    wu,
    nt,
    phase,
    base,
    kvt,
    qdt,
    bias_itt,
    vis_row,
    small,
    conv,
    order,
    gpu_ref,
    do_ref,
    dq_ref,
    dk_ref,
    dv_ref,
    ex_ref,
    dpre_ref,
    rows_ref,
):
    g = info[0]
    for m in range(4):
        nat = gall[m * IMG : (m + 1) * IMG, :].astype(F32)
        for r in range(PH):
            order[pl.ds(m * IMG + r, PW, stride=PH), :] = nat[r * PW : r * PW + PW, :]
    gpu_ref[...] = order[...].astype(BF16)
    do_ref[:1024, :] = dot(gpu_ref[...], nt[...]).astype(BF16)
    do_ref[1024:, :] = qdt[:, HD:]
    dk_ref[...] = jnp.zeros_like(dk_ref)
    dv_ref[...] = jnp.zeros_like(dv_ref)
    dq_ref[...] = jnp.zeros_like(dq_ref)
    ex_ref[...] = jnp.zeros_like(ex_ref)

    k_txt = kvt[:, :HD]
    v_txt = kvt[:, HD:]

    def lanes(column):
        return column.T[:1, :]

    def tile(q, do, lse, delta, keys, values, mask):
        scores = dot(keys, q, NT)
        if mask is not None:
            scores = mask(scores)
        probs = jnp.exp2(scores - lse)
        grad = (probs * (dot(values, do, NT) - delta)).astype(BF16)
        return probs.astype(BF16), grad

    for p in range(3):
        width = 512 if p < 2 else 128
        rows = slice(p * 512, p * 512 + width)
        q = q_ref[rows, :]
        do = do_ref[rows, :]
        lse = lanes(lse_ref[rows, :])
        dot_rows = jnp.sum(do.astype(F32) * att_ref[rows, :].astype(F32), axis=1, keepdims=True)
        delta = lanes(jnp.broadcast_to(dot_rows, (width, HD)))

        def body(j, mask, with_query):
            at = pl.ds(pl.multiple_of(j * 512, 512), 512)
            keys = k_ref[at, :]
            probs, grad = tile(q, do, lse, delta, keys, v_ref[at, :], mask)
            dv_ref[at, :] += dot(probs, do)
            dk_ref[at, :] += dot(grad, q)
            if with_query:
                rows_ref[...] += dot(grad, keys, TN)

        if p < 2:
            diagonal = g if p == 0 else 7 - g

            def unseen(scores):
                bottom = lax.broadcasted_iota(jnp.int32, scores.shape, 0) >= IMG
                left = lax.broadcasted_iota(jnp.int32, scores.shape, 1) < IMG
                return jnp.where(bottom & left, NEG, scores)

            def text(scores):
                left = jnp.broadcast_to(bias_itt[:, 2 * p : 2 * p + 1], (512, IMG))
                right = jnp.broadcast_to(bias_itt[:, 2 * p + 1 : 2 * p + 2], (512, IMG))
                return jnp.where(jnp.concatenate([left, right], axis=1) < 0.0, NEG, scores)

            _, grad = tile(q, do, lse, delta, k_txt, v_txt, text)
            rows_ref[...] = dot(grad, k_txt, TN)
            body(diagonal, unseen, True)

            @pl.loop(0, diagonal)
            def _(j):
                body(j, None, True)

            for half in range(2):
                dq_ref[info[1 + 2 * p + half]] = rows_ref[half * IMG : (half + 1) * IMG, :]
        else:
            vis = vis_row[:1, :]

            @pl.loop(0, 8 - g)
            def _(j):
                def seen(scores):
                    block = 2 * j + (
                        lax.broadcasted_iota(jnp.int32, scores.shape, 0) >= IMG
                    ).astype(jnp.int32)
                    return jnp.where(block.astype(F32) < vis, scores, NEG)

                body(j, seen, False)

    small[...] = jnp.zeros_like(small)
    for m in range(4):
        j = info[1 + m]
        rows = slice(m * IMG, (m + 1) * IMG)
        gpu = gpu_ref[rows, :]
        da = da_ref[j]
        ex_ref[j] = dot(gpu, wu[...], NT) * (1.0 / 32.0)
        small[:, 384:512] += dot(gpu, att_ref[rows, :], TN)
        small[:, 512:640] += dot(da, gpu, TN) * (1.0 / 32.0)
        small[:, 640:768] += dot(gpu, da, TN) * (1.0 / 32.0)
    wd_val = wd[...]
    mix_val = mix[...]

    @pl.loop(0, 16)
    def _(j):
        da = da_ref[j]
        da_wide = da.astype(F32)
        dawd, inv = row_scale(da, wd_val)
        cosine, sine = tables(j, phase, base)
        at = pl.ds(pl.multiple_of(j * IMG, IMG), IMG)
        gq = turn(dq_ref[j] * SCALE, cosine, -sine)
        gk = turn(dk_ref[at, :] * (1.0 / LOG2E), cosine, -sine)
        grads = jnp.concatenate([gq, gk, dv_ref[at, :]], axis=1).astype(BF16)
        back = dot(grads, mix_val, NT)
        cube = (inv * inv * inv) * (jnp.sum(back * da_wide, axis=1, keepdims=True) * (1.0 / D))
        grad = (inv * back - cube * dawd + ex_ref[j]) * sp_ref[j].astype(F32)
        dpre_ref[j] = grad.astype(BF16)
        small[:, :384] += dot((da_wide * inv).astype(BF16), grads, TN)
        small[:, 768:] += dot((da_wide * cube).astype(BF16), da, TN)

    total = jnp.zeros((384, HD), F32)
    for c in range(PW):
        grad = dpre_ref[:, c * PH : c * PH + PH, :].reshape(256, HD)
        total = total + dot(patches[c], grad, TN)
    for tap in range(3):
        conv[tap * 96 : tap * 96 + 96, :] = total[tap * 128 : tap * 128 + 96, :]


def backward(info, *args):
    sds = jax.ShapeDtypeStruct
    return pl.pallas_call(
        backward_kernel,
        out_shape=[sds((HD, 896), F32), sds((288, HD), F32)],
        in_specs=[pl.BlockSpec(memory_space=pltpu.SMEM)] + vmem(len(args)),
        out_specs=vmem(2),
        scratch_shapes=[
            pltpu.VMEM((1024, HD), F32),
            pltpu.VMEM((1024, HD), BF16),
            pltpu.VMEM((1152, HD), BF16),
            pltpu.VMEM((16, IMG, HD), F32),
            pltpu.VMEM((4096, HD), F32),
            pltpu.VMEM((4096, HD), F32),
            pltpu.VMEM((16, IMG, HD), F32),
            pltpu.VMEM((16, IMG, HD), BF16),
            pltpu.VMEM((512, HD), F32),
        ],
        compiler_params=pltpu.CompilerParams(vmem_limit_bytes=50 * 2**20),
        cost_estimate=pl.CostEstimate(
            flops=16 * 10**9, bytes_accessed=2**24, transcendentals=2**22
        ),
    )(info, *args)


def rope_base():
    half = HD // 2
    freq = np.exp(-(2.0 * np.arange(half) / HD) * math.log(ROPE_BASE))
    slot = np.arange(IMG)
    position = (slot % PH) * PW + slot // PH
    angle = position[:, None] * freq[None, :]
    cosine = np.concatenate([np.cos(angle), np.cos(angle)], axis=1)
    sine = np.concatenate([-np.sin(angle), np.sin(angle)], axis=1)
    return jnp.asarray(np.stack([cosine, sine]).astype(np.float32))


def angles(positions):
    half = HD // 2
    freq = jnp.exp(-(2.0 * jnp.arange(half, dtype=F32) / HD) * math.log(ROPE_BASE))
    angle = positions.astype(F32)[:, None] * freq[None, :]
    cosine = jnp.cos(angle)
    sine = jnp.sin(angle)
    return (
        jnp.concatenate([cosine, cosine], axis=1),
        jnp.concatenate([-sine, sine], axis=1),
    )


def split_wide(x):
    high = x.astype(BF16)
    return jnp.concatenate([high, (x - high.astype(F32)).astype(BF16)], axis=1)


def head_columns(x, i):
    return lax.dynamic_slice_in_dim(x, i * HD, HD, 1)


def shards(
    text_tokens,
    latent,
    image_offset,
    norm_gain,
    w_query,
    w_key,
    w_value,
    w_out,
    w_down_conv,
    w_down_proj,
    w_up_proj,
    w_up_out,
    pred_grad,
    text_grad,
):
    sx = lax.axis_index("sx")
    sy = lax.axis_index("sy")
    g, i = split_sy(sy)
    members = jnp.stack([sy_of(g, jnp.int32(m)) for m in range(4)])
    info = jnp.concatenate([jnp.stack([g, *members]), jnp.zeros((3,), jnp.int32)]).astype(jnp.int32)
    gain = norm_gain.astype(F32)

    text, tgrad, lat, offs = exchange(
        [
            text_tokens[0],
            text_grad[0],
            latent[0],
            jnp.broadcast_to(image_offset.astype(F32)[:, None], (8, HD)),
        ],
        [("sx", "gather"), ("sx", "gather"), ("sx", "gather"), ("sy", "gather")],
        1,
    )
    text = text.reshape(TXT, D)
    tgrad = tgrad.reshape(TXT, D)
    offsets = offs[:, 0, 0].astype(jnp.int32)

    wide = text.astype(F32)
    inverse = lax.rsqrt(jnp.mean(wide * wide, axis=-1, keepdims=True) + EPS)
    left = jnp.concatenate(
        [w_down_proj.astype(F32) * gain, wide * inverse * gain], axis=0
    ).astype(BF16)
    query = dot(left, w_query)
    key = dot(left, w_key)
    value = dot(left, w_value)
    outer = dot(jnp.concatenate([w_up_proj.T, tgrad], axis=0), w_out, NT)
    wd = split_wide(dot(w_down_proj, w_down_proj, NT))
    wu = dot(w_down_proj, w_up_proj).astype(BF16)
    own_off = image_offset[0]
    token = jnp.arange(TXT, dtype=jnp.int32)
    cosine, sine = angles(sy * SB + token + jnp.where(token >= own_off, IMG, 0))

    def heads(x):
        return x[HD:].reshape(TXT, 4, HD).transpose(1, 0, 2)

    def swap(x):
        return jnp.concatenate([x[..., HD // 2 :], x[..., : HD // 2]], axis=-1)

    q_txt = heads(query)
    k_txt = heads(key)
    q_txt = (q_txt * cosine + swap(q_txt) * sine) * (SCALE * LOG2E)
    k_txt = k_txt * cosine + swap(k_txt) * sine
    kvt = jnp.concatenate([k_txt, heads(value)], axis=2).astype(BF16)
    qdt = jnp.concatenate([q_txt, heads(outer)], axis=2).astype(BF16)
    mix = jnp.concatenate(
        [head_columns(x[:HD], i) for x in (query, key, value)], axis=1
    ).astype(BF16)
    nt = head_columns(outer[:HD], i).astype(BF16)

    kvt, qdt, lat = exchange(
        [kvt, qdt, lat.reshape(PH, PW * CH)],
        [("syhead", "scatter"), ("group", "scatter"), ("sy", "gather")],
        2,
    )
    kvt = kvt.reshape(512, 2 * HD)
    qdt = qdt.reshape(128, 2 * HD)
    lat = jnp.pad(lat.reshape(256, PW * CH), ((0, 0), (CH, 96)))

    blocks = jnp.arange(16, dtype=jnp.int32)
    phase = jnp.stack(angles(blocks * SB + offsets))
    base = rope_base()
    key_block = jnp.repeat(blocks, TXT)
    key_token = jnp.tile(token, 16)
    own_offs = offsets[members]
    seen_it = (key_block[None, :] < members[:, None]) | (
        (key_block[None, :] == members[:, None]) & (key_token[None, :] < own_offs[:, None])
    )
    bias_it = jnp.where(seen_it, 0.0, NEG).astype(F32)
    query_block = jnp.repeat(members, TXT)
    query_token = jnp.tile(token, 4)
    vis = (query_block + (query_token >= jnp.repeat(own_offs, TXT)).astype(jnp.int32)).astype(F32)
    seen_tt = (key_block[None, :] < query_block[:, None]) | (
        (key_block[None, :] == query_block[:, None]) & (key_token[None, :] <= query_token[:, None])
    )
    bias_tt = jnp.where(seen_tt, 0.0, NEG).astype(F32)

    patches, da, sp, keys, values, queries, att, lse, part = forward(
        info,
        lat,
        w_down_conv,
        wd,
        mix,
        wu,
        nt,
        phase,
        base,
        kvt,
        qdt,
        jnp.pad(bias_it, ((0, 4), (0, 0))),
        jnp.broadcast_to(vis[:, None], (128, HD)),
        bias_tt,
    )

    gall, pred, gup, atx = middle(
        part.reshape(32, 32, HD),
        pred_grad[0].reshape(32, CH),
        w_up_out,
        att[1024:].reshape(4, TXT, HD),
        3,
    )
    mixed_text = dot(atx.transpose(1, 0, 2).reshape(TXT, 512), w_out).astype(BF16)

    small, conv = backward(
        info,
        patches,
        da,
        sp,
        keys,
        values,
        queries,
        att,
        lse,
        gall.reshape(1024, HD),
        wd,
        mix,
        wu,
        nt,
        phase,
        base,
        kvt,
        qdt,
        jnp.pad(bias_it.T, ((0, 0), (0, 124))),
        jnp.broadcast_to(vis[None, :], (8, HD)),
    )

    small, conv, mixed_text = exchange(
        [
            small.reshape(4, 32, 896),
            jnp.concatenate([conv, gup], axis=0).reshape(4, 80, HD),
            mixed_text.reshape(8, 4, D),
        ],
        [("head", "scatter"), ("head", "scatter"), ("sx", "scatter")],
        4,
    )
    text_out = (
        text_tokens[0].astype(F32) + jnp.sum(mixed_text.astype(F32), axis=0)
    ).astype(BF16)
    small = jnp.sum(small, axis=0)
    conv = jnp.sum(conv, axis=0)

    low = small.astype(BF16)
    down = (
        dot(low[:, :HD], head_columns(w_query, i), NT)
        + dot(low[:, HD : 2 * HD], head_columns(w_key, i), NT)
        + dot(low[:, 2 * HD : 3 * HD], head_columns(w_value, i), NT)
    ) * gain
    down = down + dot(low[:, 512:640], w_up_proj, NT) - dot(low[:, 768:896], w_down_proj)
    up = dot(low[:, 384:512], lax.dynamic_slice_in_dim(w_out, i * HD, HD, 0)) + dot(
        low[:, 640:768], w_down_proj
    )
    parts = jnp.concatenate(
        [
            down.reshape(32, 32, HD).transpose(1, 0, 2),
            up.reshape(32, 32, HD).transpose(1, 0, 2),
            jnp.pad(conv, ((0, 16), (0, 0))).reshape(32, 3, HD),
            jnp.zeros((32, 13, HD), F32),
        ],
        axis=1,
    ).astype(BF16)
    (summed,) = exchange([parts], [("team", "scatter")], 5)
    own = jnp.sum(summed.astype(F32), axis=0).astype(BF16)
    (column,) = exchange([own], [("sx", "gather")], 6)
    (every,) = exchange([column], [("sy", "gather")], 7)

    low_half = every[:8].reshape(4, 2, 8, 80, HD)
    high_half = every[8:].reshape(4, 2, 8, 80, HD)[::-1]
    every = jnp.concatenate([low_half, high_half], axis=1).reshape(4, 32, 80, HD).astype(F32)
    grad_down_proj = every[:, :, :32].transpose(0, 2, 1, 3).reshape(HD, D)
    grad_up_proj = every[:, :, 32:64].transpose(1, 3, 0, 2).reshape(D, HD)
    rest = every[:, :, 64:67].reshape(4, 96, HD)[:, :80].reshape(320, HD)
    return (
        pred.reshape(1, 2, PW * CH),
        text_out[None],
        rest[:288],
        grad_down_proj,
        grad_up_proj,
        rest[288:].T,
    )


def solution(mesh):
    placed = (
        P("sy", "sx", None),
        P("sy", "sx", None),
        P("sy"),
        P(),
        P(None, "sx"),
        P(None, "sx"),
        P(None, "sx"),
        P("sx", None),
        P(),
        P(),
        P(),
        P(),
        P("sy", "sx", None),
        P("sy", "sx", None),
    )
    return jax.shard_map(
        shards,
        mesh=mesh,
        in_specs=placed,
        out_specs=(P("sy", "sx", None), P("sy", "sx", None), P(), P(), P(), P()),
        check_vma=False,
    )
```

time: 922 us -> 264 us (0.29)
  the two profiles are of different devices: /device:TPU:1 before, /device:TPU:113 now
where the time goes in v1:
time: 264 us; the launch traced here: 263 us
  Pallas kernels  187 us (71%)
  local copies, waits for them, and re-layouts  40.4 us (15%)
  matrix products  17.7 us (7%)
  other arithmetic  15.8 us (6%)
    pallas_call x6, Pallas kernels, exchange(): pl.pallas_call(functools.partial(exchange_kernel, items, len(arrays)), ou...  119 us
    pallas_call x1, Pallas kernels, backward(): pl.pallas_call(backward_kernel, out_shape=[sds((HD, 896), F32), sds((288,...  26.2 us
    pallas_call x1, Pallas kernels, forward(): pl.pallas_call(forward_kernel, out_shape=[sds((16, 256, 384), BF16), sds(...  21.5 us
    pallas_call x1, Pallas kernels, middle(): pl.pallas_call(middle_kernel, out_shape=[sds((32, 32, HD), BF16), sds((32...  20.6 us
    dot_general x14, matrix products, dot(): return lax.dot_general(a, b, dims, preferred_element_type=F32)  17.7 us
    unnamed x49, local copies, waits for them, and re-layouts  17.2 us

profile of v1, /device:TPU:113, one launch (start us, length us, event | category | flops | bytes accessed | tf_op | source)
XLA Modules:
  0.0 262.7 jit_solution(4887516304429776532)
XLA Ops:
  2.0 0.6 broadcast_in_dim.88.refs_3_
  2.6 1.4 reshape_squeeze.3.pgrad
  4.2 0.7 convert_element_type.118
  4.9 2.0 convolution_convert_fusion.1.wu
  6.8 1.4 copy.48.w_uo
  8.5 0.4 subtract_convert_fusion
  9.1 12.0 %shard_map.190 = (bf16[8,4,4096]{2,1,0:T(4,128)(2,1)}, bf16[8,4,4096]{2,1,0:T(4,128)(2,1)}, bf16[8,2,512]{2,1,0:T(2,128)(2,1)}, f32[16,8,128]{2,1,0:T(8,128)}) custom-call(bf16[4,4096]{1,0:T(4,128)(2,1)} %bitcast.156, bf16[4,4096]{1,0:T(4,128)(2,1)} %bitcast.158, bf16[2,512]{1,0:T(2,128)(2,1)} %bitcast.159, f32[8,128]{1,0:T(8,128)} %broadcast_in_dim.88.refs_3_), custom_call_target="tpu_custom_call" | custom-call | tf_op jit(solution)/shard_map/pallas_call | solution.py:124
  21.1 1.8 reshape.359
  22.9 1.2 convert_reduce_fusion.1
  24.1 0.6 gather_fusion
  25.0 1.2 multiply_reduce_fusion
  26.3 1.3 reshape.361.refs_2_
  28.2 1.0 reshape.384
  29.2 0.8 multiply_convert_fusion.1
  30.0 2.3 copy.44
  32.3 4.2 %fusion.3 = bf16[160,512]{1,0:T(8,128)(2,1)S(1)} fusion(bf16[512,4096]{1,0:T(8,128)(2,1)} %param.22, bf16[32,4096]{0,1:T(8,128)(2,1)} %copy.44, bf16[128,4096]{0,1:T(8,128)(2,1)S(1)} %bitcast.145), kind=kOutput, calls=%fused_computation.14 | convolution fusion | flops 673710080 | bytes 5668864 | tf_op jit(solution)/shard_map/dot_general | solution.py:36
  36.8 0.9 fusion.16
  37.7 1.2 copy-done.17
  38.9 0.9 fusion.15
  39.8 1.3 copy-done.15
  41.1 0.8 fusion.17
  42.4 0.6 pad_maximum_fusion.7.refs_1_
  43.1 0.6 pad_maximum_fusion.6.refs_0_
  43.7 14.8 %shard_map.191 = (bf16[16,32,256]{2,1,0:T(8,128)(2,1)}, bf16[4,32,256]{2,1,0:T(8,128)(2,1)}, bf16[16,16,512]{2,1,0:T(8,128)(2,1)}) custom-call(bf16[4,32,256]{2,1,0:T(8,128)(2,1)} %pad_maximum_fusion.6.refs_0_, bf16[4,32,256]{2,1,0:T(8,128)(2,1)} %pad_maximum_fusion.7.refs_1_, bf16[16,512]{1,0:T(8,128)(2,1)} %reshape.361.refs_2_), custom_call_target="tpu_custom_call" | custom-call | tf_op jit(solution)/shard_map/pallas_call | solution.py:124
  58.5 1.1 pad.17.lat
  59.6 0.9 copy-done.2
  60.6 0.8 copy-done.6
  61.4 21.5 %shard_map.192 = (bf16[16,256,384]{2,1,0:T(8,128)(2,1)}, bf16[16,256,128]{2,1,0:T(8,128)(2,1)S(1)}, bf16[16,256,128]{2,1,0:T(8,128)(2,1)}, bf16[4096,128]{1,0:T(...) custom-call(s32[8]{0:T(128)S(1)} %concatenate.72.info, ...), custom_call_target="tpu_custom_call" | custom-call | flops 8000000000 | bytes 16777216 | tf_op jit(solution)/shard_map/pallas_call | solution.py:313
  82.9 0.7 copy-done.1
  83.6 1.0 copy-done.9
  84.6 0.6 slice.102
  85.2 20.6 %shard_map.193 = (bf16[32,32,128]{2,1,0:T(8,128)(2,1)}, bf16[32,32]{1,0:T(8,128)(2,1)}, f32[32,128]{1,0:T(8,128)}, bf16[4,32,128]{2,1,0:T(8,128)(2,1)}) custom-call(bf16[32,32,128]{2,1,0:T(8,128)(2,1)} %bitcast.132, bf16[32,32]{1,0:T(8,128)(2,1)} %reshape_squeeze.3.pgrad, bf16[128,32]{1,0:T(8,128)(2,1)} %copy.48.w_uo, bf16[4,32,128]{2,1,0:T(8,128)(2,1)} %bitcast.157), custom_call_target="tpu_custom_call" | custom-call | tf_op jit(solution)/shard_map/pallas_call | solution.py:400
  105.8 1.4 reshape.369
  107.1 0.9 copy-done.4
  108.1 26.2 %shard_map.194 = (f32[128,896]{1,0:T(8,128)S(1)}, f32[288,128]{1,0:T(8,128)S(1)}) custom-call(s32[8]{0:T(128)S(1)} %concatenate.72.info, bf16[16,256,384]{2,1,0:T(8,128)(2,1)} %get-tuple-element.41.patches, bf16[16,256,128]{2,1,0:T(8,128)(2,1)} %copy-done.9, bf16[16,256,128]{2,1,0:T(8,128)(2,1)} %get-tuple-element.43.sp_ref, ...), custom_call_target="tpu_custom_call" | custom-call | flops 16000000000 | bytes 16777216 | tf_op jit(solution)/shard_map/pallas_call | solution.py:571
  134.3 0.8 copy-done
  135.1 0.7 pad_maximum_fusion.4
  135.8 0.8 convolution_convert_fusion
  136.6 0.8 reshape.374.refs_2_
  137.4 17.4 %shard_map.195 = (f32[4,32,896]{2,1,0:T(8,128)}, f32[4,80,128]{2,1,0:T(8,128)}, bf16[8,4,4096]{2,1,0:T(4,128)(2,1)}) custom-call(f32[4,32,896]{2,1,0:T(8,128)} %bitcast.131, f32[4,80,128]{2,1,0:T(8,128)} %bitcast.150, bf16[8,4,4096]{2,1,0:T(4,128)(2,1)} %reshape.374.refs_2_), custom_call_target="tpu_custom_call" | custom-call | tf_op jit(solution)/shard_map/pallas_call | solution.py:124
  154.8 1.1 convert_reduce_fusion
  155.9 0.6 fusion.23
  156.6 0.9 reduce_sum.54
  157.5 1.0 reduce_sum.53
  158.6 1.5 fusion.9
  160.4 1.8 fusion.13
  162.2 1.7 convolution_add_fusion.3
  163.9 1.7 fusion
  165.6 0.5 convolution_add_fusion.1
  166.4 1.0 maximum_maximum_fusion.refs_0_
  167.4 15.8 %shard_map.196 = bf16[32,80,128]{2,1,0:T(8,128)(2,1)} custom-call(bf16[32,80,128]{2,1,0:T(8,128)(2,1)} %maximum_maximum_fusion.refs_0_), custom_call_target="tpu_custom_call" | custom-call | tf_op jit(solution)/shard_map/pallas_call | solution.py:124
  183.3 1.8 reduce_sum.55.refs_0_
  185.1 6.8 %shard_map.197.refs_0_ = bf16[8,80,128]{2,1,0:T(8,128)(2,1)} custom-call(bf16[80,128]{1,0:T(8,128)(2,1)} %reduce_sum.55.refs_0_), custom_call_target="tpu_custom_call" | custom-call | tf_op jit(solution)/shard_map/pallas_call | solution.py:124
  191.9 51.7 %shard_map.198 = bf16[16,8,80,128]{3,2,1,0:T(8,128)(2,1)} custom-call(bf16[8,80,128]{2,1,0:T(8,128)(2,1)} %shard_map.197.refs_0_), custom_call_target="tpu_custom_call" | custom-call | tf_op jit(solution)/shard_map/pallas_call | solution.py:124
  243.6 3.0 %fusion.51 = (bf16[8,8,80,128]{3,2,1,0:T(8,128)(2,1)}, bf16[8,8,80,128]{3,2,1,0:T(8,128)(2,1)S(1)}) fusion(bf16[16,8,80,128]{3,2,1,0:T(8,128)(2,1)} %shard_map.198), kind=kLoop, calls=%fused_computation.114 | loop fusion | bytes 5242880 | tf_op jit(solution)/shard_map/slice | solution.py:810
  246.6 1.1 rev.3
  247.8 2.1 maximum_convert_fusion
  249.8 1.6 copy.83
  251.4 1.8 fusion.50
  253.3 1.6 copy.84
  254.9 1.8 copy.55
  256.7 4.5 %copy.85 = f32[16,8,32,128]{3,1,2,0:T(8,128)} copy(f32[16,8,32,128]{3,2,1,0:T(8,128)} %bitcast.141) | data formatting | bytes 4194304
  261.4 0.6 slice_bitcast_fusion.2
  262.0 0.7 slice.141
  (98 shorter events, 3.5 us)
Async XLA Ops:
  0.6 7.8 %copy-start.10 = (bf16[128,4096]{1,0:T(8,128)(2,1)S(1)}, bf16[128,4096]{1,0:T(8,128)(2,1)}, u32[]{:S(2)}) copy-start(bf16[128,4096]{1,0:T(8,128)(2,1)} %param.24) | copy-start | bytes 3145732
  21.1 11.1 %copy-start.13 = (bf16[4096,128]{1,0:T(8,128)(2,1)S(1)}, bf16[4096,128]{1,0:T(8,128)(2,1)}, u32[]{:S(2)}) copy-start(bf16[4096,128]{1,0:T(8,128)(2,1)} %param.25) | copy-start | bytes 3145732
  32.3 4.5 %copy-start.16 = (bf16[4096,512]{1,0:T(8,128)(2,1)S(1)}, bf16[4096,512]{1,0:T(8,128)(2,1)}, u32[]{:S(2)}) copy-start(bf16[4096,512]{1,0:T(8,128)(2,1)} %param.21) | copy-start | bytes 12582916
  32.3 4.5 %copy-start.18 = (bf16[32,4096]{1,0:T(8,128)(2,1)S(1)}, bf16[32,4096]{1,0:T(8,128)(2,1)}, u32[]{:S(2)}) copy-start(bf16[32,4096]{1,0:T(8,128)(2,1)} %multiply_convert_fusion.1) | copy-start | bytes 786436
  36.7 2.2 copy-start.17
  38.9 2.2 copy-start.15
  42.0 17.6 %copy-start.5 = (bf16[288,128]{1,0:T(8,128)(2,1)S(1)}, bf16[288,128]{1,0:T(8,128)(2,1)}, u32[]{:S(2)}) copy-start(bf16[288,128]{1,0:T(8,128)(2,1)} %wconv.1) | copy-start | bytes 221188
  42.0 17.6 %copy-start.8 = (f32[2,256,128]{2,1,0:T(8,128)S(1)}, f32[2,256,128]{2,1,0:T(8,128)}, u32[]{:S(2)}) copy-start(f32[2,256,128]{2,1,0:T(8,128)} %constant.87.clone.base) | copy-start | bytes 786436
  59.6 1.0 copy-start.2
  60.6 0.8 copy-start.6
  61.4 45.7 %copy-start.3 = (bf16[16,32,256]{2,1,0:T(8,128)(2,1)S(1)}, bf16[16,32,256]{2,1,0:T(8,128)(2,1)}, u32[]{:S(2)}) copy-start(bf16[16,32,256]{2,1,0:T(8,128)(2,1)} %get-tuple-element.36) | copy-start | bytes 786436
  61.4 45.7 %copy-start.7 = (bf16[4,32,256]{2,1,0:T(8,128)(2,1)S(1)}, bf16[4,32,256]{2,1,0:T(8,128)(2,1)}, u32[]{:S(2)}) copy-start(bf16[4,32,256]{2,1,0:T(8,128)(2,1)} %get-tuple-element.37) | copy-start | bytes 196612
  82.9 0.7 copy-start.1
  83.6 1.0 copy-start.9
  107.1 1.0 copy-start.4
  108.1 27.0 %copy-start.21 = (f32[32,128]{1,0:T(8,128)S(1)}, f32[32,128]{1,0:T(8,128)}, u32[]{:S(2)}) copy-start(f32[32,128]{1,0:T(8,128)} %get-tuple-element.51) | copy-start | bytes 49156
  108.1 27.7 %copy-start.12 = (bf16[512,4096]{1,0:T(8,128)(2,1)S(1)}, bf16[512,4096]{1,0:T(8,128)(2,1)}, u32[]{:S(2)}) copy-start(bf16[512,4096]{1,0:T(8,128)(2,1)} %param.22) | copy-start | bytes 12582916
  108.1 27.7 %copy-start.20 = (bf16[4,32,128]{2,1,0:T(8,128)(2,1)S(1)}, bf16[4,32,128]{2,1,0:T(8,128)(2,1)}, u32[]{:S(2)}) copy-start(bf16[4,32,128]{2,1,0:T(8,128)(2,1)} %get-tuple-element.52) | copy-start | bytes 98308
  134.3 0.8 copy-start
  135.8 20.1 %copy-start.19 = (bf16[1,4,4096]{2,1,0:T(4,128)(2,1)S(1)}, bf16[1,4,4096]{2,1,0:T(4,128)(2,1)}, u32[]{:S(2)}) copy-start(bf16[1,4,4096]{2,1,0:T(4,128)(2,1)} %param.15) | copy-start | bytes 98308
  136.6 23.5 %copy-start.11 = (bf16[128,4096]{1,0:T(8,128)(2,1)S(1)}, bf16[128,4096]{1,0:T(8,128)(2,1)}, u32[]{:S(2)}) copy-start(bf16[128,4096]{1,0:T(8,128)(2,1)} %param.24) | copy-start | bytes 3145732
  160.4 5.2 %copy-start.14 = (bf16[4096,128]{1,0:T(8,128)(2,1)S(1)}, bf16[4096,128]{1,0:T(8,128)(2,1)}, u32[]{:S(2)}) copy-start(bf16[4096,128]{1,0:T(8,128)(2,1)} %param.25) | copy-start | bytes 3145732

commit v2 on v1

--- a/solution.py
+++ b/solution.py
@@ -36,6 +36,10 @@
     return lax.dot_general(a, b, dims, preferred_element_type=F32)
 
 
+def vmem(count):
+    return [pl.BlockSpec(memory_space=pltpu.VMEM)] * count
+
+
 def sy_of(g, i):
     return jnp.where(i < 2, 2 * g + i, 12 - 2 * g + i)
 
@@ -82,57 +86,575 @@
     pl.semaphore_wait(barrier, total)
 
 
-def exchange_kernel(items, count, *refs):
-    ins = refs[:count]
-    outs = refs[count : 2 * count]
-    local, send, recv = refs[2 * count :]
-    kinds = {("sy" if kind == "syhead" else kind): 0 for kind, _ in items}
-    greet(kinds)
+def remote(src, dst, send, recv, to):
+    copy = pltpu.make_async_remote_copy(
+        src_ref=src,
+        dst_ref=dst,
+        send_sem=send,
+        recv_sem=recv,
+        device_id=to,
+        device_id_type=MESH,
+    )
+    copy.start()
+    return copy
+
+
+def swap_halves(v):
+    return pltpu.roll(v, 64, 1)
+
+
+def trig(shape, position):
+    lane = lax.broadcasted_iota(jnp.int32, shape, 1)
+    step = (lane % 64).astype(F32)
+    angle = position * jnp.exp(step * (-2.0 / HD * math.log(ROPE_BASE)))
+    sine = jnp.sin(angle)
+    return jnp.cos(angle), jnp.where(lane < 64, -sine, sine)
+
+
+def lead_kernel(
+    offset,
+    text,
+    tgrad,
+    lat,
+    gain,
+    w_down,
+    w_up,
+    w_query,
+    w_key,
+    w_value,
+    w_out,
+    mix,
+    nt,
+    wd,
+    wu,
+    kvt,
+    qdt,
+    lat_all,
+    phase,
+    bias_it,
+    bias_itt,
+    bias_tt,
+    vis_q,
+    vis_row,
+    dn,
+    up,
+    wq,
+    wk,
+    wv,
+    wo,
+    text_in,
+    tgrad_in,
+    lat_in,
+    offs,
+    own_off,
+    rows_text,
+    rows_grad,
+    rows_lat,
+    pad_lat,
+    kv_out,
+    qd_out,
+    local,
+    send_sx,
+    recv_sx,
+    send_off,
+    recv_off,
+    send_kv,
+    recv_kv,
+    send_qd,
+    recv_qd,
+    send_lat,
+    recv_lat,
+):
+    sx = lax.axis_index("sx")
+    sy = lax.axis_index("sy")
+    g, head = split_sy(sy)
+    loads = []
+    for at, (src, dst) in enumerate(
+        [(w_down, dn), (w_up, up), (w_query, wq), (w_key, wk), (w_value, wv), (w_out, wo)]
+    ):
+        copy = pltpu.make_async_copy(src, dst, local.at[at])
+        copy.start()
+        loads.append(copy)
+    greet(["sx", "sy"])
+    _, beside = ring("sx")
+    _, along = ring("sy")
+    _, mate = ring("group")
+    first = []
+    for o in range(1, 8):
+        tx, ty, _ = beside(o)
+        for n, (src, dst) in enumerate([(lat, lat_in), (text, text_in), (tgrad, tgrad_in)]):
+            first.append(
+                remote(src, dst.at[sx], send_sx.at[o, n], recv_sx.at[o, n], (tx, ty))
+            )
+    own_off[...] = jnp.full((8, HD), offset[0].astype(F32))
+    offs[sy] = own_off[...]
+    second = []
+    for o in range(1, 16):
+        tx, ty, _ = along(o)
+        second.append(remote(own_off, offs.at[sy], send_off.at[o], recv_off.at[o], (tx, ty)))
+    lat_in[sx] = lat[...]
+    text_in[sx] = text[...]
+    tgrad_in[sx] = tgrad[...]
+
+    gain_row = gain[...]
+    loads[0].wait()
+    loads[1].wait()
+    down = dn[...]
+    both = dot(down, down, NT)
+    high = both.astype(BF16)
+    wd[:, :HD] = high
+    wd[:, HD:] = (both - high.astype(F32)).astype(BF16)
+    wu[...] = dot(down, up[...]).astype(BF16)
+    scaled = (down.astype(F32) * gain_row).astype(BF16)
+    mine = pl.ds(pl.multiple_of(head * HD, HD), HD)
+    for n, weight in enumerate([wq, wk, wv]):
+        loads[2 + n].wait()
+        mix[:, n * HD : (n + 1) * HD] = dot(scaled, weight[:, mine]).astype(BF16)
+    loads[5].wait()
+    nt[...] = lax.dot_general(
+        up[...], wo[mine, :], (((0,), (1,)), ((), ())), preferred_element_type=F32
+    ).astype(BF16)
+
+    for o in range(7):
+        first[3 * o].wait_recv()
+    pad_lat[...] = jnp.zeros_like(pad_lat)
+    for n in range(8):
+        rows_lat[2 * n : 2 * n + 2, :] = lat_in[n].astype(F32)
+    pad_lat[:, CH : CH + PW * CH] = rows_lat[...].astype(BF16)
+    lat_all[sy] = pad_lat[...]
+    third = []
+    for o in range(1, 16):
+        tx, ty, _ = along(o)
+        third.append(remote(pad_lat, lat_all.at[sy], send_lat.at[o], recv_lat.at[o], (tx, ty)))
+
+    for o in range(7):
+        first[3 * o + 1].wait_recv()
+        first[3 * o + 2].wait_recv()
+    for n in range(8):
+        rows_text[4 * n : 4 * n + 4, :] = text_in[n].astype(F32)
+        rows_grad[4 * n : 4 * n + 4, :] = tgrad_in[n].astype(F32)
+    wide = rows_text[...]
+    inverse = lax.rsqrt(jnp.mean(wide * wide, axis=1, keepdims=True) + EPS)
+    normed = (wide * inverse * gain_row).astype(BF16)
+    token = lax.broadcasted_iota(jnp.int32, (TXT, HD), 0).astype(F32)
+    shift = jnp.where(token >= own_off[:1, :], float(IMG), 0.0)
+    cosine, sine = trig((TXT, HD), token + shift + (sy * SB).astype(F32))
+    query = dot(normed, wq[...])
+    key = dot(normed, wk[...])
+    value = dot(normed, wv[...])
+    outer = dot(rows_grad[...].astype(BF16), wo[...], NT)
+    for h in range(4):
+        at = slice(h * HD, (h + 1) * HD)
+        kv_out[h, :, :HD] = (key[:, at] * cosine + swap_halves(key[:, at]) * sine).astype(BF16)
+        kv_out[h, :, HD:] = value[:, at].astype(BF16)
+        turned = query[:, at] * cosine + swap_halves(query[:, at]) * sine
+        qd_out[h, :, :HD] = (turned * (SCALE * LOG2E)).astype(BF16)
+        qd_out[h, :, HD:] = outer[:, at].astype(BF16)
+    for o in range(1, 16):
+        tx, ty, _ = along(o)
+        to = split_sy(ty)[1]
+        third.append(remote(kv_out.at[to], kvt.at[sy], send_kv.at[o], recv_kv.at[o], (tx, ty)))
+    for o in range(1, 4):
+        tx, ty, to = mate(o)
+        third.append(remote(qd_out.at[to], qdt.at[head], send_qd.at[o], recv_qd.at[o], (tx, ty)))
+    kvt[sy] = kv_out[head]
+    qdt[head] = qd_out[head]
+
+    for copy in second:
+        copy.wait()
+    block = lax.broadcasted_iota(jnp.int32, (16, HD), 0).astype(F32)
+    cosine, sine = trig((16, HD), block * float(SB) + jnp.max(offs[...], axis=1))
+    phase[0] = cosine
+    phase[1] = sine
+    members = [sy_of(g, m) for m in range(4)]
+    starts = [offs[b][:1, :] for b in members]
+    lane = lax.broadcasted_iota(jnp.int32, (TXT, 512), 1)
+    key_block = lane // TXT
+    key_token = lane % TXT
+    query_token = lax.broadcasted_iota(jnp.int32, (TXT, 512), 0)
+    bias_it[...] = jnp.zeros_like(bias_it)
+    for m in range(4):
+        b = members[m]
+        start = jnp.concatenate([starts[m]] * 4, axis=1)
+        seen = (key_block[:1] < b) | (
+            (key_block[:1] == b) & (key_token[:1].astype(F32) < start)
+        )
+        bias_it[m : m + 1, :] = jnp.where(seen, 0.0, NEG)
+        seen = (key_block < b) | ((key_block == b) & (key_token <= query_token))
+        bias_tt[m * TXT : (m + 1) * TXT, :] = jnp.where(seen, 0.0, NEG)
+        late = jnp.where(token >= starts[m], 1.0, 0.0)
+        vis_q[m * TXT : (m + 1) * TXT, :] = late + b.astype(F32)
+    lane = lax.broadcasted_iota(jnp.int32, (8, HD), 1)
+    start = starts[0]
+    owner = jnp.full((8, HD), members[0], jnp.int32)
+    for m in range(1, 4):
+        start = jnp.where(lane // TXT == m, starts[m], start)
+        owner = jnp.where(lane // TXT == m, members[m], owner)
+    late = jnp.where((lane % TXT).astype(F32) >= start, 1.0, 0.0)
+    vis_row[...] = late + owner.astype(F32)
+    lane = lax.broadcasted_iota(jnp.int32, (512, HD), 1)
+    row = lax.broadcasted_iota(jnp.int32, (512, HD), 0)
+    start = jnp.broadcast_to(starts[0], (512, HD))
+    owner = jnp.full((512, HD), members[0], jnp.int32)
+    for m in range(1, 4):
+        start = jnp.where(lane == m, starts[m], start)
+        owner = jnp.where(lane == m, members[m], owner)
+    seen = (row // TXT < owner) | (
+        (row // TXT == owner) & ((row % TXT).astype(F32) < start)
+    )
+    bias_itt[...] = jnp.where(seen, 0.0, NEG)
+
+    for copy in first:
+        copy.wait_send()
+    for copy in third:
+        copy.wait()
+
+
+def lead(offset, text, tgrad, lat, gain, w_down, w_up, w_query, w_key, w_value, w_out, cid):
+    sds = jax.ShapeDtypeStruct
+    hbm = pl.BlockSpec(memory_space=pl.ANY)
+    dma = pltpu.SemaphoreType.DMA
+    return pl.pallas_call(
+        lead_kernel,
+        out_shape=[
+            sds((HD, 384), BF16),
+            sds((HD, HD), BF16),
+            sds((HD, 256), BF16),
+            sds((HD, HD), BF16),
+            sds((16, TXT, 256), BF16),
+            sds((4, TXT, 256), BF16),
+            sds((16, PH, 640), BF16),
+            sds((2, 16, HD), F32),
+            sds((8, 512), F32),
+            sds((512, HD), F32),
+            sds((128, 512), F32),
+            sds((128, HD), F32),
+            sds((8, HD), F32),
+        ],
+        in_specs=[pl.BlockSpec(memory_space=pltpu.SMEM)] + vmem(4) + [hbm] * 6,
+        out_specs=vmem(13),
+        scratch_shapes=[
+            pltpu.VMEM((HD, D), BF16),
+            pltpu.VMEM((D, HD), BF16),
+            pltpu.VMEM((D, 512), BF16),
+            pltpu.VMEM((D, 512), BF16),
+            pltpu.VMEM((D, 512), BF16),
+            pltpu.VMEM((512, D), BF16),
+            pltpu.VMEM((8, 4, D), BF16),
+            pltpu.VMEM((8, 4, D), BF16),
+            pltpu.VMEM((8, 2, PW * CH), BF16),
+            pltpu.VMEM((16, 8, HD), F32),
+            pltpu.VMEM((8, HD), F32),
+            pltpu.VMEM((TXT, D), F32),
+            pltpu.VMEM((TXT, D), F32),
+            pltpu.VMEM((PH, PW * CH), F32),
+            pltpu.VMEM((PH, 640), BF16),
+            pltpu.VMEM((4, TXT, 256), BF16),
+            pltpu.VMEM((4, TXT, 256), BF16),
+            dma((6,)),
+            dma((8, 3)),
+            dma((8, 3)),
+            dma((16,)),
+            dma((16,)),
+            dma((16,)),
+            dma((16,)),
+            dma((4,)),
+            dma((4,)),
+            dma((16,)),
+            dma((16,)),
+        ],
+        compiler_params=pltpu.CompilerParams(
+            collective_id=cid, has_side_effects=True, vmem_limit_bytes=50 * 2**20
+        ),
+    )(offset, text, tgrad, lat, gain, w_down, w_up, w_query, w_key, w_value, w_out)
+
+
+def place(x, y, z, core):
+    return 2 * x + z % 2, 4 * y + 2 * (z // 2) + core
+
+
+def tail_kernel(
+    small,
+    conv,
+    atx,
+    text,
+    gain,
+    w_down,
+    w_up,
+    w_query,
+    w_key,
+    w_value,
+    w_out,
+    every,
+    text_out,
+    wq,
+    wk,
+    wv,
+    wo,
+    small_in,
+    conv_in,
+    mixed,
+    mixed_in,
+    parts,
+    parts_in,
+    own,
+    local,
+    send_a,
+    recv_a,
+    send_c,
+    recv_c,
+    send_t,
+    recv_t,
+    send_p,
+    recv_p,
+    send_1,
+    recv_1,
+    send_2,
+    recv_2,
+    send_3,
+    recv_3,
+    send_4,
+    recv_4,
+    send_m,
+    recv_m,
+):
+    sx = lax.axis_index("sx")
+    sy = lax.axis_index("sy")
+    g, head = split_sy(sy)
+    mine = pl.ds(pl.multiple_of(head * HD, HD), HD)
+    loads = []
+    for at, (src, dst) in enumerate(
+        [
+            (w_query.at[:, mine], wq),
+            (w_key.at[:, mine], wk),
+            (w_value.at[:, mine], wv),
+            (w_out, wo),
+        ]
+    ):
+        copy = pltpu.make_async_copy(src, dst, local.at[at])
+        copy.start()
+        loads.append(copy)
+    core = sy % 2
+    x = sx // 2
+    y = sy // 4
+    z = 2 * ((sy // 2) % 2) + sx % 2
+    even = core == 0
+    p1 = jnp.where(even, x, z)
+    p2 = jnp.where(even, y, x)
+    p3 = jnp.where(even, z, y)
+
+    def chip(a, b, c):
+        a = a % 4
+        b = b % 4
+        c = c % 4
+        return place(
+            jnp.where(even, a, b), jnp.where(even, b, c), jnp.where(even, c, a), core
+        )
+
+    twin = place(x, y, z, 1 - core)
+    right = chip(p1, p2, p3 + 1)
+    left = chip(p1, p2, p3 + 3)
+    barrier = pltpu.get_barrier_semaphore()
+    peers = [chip(p1 + o, p2, p3) for o in range(1, 4)]
+    peers += [chip(p1, p2 + o, p3) for o in range(1, 4)]
+    peers += [right, left, twin]
+    for kind in ("head", "sx", "team"):
+        _, peer = ring(kind)
+        peers += [peer(o)[:2] for o in range(1, SIZES[kind])]
+    for to in peers:
+        pl.semaphore_signal(barrier, inc=1, device_id=to, device_id_type=MESH)
+    pl.semaphore_wait(barrier, len(peers))
+
+    _, peer = ring("head")
     copies = []
-    at = 0
-    for idx, (kind, mode) in enumerate(items):
-        slot, peer = ring(kind)
-        own_slot = split_sy(lax.axis_index("sy"))[1] if kind == "syhead" else slot
-        src = ins[idx] if mode == "gather" else ins[idx].at[own_slot]
-        own = pltpu.make_async_copy(src, outs[idx].at[slot], local.at[idx])
-        own.start()
-        copies.append(own)
-        for o in range(1, SIZES[kind]):
-            tx, ty, to = peer(o)
-            copy = pltpu.make_async_remote_copy(
-                src_ref=ins[idx] if mode == "gather" else ins[idx].at[to],
-                dst_ref=outs[idx].at[slot],
-                send_sem=send.at[at],
-                recv_sem=recv.at[at],
-                device_id=(tx, ty),
-                device_id_type=MESH,
-            )
-            copy.start()
-            copies.append(copy)
-            at += 1
+    for o in range(1, 4):
+        tx, ty, to = peer(o)
+        copies.append(
+            remote(small.at[to], small_in.at[g], send_a.at[o], recv_a.at[o], (tx, ty))
+        )
+        copies.append(
+            remote(conv.at[to], conv_in.at[g], send_c.at[o], recv_c.at[o], (tx, ty))
+        )
+    small_in[g] = small[g]
+    conv_in[g] = conv[g]
+    for load in loads:
+        load.wait()
     for copy in copies:
         copy.wait()
-
-
-def exchange(arrays, items, cid):
-    shapes = []
-    sems = 0
-    for array, (kind, mode) in zip(arrays, items):
-        sems += SIZES[kind] - 1
-        tail = array.shape if mode == "gather" else array.shape[1:]
-        shapes.append(jax.ShapeDtypeStruct((SIZES[kind],) + tail, array.dtype))
+    low = jnp.sum(small_in[...].astype(F32), axis=0).astype(BF16)
+    rest = jnp.sum(conv_in[...].astype(F32), axis=0).astype(BF16)
+    for e in range(32):
+        parts[e, 64:, :] = (
+            rest[16 * e : 16 * e + 16, :] if e < 5 else jnp.zeros((16, HD), BF16)
+        )
+
+    @pl.loop(0, 8)
+    def _(c):
+        at = pl.ds(pl.multiple_of(c * 512, 512), 512)
+        down = dot(low[:, :HD], wq[at, :], NT)
+        down = down + dot(low[:, HD : 2 * HD], wk[at, :], NT)
+        down = down + dot(low[:, 2 * HD : 3 * HD], wv[at, :], NT)
+        down = down * gain[:, at]
+        down = down + dot(low[:, 512:640], w_up[at, :], NT)
+        down = down - dot(low[:, 768:], w_down[:, at])
+        grad = dot(low[:, 384:512], wo[mine, at]) + dot(low[:, 640:768], w_down[:, at])
+        for k in range(4):
+            parts[4 * c + k, :32, :] = down[:, k * HD : (k + 1) * HD].astype(BF16)
+            parts[4 * c + k, 32:64, :] = grad[:, k * HD : (k + 1) * HD].astype(BF16)
+
+    e, peer = ring("team")
+    copies = []
+    for o in range(1, 32):
+        tx, ty, to = peer(o)
+        copies.append(
+            remote(parts.at[to], parts_in.at[e], send_p.at[o], recv_p.at[o], (tx, ty))
+        )
+    parts_in[e] = parts[e]
+
+    joined = jnp.concatenate([atx[h] for h in range(4)], axis=1)
+
+    @pl.loop(0, 8)
+    def _(c):
+        at = pl.ds(pl.multiple_of(c * 512, 512), 512)
+        out = dot(joined, wo[:, at])
+        for n in range(8):
+            mixed[n, :, at] = out[4 * n : 4 * n + 4, :].astype(BF16)
+
+    _, peer = ring("sx")
+    texts = []
+    for o in range(1, 8):
+        tx, ty, to = peer(o)
+        texts.append(
+            remote(mixed.at[to], mixed_in.at[sx], send_t.at[o], recv_t.at[o], (tx, ty))
+        )
+    mixed_in[sx] = mixed[sx]
+    for copy in copies:
+        copy.wait_recv()
+    own[...] = jnp.sum(parts_in[...].astype(F32), axis=0).astype(BF16)
+
+    here = every.at[core]
+    there = every.at[core]
+    spot = (p3 * 4 + p2) * 4 + p1
+    every[core, spot] = own[...]
+    ones = [
+        remote(own, here.at[spot], send_1.at[o], recv_1.at[o], chip(p1 + o, p2, p3))
+        for o in (1, 2, 3)
+    ]
+    for copy in texts:
+        copy.wait()
+    total = text[...].astype(F32)
+    for n in range(8):
+        total = total + mixed_in[n].astype(F32)
+    text_out[...] = total.astype(BF16)
+    for copy in ones:
+        copy.wait_recv()
+    line = here.at[pl.ds((p3 * 4 + p2) * 4, 4)]
+    twos = [
+        remote(line, line, send_2.at[o], recv_2.at[o], chip(p1, p2 + o, p3)) for o in (1, 2, 3)
+    ]
+    for copy in twos:
+        copy.wait_recv()
+
+    def slab(p):
+        return here.at[pl.ds((p % 4) * 16, 16)]
+
+    def half(p, h):
+        return here.at[pl.ds((p % 4) * 16 + 8 * h, 8)]
+
+    up = remote(slab(p3), slab(p3), send_3.at[0], recv_3.at[0], right)
+    dn = remote(slab(p3), slab(p3), send_3.at[1], recv_3.at[1], left)
+    twins = [remote(slab(p3), slab(p3), send_m.at[0], recv_m.at[0], twin)]
+    up.wait_recv()
+    far_up = remote(half(p3 + 3, 0), half(p3 + 3, 0), send_4.at[0], recv_4.at[0], right)
+    twins.append(remote(slab(p3 + 3), slab(p3 + 3), send_m.at[1], recv_m.at[1], twin))
+    dn.wait_recv()
+    far_dn = remote(half(p3 + 1, 1), half(p3 + 1, 1), send_4.at[1], recv_4.at[1], left)
+    twins.append(remote(slab(p3 + 1), slab(p3 + 1), send_m.at[2], recv_m.at[2], twin))
+    far_up.wait_recv()
+    far_dn.wait_recv()
+    twins.append(remote(slab(p3 + 2), slab(p3 + 2), send_m.at[3], recv_m.at[3], twin))
+    for copy in copies + ones + twos + [up, dn, far_up, far_dn]:
+        copy.wait_send()
+    for copy in twins:
+        copy.wait()
+
+
+def tail(small, conv, atx, text, gain, w_down, w_up, w_query, w_key, w_value, w_out, cid):
+    sds = jax.ShapeDtypeStruct
+    hbm = pl.BlockSpec(memory_space=pl.ANY)
+    dma = pltpu.SemaphoreType.DMA
     return pl.pallas_call(
-        functools.partial(exchange_kernel, items, len(arrays)),
-        out_shape=shapes,
-        in_specs=[pl.BlockSpec(memory_space=pl.ANY)] * len(arrays),
-        out_specs=[pl.BlockSpec(memory_space=pl.ANY)] * len(arrays),
+        tail_kernel,
+        out_shape=[sds((2, 64, 80, HD), BF16), sds((4, D), BF16)],
+        in_specs=vmem(7) + [hbm] * 4,
+        out_specs=vmem(2),
         scratch_shapes=[
-            pltpu.SemaphoreType.DMA((len(arrays),)),
-            pltpu.SemaphoreType.DMA((sems,)),
-            pltpu.SemaphoreType.DMA((sems,)),
+            pltpu.VMEM((D, HD), BF16),
+            pltpu.VMEM((D, HD), BF16),
+            pltpu.VMEM((D, HD), BF16),
+            pltpu.VMEM((512, D), BF16),
+            pltpu.VMEM((4, 32, 896), BF16),
+            pltpu.VMEM((4, 80, HD), BF16),
+            pltpu.VMEM((8, 4, D), BF16),
+            pltpu.VMEM((8, 4, D), BF16),
+            pltpu.VMEM((32, 80, HD), BF16),
+            pltpu.VMEM((32, 80, HD), BF16),
+            pltpu.VMEM((80, HD), BF16),
+            dma((4,)),
+        ]
+        + [dma((4,))] * 4
+        + [dma((8,))] * 2
+        + [dma((32,))] * 2
+        + [dma((4,))] * 10,
+        compiler_params=pltpu.CompilerParams(
+            collective_id=cid, has_side_effects=True, vmem_limit_bytes=50 * 2**20
+        ),
+    )(small, conv, atx, text, gain, w_down, w_up, w_query, w_key, w_value, w_out)
+
+
+def assemble_kernel(every, down, up, conv, gup):
+    def block(group, e):
+        sx = e % 8
+        i = e // 8
+        sy = 2 * group + i if i < 2 else 12 - 2 * group + i
+        x = sx // 2
+        y = sy // 4
+        z = 2 * ((sy // 2) % 2) + sx % 2
+        core = sy % 2
+        return core, (z * 4 + y) * 4 + x if core == 0 else (y * 4 + x) * 4 + z
+
+    for e in range(32):
+        cols = []
+        for group in range(4):
+            core, spot = block(group, e)
+            down[32 * group : 32 * group + 32, e * HD : (e + 1) * HD] = every[
+                core, spot, :32, :
+            ].astype(F32)
+            cols.append(every[core, spot, 32:64, :].astype(F32))
+            if e < 5:
+                at = 80 * group + 16 * e
+                piece = every[core, spot, 64:80, :].astype(F32)
+                if at < 288:
+                    conv[at : at + 16, :] = piece
+                else:
+                    gup[at - 288 : at - 272, :] = piece
+        up[e * HD : (e + 1) * HD, :] = jnp.concatenate(cols, axis=0).T
+
+
+def assemble(every):
+    sds = jax.ShapeDtypeStruct
+    return pl.pallas_call(
+        assemble_kernel,
+        out_shape=[
+            sds((HD, D), F32),
+            sds((D, HD), F32),
+            sds((288, HD), F32),
+            sds((CH, HD), F32),
         ],
-        compiler_params=pltpu.CompilerParams(collective_id=cid, has_side_effects=True),
-    )(*arrays)
+        in_specs=vmem(1),
+        out_specs=vmem(4),
+        compiler_params=pltpu.CompilerParams(vmem_limit_bytes=50 * 2**20),
+    )(every)
 
 
 def sigmoid(v):
@@ -302,10 +824,6 @@
             part_ref[m * IMG + r * PW : m * IMG + r * PW + PW, :] = reorder[
                 pl.ds(r, PW, stride=PH), :
             ].astype(BF16)
-
-
-def vmem(count):
-    return [pl.BlockSpec(memory_space=pltpu.VMEM)] * count
 
 
 def forward(info, *args):
@@ -435,8 +953,10 @@
     qdt,
     bias_itt,
     vis_row,
+    gup,
+    small_out,
+    conv,
     small,
-    conv,
     order,
     gpu_ref,
     do_ref,
@@ -563,17 +1083,20 @@
         grad = dpre_ref[:, c * PH : c * PH + PH, :].reshape(256, HD)
         total = total + dot(patches[c], grad, TN)
     for tap in range(3):
-        conv[tap * 96 : tap * 96 + 96, :] = total[tap * 128 : tap * 128 + 96, :]
+        conv[tap * 96 : tap * 96 + 96, :] = total[tap * 128 : tap * 128 + 96, :].astype(BF16)
+    conv[288:, :] = gup[...].astype(BF16)
+    small_out[...] = small[...].astype(BF16)
 
 
 def backward(info, *args):
     sds = jax.ShapeDtypeStruct
     return pl.pallas_call(
         backward_kernel,
-        out_shape=[sds((HD, 896), F32), sds((288, HD), F32)],
+        out_shape=[sds((HD, 896), BF16), sds((320, HD), BF16)],
         in_specs=[pl.BlockSpec(memory_space=pltpu.SMEM)] + vmem(len(args)),
         out_specs=vmem(2),
         scratch_shapes=[
+            pltpu.VMEM((HD, 896), F32),
             pltpu.VMEM((1024, HD), F32),
             pltpu.VMEM((1024, HD), BF16),
             pltpu.VMEM((1152, HD), BF16),
@@ -600,27 +1123,6 @@
     cosine = np.concatenate([np.cos(angle), np.cos(angle)], axis=1)
     sine = np.concatenate([-np.sin(angle), np.sin(angle)], axis=1)
     return jnp.asarray(np.stack([cosine, sine]).astype(np.float32))
-
-
-def angles(positions):
-    half = HD // 2
-    freq = jnp.exp(-(2.0 * jnp.arange(half, dtype=F32) / HD) * math.log(ROPE_BASE))
-    angle = positions.astype(F32)[:, None] * freq[None, :]
-    cosine = jnp.cos(angle)
-    sine = jnp.sin(angle)
-    return (
-        jnp.concatenate([cosine, cosine], axis=1),
-        jnp.concatenate([-sine, sine], axis=1),
-    )
-
-
-def split_wide(x):
-    high = x.astype(BF16)
-    return jnp.concatenate([high, (x - high.astype(F32)).astype(BF16)], axis=1)
-
-
-def head_columns(x, i):
-    return lax.dynamic_slice_in_dim(x, i * HD, HD, 1)
 
 
 def shards(
@@ -644,84 +1146,29 @@
     g, i = split_sy(sy)
     members = jnp.stack([sy_of(g, jnp.int32(m)) for m in range(4)])
     info = jnp.concatenate([jnp.stack([g, *members]), jnp.zeros((3,), jnp.int32)]).astype(jnp.int32)
-    gain = norm_gain.astype(F32)
-
-    text, tgrad, lat, offs = exchange(
-        [
-            text_tokens[0],
-            text_grad[0],
-            latent[0],
-            jnp.broadcast_to(image_offset.astype(F32)[:, None], (8, HD)),
-        ],
-        [("sx", "gather"), ("sx", "gather"), ("sx", "gather"), ("sy", "gather")],
+    gain = norm_gain.astype(F32)[None]
+
+    mix, nt, wd, wu, kvt, qdt, lat, phase, bias_it, bias_itt, bias_tt, vis_q, vis_row = lead(
+        image_offset,
+        text_tokens[0],
+        text_grad[0],
+        latent[0],
+        gain,
+        w_down_proj,
+        w_up_proj,
+        w_query,
+        w_key,
+        w_value,
+        w_out,
         1,
-    )
-    text = text.reshape(TXT, D)
-    tgrad = tgrad.reshape(TXT, D)
-    offsets = offs[:, 0, 0].astype(jnp.int32)
-
-    wide = text.astype(F32)
-    inverse = lax.rsqrt(jnp.mean(wide * wide, axis=-1, keepdims=True) + EPS)
-    left = jnp.concatenate(
-        [w_down_proj.astype(F32) * gain, wide * inverse * gain], axis=0
-    ).astype(BF16)
-    query = dot(left, w_query)
-    key = dot(left, w_key)
-    value = dot(left, w_value)
-    outer = dot(jnp.concatenate([w_up_proj.T, tgrad], axis=0), w_out, NT)
-    wd = split_wide(dot(w_down_proj, w_down_proj, NT))
-    wu = dot(w_down_proj, w_up_proj).astype(BF16)
-    own_off = image_offset[0]
-    token = jnp.arange(TXT, dtype=jnp.int32)
-    cosine, sine = angles(sy * SB + token + jnp.where(token >= own_off, IMG, 0))
-
-    def heads(x):
-        return x[HD:].reshape(TXT, 4, HD).transpose(1, 0, 2)
-
-    def swap(x):
-        return jnp.concatenate([x[..., HD // 2 :], x[..., : HD // 2]], axis=-1)
-
-    q_txt = heads(query)
-    k_txt = heads(key)
-    q_txt = (q_txt * cosine + swap(q_txt) * sine) * (SCALE * LOG2E)
-    k_txt = k_txt * cosine + swap(k_txt) * sine
-    kvt = jnp.concatenate([k_txt, heads(value)], axis=2).astype(BF16)
-    qdt = jnp.concatenate([q_txt, heads(outer)], axis=2).astype(BF16)
-    mix = jnp.concatenate(
-        [head_columns(x[:HD], i) for x in (query, key, value)], axis=1
-    ).astype(BF16)
-    nt = head_columns(outer[:HD], i).astype(BF16)
-
-    kvt, qdt, lat = exchange(
-        [kvt, qdt, lat.reshape(PH, PW * CH)],
-        [("syhead", "scatter"), ("group", "scatter"), ("sy", "gather")],
-        2,
     )
     kvt = kvt.reshape(512, 2 * HD)
     qdt = qdt.reshape(128, 2 * HD)
-    lat = jnp.pad(lat.reshape(256, PW * CH), ((0, 0), (CH, 96)))
-
-    blocks = jnp.arange(16, dtype=jnp.int32)
-    phase = jnp.stack(angles(blocks * SB + offsets))
     base = rope_base()
-    key_block = jnp.repeat(blocks, TXT)
-    key_token = jnp.tile(token, 16)
-    own_offs = offsets[members]
-    seen_it = (key_block[None, :] < members[:, None]) | (
-        (key_block[None, :] == members[:, None]) & (key_token[None, :] < own_offs[:, None])
-    )
-    bias_it = jnp.where(seen_it, 0.0, NEG).astype(F32)
-    query_block = jnp.repeat(members, TXT)
-    query_token = jnp.tile(token, 4)
-    vis = (query_block + (query_token >= jnp.repeat(own_offs, TXT)).astype(jnp.int32)).astype(F32)
-    seen_tt = (key_block[None, :] < query_block[:, None]) | (
-        (key_block[None, :] == query_block[:, None]) & (key_token[None, :] <= query_token[:, None])
-    )
-    bias_tt = jnp.where(seen_tt, 0.0, NEG).astype(F32)
 
     patches, da, sp, keys, values, queries, att, lse, part = forward(
         info,
-        lat,
+        lat.reshape(256, 640),
         w_down_conv,
         wd,
         mix,
@@ -731,8 +1178,8 @@
         base,
         kvt,
         qdt,
-        jnp.pad(bias_it, ((0, 4), (0, 0))),
-        jnp.broadcast_to(vis[:, None], (128, HD)),
+        bias_it,
+        vis_q,
         bias_tt,
     )
 
@@ -741,9 +1188,8 @@
         pred_grad[0].reshape(32, CH),
         w_up_out,
         att[1024:].reshape(4, TXT, HD),
-        3,
+        2,
     )
-    mixed_text = dot(atx.transpose(1, 0, 2).reshape(TXT, 512), w_out).astype(BF16)
 
     small, conv = backward(
         info,
@@ -764,62 +1210,33 @@
         base,
         kvt,
         qdt,
-        jnp.pad(bias_it.T, ((0, 0), (0, 124))),
-        jnp.broadcast_to(vis[None, :], (8, HD)),
+        bias_itt,
+        vis_row,
+        gup,
     )
 
-    small, conv, mixed_text = exchange(
-        [
-            small.reshape(4, 32, 896),
-            jnp.concatenate([conv, gup], axis=0).reshape(4, 80, HD),
-            mixed_text.reshape(8, 4, D),
-        ],
-        [("head", "scatter"), ("head", "scatter"), ("sx", "scatter")],
-        4,
+    every, text_out = tail(
+        small.reshape(4, 32, 896),
+        conv.reshape(4, 80, HD),
+        atx,
+        text_tokens[0],
+        gain,
+        w_down_proj,
+        w_up_proj,
+        w_query,
+        w_key,
+        w_value,
+        w_out,
+        3,
     )
-    text_out = (
-        text_tokens[0].astype(F32) + jnp.sum(mixed_text.astype(F32), axis=0)
-    ).astype(BF16)
-    small = jnp.sum(small, axis=0)
-    conv = jnp.sum(conv, axis=0)
-
-    low = small.astype(BF16)
-    down = (
-        dot(low[:, :HD], head_columns(w_query, i), NT)
-        + dot(low[:, HD : 2 * HD], head_columns(w_key, i), NT)
-        + dot(low[:, 2 * HD : 3 * HD], head_columns(w_value, i), NT)
-    ) * gain
-    down = down + dot(low[:, 512:640], w_up_proj, NT) - dot(low[:, 768:896], w_down_proj)
-    up = dot(low[:, 384:512], lax.dynamic_slice_in_dim(w_out, i * HD, HD, 0)) + dot(
-        low[:, 640:768], w_down_proj
-    )
-    parts = jnp.concatenate(
-        [
-            down.reshape(32, 32, HD).transpose(1, 0, 2),
-            up.reshape(32, 32, HD).transpose(1, 0, 2),
-            jnp.pad(conv, ((0, 16), (0, 0))).reshape(32, 3, HD),
-            jnp.zeros((32, 13, HD), F32),
-        ],
-        axis=1,
-    ).astype(BF16)
-    (summed,) = exchange([parts], [("team", "scatter")], 5)
-    own = jnp.sum(summed.astype(F32), axis=0).astype(BF16)
-    (column,) = exchange([own], [("sx", "gather")], 6)
-    (every,) = exchange([column], [("sy", "gather")], 7)
-
-    low_half = every[:8].reshape(4, 2, 8, 80, HD)
-    high_half = every[8:].reshape(4, 2, 8, 80, HD)[::-1]
-    every = jnp.concatenate([low_half, high_half], axis=1).reshape(4, 32, 80, HD).astype(F32)
-    grad_down_proj = every[:, :, :32].transpose(0, 2, 1, 3).reshape(HD, D)
-    grad_up_proj = every[:, :, 32:64].transpose(1, 3, 0, 2).reshape(D, HD)
-    rest = every[:, :, 64:67].reshape(4, 96, HD)[:, :80].reshape(320, HD)
+    grad_down_proj, grad_up_proj, grad_conv, grad_up_out = assemble(every)
     return (
         pred.reshape(1, 2, PW * CH),
         text_out[None],
-        rest[:288],
+        grad_conv,
         grad_down_proj,
         grad_up_proj,
-        rest[288:].T,
+        grad_up_out.T,
     )
 
 

time: 264 us -> 168 us (0.64)
  the two profiles are of different devices: /device:TPU:113 before, /device:TPU:1 now
where the time goes in v2:
time: 168 us; the launch traced here: 167 us
  Pallas kernels  153 us (91%)
  local copies, waits for them, and re-layouts  12.2 us (7%)
    pallas_call x1, Pallas kernels, tail(): pl.pallas_call(tail_kernel, out_shape=[sds((2, 64, 80, HD), BF16), sds((4...  47.7 us
    pallas_call x1, Pallas kernels, lead(): pl.pallas_call(lead_kernel, out_shape=[sds((HD, 384), BF16), sds((HD, HD)...  27.7 us
    pallas_call x1, Pallas kernels, backward(): pl.pallas_call(backward_kernel, out_shape=[sds((HD, 896), BF16), sds((320...  26.7 us
    pallas_call x1, Pallas kernels, middle(): pl.pallas_call(middle_kernel, out_shape=[sds((32, 32, HD), BF16), sds((32...  25.9 us
    pallas_call x1, Pallas kernels, forward(): pl.pallas_call(forward_kernel, out_shape=[sds((16, 256, 384), BF16), sds(...  22.3 us
    unnamed x38, local copies, waits for them, and re-layouts  10.1 us

profile of v2, /device:TPU:1, one launch (start us, length us, event | category | flops | bytes accessed | tf_op | source)
XLA Modules:
  0.0 167.2 jit_solution(7207906652940700513)
XLA Ops:
  0.7 0.1 concatenate.3.info
  0.8 0.7 broadcast_in_dim.11
  2.1 0.0 copy-start
  2.1 1.2 copy-done
  3.3 0.0 copy-start.2
  3.3 1.2 copy-done.2
  4.6 0.0 copy-start.6
  4.6 0.8 copy-done.6
  5.3 0.0 copy-start.8
  5.3 0.8 copy-done.8
  6.1 0.0 copy-start.10
  6.1 0.7 copy-done.10
  6.8 0.0 copy-start.12
  6.8 0.0 copy-start.14
  6.8 27.7 %shard_map.190 = (bf16[128,384]{1,0:T(8,128)(2,1)S(1)}, bf16[128,128]{1,0:T(8,128)(2,1)S(1)}, bf16[128,256]{1,0:T(8,128)(2,1)S(1)}, bf16[128,128]{1,0:T(8,128)(2...) custom-call(s32[1]{0:T(128)S(6)} %copy.23.offset, ...), custom_call_target="tpu_custom_call" | custom-call | tf_op jit(solution)/shard_map/pallas_call | solution.py:317
  34.5 0.0 copy-done.12
  34.5 0.0 copy-done.14
  34.5 0.0 copy-start.15
  34.5 0.0 copy-start.17
  34.6 22.3 %shard_map.191 = (bf16[16,256,384]{2,1,0:T(8,128)(2,1)}, bf16[16,256,128]{2,1,0:T(8,128)(2,1)S(1)}, bf16[16,256,128]{2,1,0:T(8,128)(2,1)}, bf16[4096,128]{1,0:T(...) custom-call(s32[8]{0:T(128)S(1)} %concatenate.3.info, ...), custom_call_target="tpu_custom_call" | custom-call | flops 8000000000 | bytes 16777216 | tf_op jit(solution)/shard_map/pallas_call | solution.py:831
  56.9 0.0 copy-start.5
  56.9 0.7 copy-done.5
  57.6 0.6 slice.3
  58.2 0.0 copy-done.15
  58.2 0.7 copy.21.w_uo
  58.9 0.0 copy-done.17
  58.9 0.7 reshape_squeeze.3.pgrad
  59.6 25.9 %shard_map.192 = (bf16[32,32,128]{2,1,0:T(8,128)(2,1)}, bf16[32,32]{1,0:T(8,128)(2,1)}, f32[32,128]{1,0:T(8,128)}, bf16[4,32,128]{2,1,0:T(8,128)(2,1)}) custom-call(bf16[32,32,128]{2,1,0:T(8,128)(2,1)} %bitcast.19, bf16[32,32]{1,0:T(8,128)(2,1)} %reshape_squeeze.3.pgrad, bf16[128,32]{1,0:T(8,128)(2,1)} %copy.21.w_uo, bf16[4,32,128]{2,1,0:T(8,128)(2,1)} %bitcast.35), custom_call_target="tpu_custom_call" | custom-call | tf_op jit(solution)/shard_map/pallas_call | solution.py:918
  85.5 0.0 copy-start.11
  85.5 0.9 copy-done.11
  86.5 0.0 copy-start.13
  86.5 0.7 copy-done.13
  87.2 0.0 copy-start.1
  87.2 0.0 copy-start.3
  87.2 0.0 copy-start.7
  87.2 0.0 copy-start.9
  87.2 26.7 %shard_map.193 = (bf16[128,896]{1,0:T(8,128)(2,1)S(1)}, bf16[320,128]{1,0:T(8,128)(2,1)S(1)}) custom-call(s32[8]{0:T(128)S(1)} %concatenate.3.info, bf16[16,256,384]{2,1,0:T(8,128)(2,1)} %get-tuple-element.54.patches, bf16[16,256,128]{2,1,0:T(8,128)(2,1)S(1)} %get-tuple-element.55.da_ref, bf16[16,256,128]{2,1,0:T(8,128)(2,1)} %get-tuple-element.56.sp_ref, ...), custom_call_target="tpu_custom_call" | custom-call | flops 16000000000 | bytes 16777216 | tf_op jit(solution)/shard_map/pallas_call | solution.py:1093
  113.9 0.0 copy-done.1
  113.9 0.0 copy-done.3
  114.0 0.0 copy-done.7
  114.0 0.0 copy-done.9
  114.0 0.0 copy-start.16
  114.0 47.7 %shard_map.194 = (bf16[2,64,80,128]{3,2,1,0:T(8,128)(2,1)}, bf16[4,4096]{1,0:T(4,128)(2,1)S(1)}) custom-call(bf16[4,32,896]{2,1,0:T(8,128)(2,1)S(1)} %bitcast.20, bf16[4,80,128]{2,1,0:T(8,128)(2,1)S(1)} %bitcast.25, bf16[4,32,128]{2,1,0:T(8,128)(2,1)S(1)} %copy-done.9, bf16[4,4096]{1,0:T(4,128)(2,1)S(1)} %bitcast.24, f32[1,4096]{1,0:T(1,128)S(1)} %bitcast.22, ...), custom_call_target="tpu_custom_call" | custom-call | tf_op jit(solution)/shard_map/pallas_call | solution.py:586
  161.7 0.0 copy-start.4
  161.8 1.7 %copy-done.4 = bf16[2,64,80,128]{3,2,1,0:T(8,128)(2,1)S(1)} copy-done((bf16[2,64,80,128]{3,2,1,0:T(8,128)(2,1)S(1)}, bf16[2,64,80,128]{3,2,1,0:T(8,128)(2,1)}, u32[]{:S(2)}) %copy-start.4) | copy-done | bytes 2621464
  163.5 2.5 %shard_map.195 = (f32[128,4096]{1,0:T(8,128)}, f32[4096,128]{1,0:T(8,128)}, f32[288,128]{1,0:T(8,128)}, f32[32,128]{1,0:T(8,128)}) custom-call(bf16[2,64,80,128]{3,2,1,0:T(8,128)(2,1)S(1)} %copy-done.4), custom_call_target="tpu_custom_call" | custom-call | tf_op jit(solution)/shard_map/pallas_call | solution.py:646
  165.9 0.0 copy-done.16
  165.9 0.7 reshape.44
  166.6 0.6 copy.24
  (1 shorter events, 0.0 us)
Async XLA Ops:
  2.1 1.2 copy-start
  3.3 1.2 copy-start.2
  4.6 0.8 copy-start.6
  5.3 0.8 copy-start.8
  6.1 0.7 copy-start.10
  6.8 27.8 %copy-start.12 = (bf16[288,128]{1,0:T(8,128)(2,1)S(1)}, bf16[288,128]{1,0:T(8,128)(2,1)}, u32[]{:S(2)}) copy-start(bf16[288,128]{1,0:T(8,128)(2,1)} %wconv.1) | copy-start | bytes 221188
  6.8 27.8 %copy-start.14 = (f32[2,256,128]{2,1,0:T(8,128)S(1)}, f32[2,256,128]{2,1,0:T(8,128)}, u32[]{:S(2)}) copy-start(f32[2,256,128]{2,1,0:T(8,128)} %constant.41.clone.base) | copy-start | bytes 786436
  34.5 23.7 %copy-start.15 = (bf16[128,32]{0,1:T(8,128)(2,1)S(1)}, bf16[128,32]{0,1:T(8,128)(2,1)}, u32[]{:S(2)}) copy-start(bf16[128,32]{0,1:T(8,128)(2,1)} %param.26) | copy-start | bytes 24580
  34.5 24.4 %copy-start.17 = (bf16[1,2,512]{2,1,0:T(2,128)(2,1)S(1)}, bf16[1,2,512]{2,1,0:T(2,128)(2,1)}, u32[]{:S(2)}) copy-start(bf16[1,2,512]{2,1,0:T(2,128)(2,1)} %param.27) | copy-start | bytes 6148
  56.9 0.7 copy-start.5
  85.5 1.0 copy-start.11
  86.5 0.7 copy-start.13
  87.2 26.8 %copy-start.1 = (bf16[128,4096]{1,0:T(8,128)(2,1)S(1)}, bf16[128,4096]{1,0:T(8,128)(2,1)}, u32[]{:S(2)}) copy-start(bf16[128,4096]{1,0:T(8,128)(2,1)} %w_down.3) | copy-start | bytes 3145732
  87.2 26.8 %copy-start.3 = (bf16[4096,128]{1,0:T(8,128)(2,1)S(1)}, bf16[4096,128]{1,0:T(8,128)(2,1)}, u32[]{:S(2)}) copy-start(bf16[4096,128]{1,0:T(8,128)(2,1)} %w_up.3) | copy-start | bytes 3145732
  87.2 26.8 %copy-start.7 = (bf16[1,4,4096]{2,1,0:T(4,128)(2,1)S(1)}, bf16[1,4,4096]{2,1,0:T(4,128)(2,1)}, u32[]{:S(2)}) copy-start(bf16[1,4,4096]{2,1,0:T(4,128)(2,1)} %param.15) | copy-start | bytes 98308
  87.2 26.8 %copy-start.9 = (bf16[4,32,128]{2,1,0:T(8,128)(2,1)S(1)}, bf16[4,32,128]{2,1,0:T(8,128)(2,1)}, u32[]{:S(2)}) copy-start(bf16[4,32,128]{2,1,0:T(8,128)(2,1)} %get-tuple-element.67.atx) | copy-start | bytes 98308
  114.0 52.0 %copy-start.16 = (bf16[32,32]{1,0:T(8,128)(2,1)S(1)}, bf16[32,32]{1,0:T(8,128)(2,1)}, u32[]{:S(2)}) copy-start(bf16[32,32]{1,0:T(8,128)(2,1)} %get-tuple-element.53) | copy-start | bytes 6148
  161.7 1.7 %copy-start.4 = (bf16[2,64,80,128]{3,2,1,0:T(8,128)(2,1)S(1)}, bf16[2,64,80,128]{3,2,1,0:T(8,128)(2,1)}, u32[]{:S(2)}) copy-start(bf16[2,64,80,128]{3,2,1,0:T(8,128)(2,1)} %get-tuple-element.69.every) | copy-start | bytes 7864324

commit v3 on v0

v3 whole, which is shorter than its diff:
```python
import functools
import math
import types

import jax
import jax.numpy as jnp
import numpy as np
from jax import lax
from jax.experimental import pallas as pl
from jax.experimental.pallas import tpu as pltpu
from jax.sharding import PartitionSpec as P

MESH = pl.DeviceIdType.MESH
F32 = jnp.float32
BF16 = jnp.bfloat16
HD = 128
SB = 288
TXT = 32
IMG = 256
PH = 16
PW = 16
CH = 32
D = 4096
EPS = 1e-05
NEG = -1e30
LOG2E = math.log2(math.e)
SCALE = HD ** (-0.5)
ROPE_BASE = 500000.0
SIZES = {"sx": 8, "sy": 16, "group": 4, "head": 4, "team": 32}
NT = (((1,), (1,)), ((), ()))
TN = (((0,), (0,)), ((), ()))


def dot(a, b, dims=(((1,), (0,)), ((), ()))):
    return lax.dot_general(a, b, dims, preferred_element_type=F32)


def vmem(count):
    return [pl.BlockSpec(memory_space=pltpu.VMEM)] * count


def mod(a, n):
    return a % n if isinstance(a, int) else lax.rem(a, n)


def div(a, n):
    return a // n if isinstance(a, int) else lax.div(a, n)


def sy_of(g, i):
    if isinstance(i, int):
        return 2 * g + i if i < 2 else 12 - 2 * g + i
    return jnp.where(i < 2, 2 * g + i, 12 - 2 * g + i)


def split_sy(sy):
    low = sy < 8
    g = jnp.where(low, div(sy, 2), div(15 - sy, 2))
    i = mod(sy, 2) + jnp.where(low, 0, 2)
    return g, i


def ring(kind):
    sx = lax.axis_index("sx")
    sy = lax.axis_index("sy")
    g, i = split_sy(sy)
    if kind == "sx":
        return sx, lambda o: (mod(sx + o, 8), sy, mod(sx + o, 8))
    if kind == "sy":
        return sy, lambda o: (sx, mod(sy + o, 16), mod(sy + o, 16))
    if kind == "group":
        return i, lambda o: (sx, sy_of(g, mod(i + o, 4)), mod(i + o, 4))
    if kind == "head":
        return g, lambda o: (sx, sy_of(mod(g + o, 4), i), mod(g + o, 4))
    e = i * 8 + sx

    def peer(o):
        f = mod(e + o, 32)
        return mod(f, 8), sy_of(g, div(f, 8)), f

    return e, peer


def remote(src, dst, send, recv, to):
    copy = pltpu.make_async_remote_copy(
        src_ref=src,
        dst_ref=dst,
        send_sem=send,
        recv_sem=recv,
        device_id=to,
        device_id_type=MESH,
    )
    copy.start()
    return copy


class Fan:
    def __init__(self, kind, source, land, sems, slot_of=None):
        own, peer = ring(kind)
        self.land = land.at[pl.ds(0, SIZES[kind] - 1)]
        self.sems = sems

        @pl.loop(1, SIZES[kind])
        def _(o):
            tx, ty, to = peer(o)
            src = source if slot_of is None else source.at[slot_of(ty, to)]
            remote(src, land.at[own], sems.at[0], sems.at[1], (tx, ty))

    def arrived(self):
        pltpu.make_async_copy(self.land, self.land, self.sems.at[1]).wait()

    def sent(self):
        pltpu.make_async_copy(self.land, self.land, self.sems.at[0]).wait()


def sigmoid(v):
    return 1.0 / (1.0 + jnp.exp(-v))


def turn(v, cosine, sine):
    return v * cosine + pltpu.roll(v, 64, 1) * sine


def trig(shape, position):
    lane = lax.broadcasted_iota(jnp.int32, shape, 1)
    step = (lane % 64).astype(F32)
    angle = position * jnp.exp(step * (-2.0 / HD * math.log(ROPE_BASE)))
    sine = jnp.sin(angle)
    return jnp.cos(angle), jnp.where(lane < 64, -sine, sine)


def tables(j, phase_ref, base_ref):
    pc = phase_ref[0, pl.ds(j, 1), :]
    ps = phase_ref[1, pl.ds(j, 1), :]
    bc = base_ref[0]
    bs = base_ref[1]
    return pc * bc - ps * bs, ps * bc + pc * bs


def row_scale(da, wd):
    both = dot(da, wd)
    dawd = both[:, :HD] + both[:, HD:]
    mean = jnp.sum(dawd * da.astype(F32), axis=1, keepdims=True) * (1.0 / D)
    return dawd, lax.rsqrt(mean + EPS)


def lanes(column):
    return column.T[:1, :]


def place(x, y, z, core):
    return 2 * x + mod(z, 2), 4 * y + 2 * div(z, 2) + core


class Spread:
    def __init__(self, every, sems):
        self.every = every
        self.sems = sems
        sx = lax.axis_index("sx")
        sy = lax.axis_index("sy")
        self.core = mod(sy, 2)
        x = div(sx, 2)
        y = div(sy, 4)
        z = 2 * mod(div(sy, 2), 2) + mod(sx, 2)
        self.even = self.core == 0
        self.p1 = jnp.where(self.even, x, z)
        self.p2 = jnp.where(self.even, y, x)
        self.p3 = jnp.where(self.even, z, y)
        self.twin = place(x, y, z, 1 - self.core)
        self.here = every.at[self.core]
        self.spot = (self.p3 * 4 + self.p2) * 4 + self.p1
        self.live = []

    def chip(self, a, b, c):
        a = mod(a, 4)
        b = mod(b, 4)
        c = mod(c, 4)
        even = self.even
        return place(
            jnp.where(even, a, b), jnp.where(even, b, c), jnp.where(even, c, a), self.core
        )

    def send(self, ref, n, to):
        copy = remote(ref, ref, self.sems.at[0, n], self.sems.at[1, n], to)
        self.live.append(copy)
        return copy

    def slab(self, p):
        return self.here.at[pl.ds(mod(p, 4) * 16, 16)]

    def plane(self, block):
        self.every[self.core, self.spot] = block
        mine = self.here.at[self.spot]

        @pl.loop(1, 16)
        def _(o):
            to = self.chip(self.p1 + mod(o, 4), self.p2 + div(o, 4), self.p3)
            remote(mine, mine, self.sems.at[0, 0], self.sems.at[1, 0], to)

    def slabs(self):
        plane = self.here.at[pl.ds(0, 15)]
        pltpu.make_async_copy(plane, plane, self.sems.at[1, 0]).wait()
        own = self.slab(self.p3)
        self.wave = [self.send(own, o, self.chip(self.p1, self.p2, self.p3 + o)) for o in (1, 3, 2)]
        self.twins = [self.send(own, 4, self.twin)]

    def pass_on(self):
        for o, copy in zip((1, 3, 2), self.wave):
            copy.wait_recv()
            self.twins.append(self.send(self.slab(self.p3 + 4 - o), 4 + o, self.twin))

    def arrived(self):
        for copy in self.twins:
            copy.wait_recv()

    def sent(self):
        plane = self.here.at[pl.ds(0, 15)]
        pltpu.make_async_copy(plane, plane, self.sems.at[0, 0]).wait()
        for copy in self.live:
            copy.wait_send()


def greet(wide):
    barrier = pltpu.get_barrier_semaphore()
    for kind in ("team", "sy"):
        _, peer = ring(kind)

        @pl.loop(1, SIZES[kind])
        def _(o):
            tx, ty, _ = peer(o)
            pl.semaphore_signal(barrier, inc=1, device_id=(tx, ty), device_id_type=MESH)

    @pl.loop(1, 16)
    def _(o):
        to = wide.chip(wide.p1 + mod(o, 4), wide.p2 + div(o, 4), wide.p3)
        pl.semaphore_signal(barrier, inc=1, device_id=to, device_id_type=MESH)

    @pl.loop(1, 4)
    def _(o):
        to = wide.chip(wide.p1, wide.p2, wide.p3 + o)
        pl.semaphore_signal(barrier, inc=1, device_id=to, device_id_type=MESH)

    pl.semaphore_wait(barrier, 31 + 15 + 15 + 3)


def masks(r, g, members):
    block = lax.broadcasted_iota(jnp.int32, (16, HD), 0).astype(F32)
    cosine, sine = trig((16, HD), block * float(SB) + jnp.max(r.offs[...], axis=1))
    r.phase[0] = cosine
    r.phase[1] = sine
    starts = [r.offs[b][:1, :] for b in members]
    row = lax.broadcasted_iota(jnp.int32, (512, TXT), 0)
    query = lax.broadcasted_iota(jnp.int32, (512, TXT), 1)
    for m in range(4):
        b = members[m]
        seen = (row // TXT < b) | ((row // TXT == b) & (row % TXT <= query))
        r.bias_tt[:, m * TXT : (m + 1) * TXT] = jnp.where(seen, 0.0, NEG)
    lane = lax.broadcasted_iota(jnp.int32, (8, HD), 1)
    start = starts[0]
    owner = jnp.full((8, HD), members[0], jnp.int32)
    for m in range(1, 4):
        start = jnp.where(lane // TXT == m, starts[m], start)
        owner = jnp.where(lane // TXT == m, members[m], owner)
    late = jnp.where((lane % TXT).astype(F32) >= start, 1.0, 0.0)
    r.vis[...] = late + owner.astype(F32)
    lane = lax.broadcasted_iota(jnp.int32, (512, HD), 1)
    row = lax.broadcasted_iota(jnp.int32, (512, HD), 0)
    start = jnp.broadcast_to(starts[0], (512, HD))
    owner = jnp.full((512, HD), members[0], jnp.int32)
    for m in range(1, 4):
        start = jnp.where(lane == m, starts[m], start)
        owner = jnp.where(lane == m, members[m], owner)
    seen = (row // TXT < owner) | ((row // TXT == owner) & ((row % TXT).astype(F32) < start))
    r.bias_ti[...] = jnp.where(seen, 0.0, NEG)


def down_block(r):
    r.wpad[...] = jnp.zeros_like(r.wpad)
    for tap in range(3):
        r.wpad[tap * 128 : tap * 128 + 96, :] = r.wconv[tap * 96 : tap * 96 + 96, :].astype(F32)
    mid = r.lat_all[...].reshape(256, 640).astype(F32)
    row = lax.broadcasted_iota(jnp.int32, mid.shape, 0) % PH
    r.wide[0] = jnp.where(row == 0, 0.0, pltpu.roll(mid, 1, 0))
    r.wide[1] = mid
    r.wide[2] = jnp.where(row == PH - 1, 0.0, pltpu.roll(mid, 16 * PH - 1, 0))
    weight = r.wpad[...].astype(BF16)
    for c in range(PW):
        for tap in range(3):
            r.patches[c, :, tap * 128 : tap * 128 + 128] = r.wide[
                tap, :, c * CH : c * CH + 128
            ].astype(BF16)
        pre = dot(r.patches[c], weight)
        sig = sigmoid(pre)
        r.da[:, c * PH : c * PH + PH, :] = (pre * sig).astype(BF16).reshape(16, PH, HD)
        r.sp[:, c * PH : c * PH + PH, :] = (
            (sig * (1.0 + pre * (1.0 - sig))).astype(BF16).reshape(16, PH, HD)
        )


def project(r, members):
    mix_kv = r.mix[:, HD:]
    mix_q = r.mix[:, :HD]
    wd = r.wd[...]

    @pl.loop(0, 16, unroll=4)
    def _(j):
        da = r.da[j]
        _, inv = row_scale(da, wd)
        kv = dot(da, mix_kv) * inv
        cosine, sine = tables(j, r.phase, r.base)
        rows = pl.ds(pl.multiple_of(j * IMG, IMG), IMG)
        r.k[rows, :] = turn(kv[:, :HD], cosine, sine).astype(BF16)
        r.v[rows, :] = kv[:, HD:].astype(BF16)
        r.vt[:, rows] = kv[:, HD:].T.astype(BF16)

    for m in range(4):
        da = r.da[members[m]]
        r.da_own[m * IMG : (m + 1) * IMG, :] = da
        _, inv = row_scale(da, wd)
        cosine, sine = tables(members[m], r.phase, r.base)
        r.q[m * IMG : (m + 1) * IMG, :] = (
            turn(dot(da, mix_q) * inv, cosine, sine) * (SCALE * LOG2E)
        ).astype(BF16)


def tile_rows(j):
    return pl.ds(pl.multiple_of(j * 512, 512), 512)


def absorb(state, scores, vt, e_ref, m_ref):
    top = jnp.max(scores, axis=0, keepdims=True)
    new = top if state is None else jnp.maximum(state[0], top)
    raised = jnp.exp2(scores - new)
    low = raised.astype(BF16)
    e_ref[...] = low
    m_ref[...] = jnp.broadcast_to(new, m_ref.shape)
    total = jnp.sum(raised, axis=0, keepdims=True)
    mixed = dot(vt, low)
    if state is None:
        return new, total, mixed
    old = jnp.exp2(state[0] - new)
    return new, state[1] * old + total, state[2] * old + mixed


def conclude(r, p, width, state):
    peak, total, acc = state
    r.att[p * 512 : p * 512 + width, :] = (acc / total).T.astype(BF16)
    r.lse[p, :, :width] = jnp.broadcast_to(peak + jnp.log2(total), (8, width))


def diagonal_mask(scores):
    bottom = lax.broadcasted_iota(jnp.int32, scores.shape, 0) >= IMG
    left = lax.broadcasted_iota(jnp.int32, scores.shape, 1) < IMG
    return jnp.where(bottom & left, NEG, scores)


def attend_images(r, p, diagonal, text_ready):
    q = r.q[p * 512 : p * 512 + 512, :]
    base = 4 * p

    def tile(j):
        return dot(r.k[tile_rows(j), :], q, NT)

    state = absorb(
        None,
        diagonal_mask(tile(diagonal)),
        r.vt[:, tile_rows(diagonal)],
        r.e_img.at[base + diagonal],
        r.m_img.at[base + diagonal],
    )

    def body(j, state):
        return absorb(
            state, tile(j), r.vt[:, tile_rows(j)], r.e_img.at[base + j], r.m_img.at[base + j]
        )

    state = lax.fori_loop(0, diagonal, body, state)
    text_ready()
    scores = dot(r.kt[...], q, NT)
    bias = jnp.concatenate(
        [
            jnp.broadcast_to(r.bias_ti[:, 2 * p + half : 2 * p + half + 1], (512, IMG))
            for half in range(2)
        ],
        axis=1,
    )
    scores = jnp.where(bias < 0.0, NEG, scores)
    state = absorb(state, scores, r.vtt[...], r.e_txt.at[p], r.m_txt.at[p])
    conclude(r, p, 512, state)


def attend_text(r, count, kept):
    q = r.q[1024:, :]
    vis = r.vis[:1, :]
    scores = jnp.where(r.bias_tt[...] < 0.0, NEG, dot(r.kt[...], q, NT))
    state = absorb(None, scores, r.vtt[...], r.e_q.at[8], r.m_q.at[8])

    def body(j, state):
        scores = dot(r.k[tile_rows(j), :], q, NT)
        block = 2 * j + (lax.broadcasted_iota(jnp.int32, scores.shape, 0) >= IMG).astype(jnp.int32)
        scores = jnp.where(block.astype(F32) < vis, scores, NEG)
        return absorb(state, scores, r.vt[:, tile_rows(j)], r.e_q.at[j], r.m_q.at[j])

    conclude(r, 2, 128, lax.fori_loop(0, count, body, state))


def normalise(e_ref, m_ref, lse):
    factor = jnp.exp2(m_ref[:1, :] - lse)
    e_ref[...] = (e_ref[...].astype(F32) * factor).astype(BF16)


def backward_rows(r, p, width):
    rows = slice(p * 512, p * 512 + width)
    q = r.q[rows, :]
    do = r.do[rows, :]
    sums = jnp.sum(do.astype(F32) * r.att[rows, :].astype(F32), axis=1, keepdims=True)
    return q, do, lanes(jnp.broadcast_to(sums, (width, HD)))


def backward_images(r, p, diagonal, members):
    q, do, delta = backward_rows(r, p, 512)
    base = 4 * p

    probs = r.e_txt[p].astype(F32)
    grad = (probs * (dot(r.vtx[...], do, NT) - delta)).astype(BF16)
    r.dqs[...] = dot(grad, r.kt[...], TN)

    @pl.loop(0, diagonal + 1)
    def _(j):
        at = tile_rows(j)
        keys = r.k[at, :]
        probs = r.e_img[base + j]
        grad = (probs.astype(F32) * (dot(r.v[at, :], do, NT) - delta)).astype(BF16)
        r.dv[at, :] += dot(probs, do)
        r.dk[at, :] += dot(grad, q)
        r.dqs[...] += dot(grad, keys, TN)

    for half in range(2):
        r.dq[2 * p + half] = r.dqs[half * IMG : (half + 1) * IMG, :]


def backward_text(r, count):
    q, do, delta = backward_rows(r, 2, 128)

    @pl.loop(0, count)
    def _(j):
        at = tile_rows(j)
        probs = r.e_q[j]
        grad = (probs.astype(F32) * (dot(r.v[at, :], do, NT) - delta)).astype(BF16)
        r.dv[at, :] += dot(probs, do)
        r.dk[at, :] += dot(grad, q)


def image_grads(r, g):
    wd = r.wd[...]
    mix = r.mix[...]
    r.small[...] = jnp.zeros_like(r.small)

    @pl.loop(0, 16, unroll=2)
    def _(j):
        group, m = split_sy(j)
        ours = (group == g).astype(F32)
        da = r.da[j]
        da_wide = da.astype(F32)
        dawd, inv = row_scale(da, wd)
        cosine, sine = tables(j, r.phase, r.base)
        at = pl.ds(pl.multiple_of(j * IMG, IMG), IMG)
        gq = turn(r.dq[m] * (ours * SCALE), cosine, -sine)
        gk = turn(r.dk[at, :] * (1.0 / LOG2E), cosine, -sine)
        grads = jnp.concatenate([gq, gk, r.dv[at, :]], axis=1).astype(BF16)
        back = dot(grads, mix, NT)
        cube = (inv * inv * inv) * (jnp.sum(back * da_wide, axis=1, keepdims=True) * (1.0 / D))
        grad = (inv * back - cube * dawd + r.ex[m] * ours) * r.sp[j].astype(F32)
        r.dpre[j] = grad.astype(BF16)
        r.small[:, :384] += dot((da_wide * inv).astype(BF16), grads, TN)
        r.small[:, 384:] += dot((da_wide * cube).astype(BF16), da, TN)


def conv_grad(r):
    total = jnp.zeros((384, HD), F32)
    for c in range(PW):
        grad = r.dpre[:, c * PH : c * PH + PH, :].reshape(256, HD)
        total = total + dot(r.patches[c], grad, TN)
    rows = [total[tap * 128 : tap * 128 + 96, :] for tap in range(3)] + [r.gup[...]]
    whole = jnp.concatenate(rows, axis=0).astype(BF16)
    for n in range(4):
        r.conv[n] = whole[80 * n : 80 * n + 80, :]


def block_of(group, e):
    i = div(e, 8)
    sx = mod(e, 8)
    sy = sy_of(group, i)
    x = div(sx, 2)
    y = div(sy, 4)
    z = 2 * mod(div(sy, 2), 2) + mod(sx, 2)
    core = mod(i, 2)
    return core, jnp.where(core == 0, (z * 4 + y) * 4 + x, (y * 4 + x) * 4 + z)


def lay_up(r):
    @pl.loop(0, 32, unroll=2)
    def _(e):
        cols = [r.every_u[block_of(group, e)].astype(F32) for group in range(4)]
        at = pl.ds(pl.multiple_of(e * HD, HD), HD)
        r.grad_up[at, :] = jnp.concatenate(cols, axis=0).T.astype(BF16)


def lay_down(r):
    @pl.loop(0, 32, unroll=2)
    def _(e):
        at = pl.ds(pl.multiple_of(e * HD, HD), HD)
        for group in range(4):
            r.grad_down[32 * group : 32 * group + 32, at] = r.every_d[block_of(group, e)]


def whole_kernel(names, *refs):
    r = types.SimpleNamespace(**dict(zip(names, refs)))
    sx = lax.axis_index("sx")
    sy = lax.axis_index("sy")
    g, head = split_sy(sy)
    members = [sy_of(g, m) for m in range(4)]
    mine = pl.ds(pl.multiple_of(head * HD, HD), HD)
    loads = []
    for at, (src, dst) in enumerate(
        [
            (r.w_down, r.dn),
            (r.w_up, r.up),
            (r.w_query, r.wq),
            (r.w_key, r.wk),
            (r.w_value, r.wv),
            (r.w_out, r.wo),
        ]
    ):
        copy = pltpu.make_async_copy(src, dst, r.local.at[at])
        copy.start()
        loads.append(copy)
    wide_u = Spread(r.every_u, r.s_wide_u)
    wide_d = Spread(r.every_d, r.s_wide_d)
    greet(wide_u)

    lat = Fan("sx", r.lat, r.lat_in, r.s_lat)
    r.own_off[...] = jnp.full((8, HD), r.offset[0].astype(F32))
    for k in range(2):
        row = r.pgrad[...].astype(F32)[k : k + 1, :]
        for c in range(PW):
            r.pg[k * PW + c : k * PW + c + 1, :] = row[:, c * CH : c * CH + CH]
    offs = Fan("sy", r.own_off, r.offs, r.s_off)
    text = Fan("sx", r.text, r.text_in, r.s_text)
    tgrad = Fan("sx", r.tgrad, r.tgrad_in, r.s_tgrad)
    r.lat_in[sx] = r.lat[...]
    r.offs[sy] = r.own_off[...]
    r.text_in[sx] = r.text[...]
    r.tgrad_in[sx] = r.tgrad[...]

    r.pad_lat[...] = jnp.zeros_like(r.pad_lat)
    lat.arrived()
    for n in range(8):
        r.rows_lat[2 * n : 2 * n + 2, :] = r.lat_in[n].astype(F32)
    r.pad_lat[:, CH : CH + PW * CH] = r.rows_lat[...].astype(BF16)
    lats = Fan("sy", r.pad_lat, r.lat_all, r.s_lats)
    r.lat_all[sy] = r.pad_lat[...]

    gain = r.gain[...].astype(F32)
    loads[0].wait()
    loads[1].wait()
    down = r.dn[...]
    both = dot(down, down, NT)
    high = both.astype(BF16)
    r.wd[:, :HD] = high
    r.wd[:, HD:] = (both - high.astype(F32)).astype(BF16)
    r.wu[...] = dot(down, r.up[...]).astype(BF16)
    scaled = (down.astype(F32) * gain).astype(BF16)
    for n, weight in enumerate([r.wq, r.wk, r.wv]):
        loads[2 + n].wait()
        r.mix[:, n * HD : (n + 1) * HD] = dot(scaled, weight[:, mine]).astype(BF16)
    loads[5].wait()
    r.nt[...] = dot(r.up[...], r.wo[mine, :], (((0,), (1,)), ((), ()))).astype(BF16)

    text.arrived()
    tgrad.arrived()
    for n in range(8):
        r.rows_text[4 * n : 4 * n + 4, :] = r.text_in[n].astype(F32)
        r.rows_grad[4 * n : 4 * n + 4, :] = r.tgrad_in[n].astype(F32)
    wide = r.rows_text[...]
    inverse = lax.rsqrt(jnp.mean(wide * wide, axis=1, keepdims=True) + EPS)
    normed = (wide * inverse * gain).astype(BF16)
    token = lax.broadcasted_iota(jnp.int32, (TXT, HD), 0).astype(F32)
    shift = jnp.where(token >= r.own_off[:1, :], float(IMG), 0.0)
    cosine, sine = trig((TXT, HD), token + shift + (sy * SB).astype(F32))
    query = dot(normed, r.wq[...])
    key = dot(normed, r.wk[...])
    value = dot(normed, r.wv[...])
    outer = dot(r.rows_grad[...].astype(BF16), r.wo[...], NT)
    for h in range(4):
        at = slice(h * HD, (h + 1) * HD)
        r.kv_out[h, :, :HD] = turn(key[:, at], cosine, sine).astype(BF16)
        r.kv_out[h, :, HD:] = value[:, at].astype(BF16)
        turned = turn(query[:, at], cosine, sine)
        r.qd_out[h, :, :HD] = (turned * (SCALE * LOG2E)).astype(BF16)
        r.qd_out[h, :, HD:] = outer[:, at].astype(BF16)
    kvs = Fan("sy", r.kv_out, r.kv_in, r.s_kv, lambda ty, to: split_sy(ty)[1])
    qds = Fan("group", r.qd_out, r.qd_in, r.s_qd, lambda ty, to: to)
    r.kv_in[sy] = r.kv_out[head]
    r.qd_in[head] = r.qd_out[head]

    offs.arrived()
    masks(r, g, members)

    lats.arrived()
    down_block(r)
    project(r, members)

    def text_ready():
        kvs.arrived()
        qds.arrived()
        kv = r.kv_in[...].reshape(512, 256)
        qd = r.qd_in[...].reshape(128, 256)
        r.kt[...] = kv[:, :HD]
        r.vtx[...] = kv[:, HD:]
        r.vtt[...] = kv[:, HD:].astype(F32).T.astype(BF16)
        r.q[1024:, :] = qd[:, :HD]
        r.do[1024:, :] = qd[:, HD:]

    def add_part(m):
        r.reorder[...] = dot(r.att[m * IMG : (m + 1) * IMG, :], r.nt[...], NT) + dot(
            r.da_own[m * IMG : (m + 1) * IMG, :], r.wu[...]
        ) * (1.0 / 32.0)
        for n in range(8):
            for k in range(2):
                r.part[8 * m + n, k * PW : (k + 1) * PW, :] = r.reorder[
                    pl.ds(2 * n + k, PW, stride=PH), :
                ].astype(BF16)

    attend_images(r, 1, 7 - g, text_ready)
    add_part(2)
    add_part(3)
    attend_images(r, 0, g, lambda: None)
    add_part(0)
    add_part(1)

    e, _ = ring("team")
    parts = Fan("team", r.part, r.part_in, r.s_part, lambda ty, to: to)
    r.part_in[e] = r.part[e]
    attend_text(r, 8 - g, None)
    for m in range(4):
        r.att_txt[m] = r.att[1024 + m * TXT : 1024 + (m + 1) * TXT, :]
    atx = Fan("group", r.att_txt, r.atx, r.s_atx, lambda ty, to: to)
    r.atx[head] = r.att_txt[head]
    r.dk[...] = jnp.zeros_like(r.dk)
    r.dv[...] = jnp.zeros_like(r.dv)
    parts.arrived()
    pre = jnp.sum(r.part_in[...].astype(F32), axis=0)
    sig = sigmoid(pre)
    act = (pre * sig).astype(BF16)
    slope = sig * (1.0 + pre * (1.0 - sig))
    pgrad = r.pg[...].astype(BF16)
    r.gown[...] = (dot(pgrad, r.w_uo[...]) * slope).astype(BF16)
    ups = Fan("team", r.gown, r.gall, r.s_up)
    r.gall[e] = r.gown[...]
    pred = dot(act, r.w_uo[...], NT)
    for k in range(2):
        for c in range(PW):
            r.pred_rows[k : k + 1, c * CH : c * CH + CH] = pred[k * PW + c : k * PW + c + 1, :]
    r.pred[...] = r.pred_rows[...].astype(BF16)
    r.gup[...] = dot(pgrad, act, TN)
    for p, diagonal in ((0, g), (1, 7 - g)):
        lse = r.lse[p, :1, :]

        @pl.loop(0, diagonal + 1)
        def _(j):
            normalise(r.e_img.at[4 * p + j], r.m_img.at[4 * p + j], lse)

        normalise(r.e_txt.at[p], r.m_txt.at[p], lse)

    @pl.loop(0, 8 - g)
    def _(j):
        normalise(r.e_q.at[j], r.m_q.at[j], r.lse[2, :1, :HD])

    ups.arrived()
    for m in range(4):
        for n in range(8):
            nat = r.gall[8 * m + n].astype(F32)
            for k in range(2):
                r.order[pl.ds(m * IMG + 2 * n + k, PW, stride=PH), :] = nat[
                    k * PW : (k + 1) * PW, :
                ]
    r.gpu[...] = r.order[...].astype(BF16)
    r.do[:1024, :] = dot(r.gpu[...], r.nt[...]).astype(BF16)

    gpu = r.gpu[...]
    grad = dot(gpu, r.wu[...], NT) * (1.0 / 32.0)
    for m in range(4):
        r.ex[m] = grad[m * IMG : (m + 1) * IMG, :]
    own = r.da_own[...]
    r.small_u[:, :HD] = dot(gpu, r.att[:1024, :], TN)
    r.small_u[:, HD : 2 * HD] = dot(gpu, own, TN) * (1.0 / 32.0)
    r.small_u[:, 2 * HD :] = dot(own, gpu, TN) * (1.0 / 32.0)
    for n in range(4):
        r.low_u[n] = r.small_u[32 * n : 32 * n + 32, :].astype(BF16)
    heads_u = Fan("head", r.low_u, r.low_u_in, r.s_hu, lambda ty, to: to)
    r.low_u_in[g] = r.low_u[g]

    backward_images(r, 1, 7 - g, members)

    heads_u.arrived()
    low_u = jnp.sum(r.low_u_in[...].astype(F32), axis=0).astype(BF16)

    @pl.loop(0, 8)
    def _(c):
        at = pl.ds(pl.multiple_of(c * 512, 512), 512)
        grad = dot(low_u[:, :HD], r.wo[mine, at]) + dot(low_u[:, HD : 2 * HD], r.dn[:, at])
        for k in range(4):
            r.wide_u[4 * c + k] = grad[:, k * HD : (k + 1) * HD].astype(BF16)

    sums_u = Fan("team", r.wide_u, r.wide_u_in, r.s_su, lambda ty, to: to)
    r.wide_u_in[e] = r.wide_u[e]

    backward_images(r, 0, g, members)

    atx.arrived()
    joined = jnp.concatenate([r.atx[h] for h in range(4)], axis=1)

    @pl.loop(0, 8)
    def _(c):
        at = pl.ds(pl.multiple_of(c * 512, 512), 512)
        out = dot(joined, r.wo[:, at])
        for n in range(8):
            r.mixed[n, :, at] = out[4 * n : 4 * n + 4, :].astype(BF16)

    mixes = Fan("sx", r.mixed, r.mixed_in, r.s_mix, lambda ty, to: to)
    r.mixed_in[sx] = r.mixed[sx]

    backward_text(r, 8 - g)

    sums_u.arrived()
    wide_u.plane(jnp.sum(r.wide_u_in[...].astype(F32), axis=0).astype(BF16))
    image_grads(r, g)

    for n in range(4):
        r.low_d[n] = r.small[32 * n : 32 * n + 32, :].astype(BF16)
    heads_d = Fan("head", r.low_d, r.low_d_in, r.s_hd, lambda ty, to: to)
    r.low_d_in[g] = r.low_d[g]
    wide_u.slabs()
    conv_grad(r)
    convs = Fan("head", r.conv, r.conv_in, r.s_c1, lambda ty, to: to)
    r.conv_in[g] = r.conv[g]
    heads_d.arrived()
    low = jnp.sum(r.low_d_in[...].astype(F32), axis=0).astype(BF16)

    @pl.loop(0, 8)
    def _(c):
        at = pl.ds(pl.multiple_of(c * 512, 512), 512)
        grad = dot(low[:, :HD], r.wq[at, mine], NT)
        grad = grad + dot(low[:, HD : 2 * HD], r.wk[at, mine], NT)
        grad = grad + dot(low[:, 2 * HD : 3 * HD], r.wv[at, mine], NT)
        grad = grad * r.gain[:, at].astype(F32)
        grad = grad + dot(low_u[:, 2 * HD :], r.up[at, :], NT)
        grad = grad - dot(low[:, 3 * HD :], r.dn[:, at])
        for k in range(4):
            r.wide_d[4 * c + k] = grad[:, k * HD : (k + 1) * HD].astype(BF16)

    sums_d = Fan("team", r.wide_d, r.wide_d_in, r.s_sd, lambda ty, to: to)
    r.wide_d_in[e] = r.wide_d[e]
    convs.arrived()
    r.conv_a[...] = jnp.sum(r.conv_in[...].astype(F32), axis=0).astype(BF16)
    beside = Fan("sx", r.conv_a, r.conv_sx, r.s_c2)
    r.conv_sx[sx] = r.conv_a[...]
    wide_u.pass_on()
    mixes.arrived()
    total = r.text[...].astype(F32)
    for n in range(8):
        total = total + r.mixed_in[n].astype(F32)
    r.text_out[...] = total.astype(BF16)
    beside.arrived()
    r.conv_b[...] = jnp.sum(r.conv_sx[...].astype(F32), axis=0).astype(BF16)
    along = Fan("group", r.conv_b, r.conv_gr, r.s_c3)
    r.conv_gr[head] = r.conv_b[...]
    sums_d.arrived()
    wide_d.plane(jnp.sum(r.wide_d_in[...].astype(F32), axis=0).astype(BF16))
    along.arrived()
    r.conv_c[...] = jnp.sum(r.conv_gr[...].astype(F32), axis=0).astype(BF16)
    across = Fan("head", r.conv_c, r.conv_all, r.s_c4)
    r.conv_all[g] = r.conv_c[...]
    wide_d.slabs()
    wide_u.arrived()
    lay_up(r)
    wide_d.pass_on()
    across.arrived()
    wide_d.arrived()
    lay_down(r)
    for fan in (
        lat,
        offs,
        text,
        tgrad,
        lats,
        kvs,
        qds,
        parts,
        atx,
        ups,
        heads_u,
        sums_u,
        mixes,
        heads_d,
        convs,
        sums_d,
        beside,
        along,
        across,
    ):
        fan.sent()
    wide_u.sent()
    wide_d.sent()


def whole(inputs, cid):
    sds = jax.ShapeDtypeStruct
    dma = pltpu.SemaphoreType.DMA
    space = pltpu.VMEM
    outs = {
        "pred": ((2, PW * CH), BF16),
        "text_out": ((4, D), BF16),
        "grad_down": ((HD, D), BF16),
        "grad_up": ((D, HD), BF16),
        "conv_all": ((4, 80, HD), BF16),
    }
    scratch = {
        "pg": ((32, CH), F32),
        "pred_rows": ((2, PW * CH), F32),
        "every_u": ((2, 64, 32, HD), BF16),
        "every_d": ((2, 64, 32, HD), BF16),
        "dn": ((HD, D), BF16),
        "up": ((D, HD), BF16),
        "wq": ((D, 512), BF16),
        "wk": ((D, 512), BF16),
        "wv": ((D, 512), BF16),
        "wo": ((512, D), BF16),
        "lat_in": ((8, 2, PW * CH), BF16),
        "text_in": ((8, 4, D), BF16),
        "tgrad_in": ((8, 4, D), BF16),
        "own_off": ((8, HD), F32),
        "offs": ((16, 8, HD), F32),
        "pad_lat": ((PH, 640), BF16),
        "rows_lat": ((PH, PW * CH), F32),
        "lat_all": ((16, PH, 640), BF16),
        "rows_text": ((TXT, D), F32),
        "rows_grad": ((TXT, D), F32),
        "wd": ((HD, 256), BF16),
        "wu": ((HD, HD), BF16),
        "mix": ((HD, 384), BF16),
        "nt": ((HD, HD), BF16),
        "kv_out": ((4, TXT, 256), BF16),
        "qd_out": ((4, TXT, 256), BF16),
        "kv_in": ((16, TXT, 256), BF16),
        "qd_in": ((4, TXT, 256), BF16),
        "phase": ((2, 16, HD), F32),
        "bias_tt": ((512, 128), F32),
        "bias_ti": ((512, HD), F32),
        "vis": ((8, HD), F32),
        "wpad": ((384, HD), F32),
        "wide": ((3, 256, 640), F32),
        "patches": ((16, 256, 384), BF16),
        "da": ((16, 256, HD), BF16),
        "sp": ((16, 256, HD), BF16),
        "da_own": ((1024, HD), BF16),
        "k": ((4096, HD), BF16),
        "v": ((4096, HD), BF16),
        "vt": ((HD, 4096), BF16),
        "q": ((1152, HD), BF16),
        "kt": ((512, HD), BF16),
        "vtx": ((512, HD), BF16),
        "vtt": ((HD, 512), BF16),
        "e_img": ((12, 512, 512), BF16),
        "m_img": ((12, 8, 512), F32),
        "e_txt": ((2, 512, 512), BF16),
        "m_txt": ((2, 8, 512), F32),
        "e_q": ((9, 512, 128), BF16),
        "m_q": ((9, 8, 128), F32),
        "lse": ((3, 8, 512), F32),
        "att": ((1152, HD), BF16),
        "reorder": ((IMG, HD), F32),
        "part": ((32, 32, HD), BF16),
        "part_in": ((32, 32, HD), BF16),
        "att_txt": ((4, TXT, HD), BF16),
        "atx": ((4, TXT, HD), BF16),
        "gown": ((32, HD), BF16),
        "gall": ((32, 32, HD), BF16),
        "gup": ((CH, HD), F32),
        "order": ((1024, HD), F32),
        "gpu": ((1024, HD), BF16),
        "do": ((1152, HD), BF16),
        "dk": ((4096, HD), F32),
        "dv": ((4096, HD), F32),
        "dq": ((4, IMG, HD), F32),
        "dqs": ((512, HD), F32),
        "ex": ((4, IMG, HD), F32),
        "dpre": ((16, IMG, HD), BF16),
        "small_u": ((HD, 384), F32),
        "low_u": ((4, 32, 384), BF16),
        "low_u_in": ((4, 32, 384), BF16),
        "small": ((HD, 512), F32),
        "low_d": ((4, 32, 512), BF16),
        "low_d_in": ((4, 32, 512), BF16),
        "wide_u": ((32, 32, HD), BF16),
        "wide_u_in": ((32, 32, HD), BF16),
        "wide_d": ((32, 32, HD), BF16),
        "wide_d_in": ((32, 32, HD), BF16),
        "mixed": ((8, 4, D), BF16),
        "mixed_in": ((8, 4, D), BF16),
        "conv": ((4, 80, HD), BF16),
        "conv_in": ((4, 80, HD), BF16),
        "conv_a": ((80, HD), BF16),
        "conv_sx": ((8, 80, HD), BF16),
        "conv_b": ((80, HD), BF16),
        "conv_gr": ((4, 80, HD), BF16),
        "conv_c": ((80, HD), BF16),
    }
    sems = {"local": (6,), "s_wide_u": (2, 8), "s_wide_d": (2, 8)}
    for name in (
        ("lat", "off", "text", "tgrad", "lats", "kv", "qd", "part", "atx", "up", "hu", "su")
        + ("mix", "hd", "sd", "c1", "c2", "c3", "c4")
    ):
        sems["s_" + name] = (2,)
    names = list(inputs) + list(outs) + list(scratch) + list(sems)
    hbm = {"w_down", "w_up", "w_query", "w_key", "w_value", "w_out"}
    specs = []
    for name in inputs:
        kind = pl.ANY if name in hbm else pltpu.SMEM if name == "offset" else pltpu.VMEM
        specs.append(pl.BlockSpec(memory_space=kind))
    return pl.pallas_call(
        functools.partial(whole_kernel, names),
        out_shape=[sds(*v) for v in outs.values()],
        in_specs=specs,
        out_specs=vmem(len(outs)),
        scratch_shapes=[space(*v) for v in scratch.values()] + [dma(v) for v in sems.values()],
        compiler_params=pltpu.CompilerParams(
            collective_id=cid, has_side_effects=True, vmem_limit_bytes=60 * 2**20
        ),
    )(*inputs.values())


def rope_base():
    half = HD // 2
    freq = np.exp(-(2.0 * np.arange(half) / HD) * math.log(ROPE_BASE))
    slot = np.arange(IMG)
    position = (slot % PH) * PW + slot // PH
    angle = position[:, None] * freq[None, :]
    cosine = np.concatenate([np.cos(angle), np.cos(angle)], axis=1)
    sine = np.concatenate([-np.sin(angle), np.sin(angle)], axis=1)
    return jnp.asarray(np.stack([cosine, sine]).astype(np.float32))


def shards(
    text_tokens,
    latent,
    image_offset,
    norm_gain,
    w_query,
    w_key,
    w_value,
    w_out,
    w_down_conv,
    w_down_proj,
    w_up_proj,
    w_up_out,
    pred_grad,
    text_grad,
):
    pred, text_out, grad_down_proj, grad_up_proj, conv = whole(
        {
            "offset": image_offset,
            "text": text_tokens[0],
            "tgrad": text_grad[0],
            "lat": latent[0],
            "gain": norm_gain[None],
            "pgrad": pred_grad[0],
            "wconv": w_down_conv,
            "w_uo": w_up_out.T,
            "base": rope_base(),
            "w_down": w_down_proj,
            "w_up": w_up_proj,
            "w_query": w_query,
            "w_key": w_key,
            "w_value": w_value,
            "w_out": w_out,
        },
        1,
    )
    conv = conv.reshape(320, HD).astype(F32)
    return (
        pred[None],
        text_out[None],
        conv[:288],
        grad_down_proj.astype(F32),
        grad_up_proj.astype(F32),
        conv[288:].T,
    )


def solution(mesh):
    placed = (
        P("sy", "sx", None),
        P("sy", "sx", None),
        P("sy"),
        P(),
        P(None, "sx"),
        P(None, "sx"),
        P(None, "sx"),
        P("sx", None),
        P(),
        P(),
        P(),
        P(),
        P("sy", "sx", None),
        P("sy", "sx", None),
    )
    return jax.shard_map(
        shards,
        mesh=mesh,
        in_specs=placed,
        out_specs=(P("sy", "sx", None), P("sy", "sx", None), P(), P(), P(), P()),
        check_vma=False,
    )
```

time: 922 us -> 124 us (0.13)
  waiting for transfers between devices: 396 us -> 0 us
  blocking collectives: 183 us -> 0 us
  matrix products: 127 us -> 0 us
  Pallas kernels: 0 us -> 114 us
  local copies, waits for them, and re-layouts: 108 us -> 3.8 us
  other arithmetic: 70.2 us -> 5.19 us
  between operations: 15.7 us -> 1.32 us
  starting transfers between devices: 10.3 us -> 0 us
    all_gather x3 -> x0, waiting for transfers between devices: 196 us -> none  [the longest x1 78.3 us: shards(): every_key = lax.all_gather(keys_values, 'sy', axis=0, tiled=True)]
    dot_general x77 -> x0, matrix products: 127 us -> none  [the longest x9 20.6 us: back_keys(): jnp.einsum('hqk,khd->qhd', grad_score, key_heads, preferred_element_type=...]
    pallas_call x0 -> x1, Pallas kernels: none -> 114 us  [whole(): pl.pallas_call(functools.partial(whole_kernel, names), out_shape=[sds(*v)...]
    unnamed x2 -> x0, blocking collectives: 111 us -> none
    reduce_scatter x1 -> x0, waiting for transfers between devices: 107 us -> none  [shards(): lax.psum_scatter(grads_term.astype(wide_type).astype(jnp.bfloat16), 'sy',...]
    psum x1 -> x0, waiting for transfers between devices: 88.8 us -> none  [shards(): lax.psum((grad_down_conv, grad_down_proj, grad_up_proj, grad_up_out), ('s...]
    psum x1 -> x0, blocking collectives: 71.2 us -> none  [shards(): lax.psum((grad_down_conv, grad_down_proj, grad_up_proj, grad_up_out), ('s...]
    unnamed x85 -> x8, local copies, waits for them, and re-layouts: 41.2 us -> 1.21 us
  transfers between devices with their start and end apart: 9 -> 0, of which waited for: 8 -> 0; matrix products, arithmetic and copies ran while one was open for 2% -> 0% of each run, Pallas kernels for 0% -> 0%
where the time goes in v3:
time: 124 us
  Pallas kernels  114 us (92%)
  other arithmetic  5.19 us (4%)
  local copies, waits for them, and re-layouts  3.8 us (3%)
  between operations  1.32 us (1%)
    pallas_call x1, Pallas kernels, whole(): pl.pallas_call(functools.partial(whole_kernel, names), out_shape=[sds(*v)...  114 us
    convert_element_type x1, other arithmetic, shards(): grad_down_proj.astype(F32)  2.76 us

profile of v3, /device:TPU:1, one launch (start us, length us, event | category | flops | bytes accessed | tf_op | source)
XLA Modules:
  0.0 124.2 jit_solution(8880211306346287313)
XLA Ops:
  1.3 1.3 %broadcast_in_dim.9.refs_4_ = bf16[1,4096]{1,0:T(2,128)(2,1)} reshape(bf16[4096]{0:T(1024)(128)(2,1)} %param.18) | data formatting | bytes 16384 | tf_op jit(solution)/shard_map/broadcast_in_dim | solution.py:977
  2.6 113.9 %shard_map.190 = (bf16[2,512]{1,0:T(2,128)(2,1)}, bf16[4,4096]{1,0:T(4,128)(2,1)}, bf16[128,4096]{1,0:T(8,128)(2,1)}, bf16[4096,128]{1,0:T(8,128)(2,1)}, bf16[4,80,128]{2,1,0:T(8,128)(2,1)}) custom-call(s32[1]{0:T(128)S(6)} %copy.23.refs_0_, bf16[4,4096]{1,0:T(4,128)(2,1)} %bitcast.12, bf16[4,4096]{1,0:T(4,128)(2,1)} %bitcast.13, bf16[2,512]{1,0:T(2,128)(2,1)} %bitcast.16, ...), custom_call_target="tpu_custom_call" | custom-call | tf_op jit(solution)/shard_map/pallas_call | solution.py:932
  116.5 0.0 copy-start
  116.5 0.0 copy-start.2
  116.5 0.0 copy-start.1
  116.5 1.0 bitcast_convert_fusion
  117.5 0.6 slice_bitcast_fusion
  118.1 0.7 slice.8
  118.8 2.8 %convert_element_type.14 = f32[128,4096]{1,0:T(8,128)} convert(bf16[128,4096]{1,0:T(8,128)(2,1)} %get-tuple-element.14) | non-fusion elementwise | flops 524288 | bytes 3145728 | tf_op jit(solution)/shard_map/convert_element_type | solution.py:996
  121.5 0.0 copy-done
  121.5 1.5 %convert_element_type.15 = f32[4096,128]{1,0:T(8,128)} convert(bf16[4096,128]{1,0:T(8,128)(2,1)S(1)} %copy-done) | non-fusion elementwise | flops 524288 | bytes 3145728 | tf_op jit(solution)/shard_map/convert_element_type | solution.py:997
  123.0 0.0 copy-done.2
  123.0 0.6 copy.24
  123.6 0.0 copy-done.1
  123.6 0.6 copy.25
Async XLA Ops:
  116.5 5.1 %copy-start = (bf16[4096,128]{1,0:T(8,128)(2,1)S(1)}, bf16[4096,128]{1,0:T(8,128)(2,1)}, u32[]{:S(2)}) copy-start(bf16[4096,128]{1,0:T(8,128)(2,1)} %get-tuple-element.15) | copy-start | bytes 3145732
  116.5 6.5 %copy-start.2 = (bf16[2,512]{1,0:T(2,128)(2,1)S(1)}, bf16[2,512]{1,0:T(2,128)(2,1)}, u32[]{:S(2)}) copy-start(bf16[2,512]{1,0:T(2,128)(2,1)} %get-tuple-element.11) | copy-start | bytes 6148
  116.5 7.1 %copy-start.1 = (bf16[4,4096]{1,0:T(4,128)(2,1)S(1)}, bf16[4,4096]{1,0:T(4,128)(2,1)}, u32[]{:S(2)}) copy-start(bf16[4,4096]{1,0:T(4,128)(2,1)} %get-tuple-element.12) | copy-start | bytes 98308

commit v4 on v3

--- a/solution.py
+++ b/solution.py
@@ -137,11 +137,14 @@
     return pc * bc - ps * bs, ps * bc + pc * bs
 
 
+def row_sum(v):
+    return dot(v.astype(BF16), jnp.ones((HD, HD), BF16))
+
+
 def row_scale(da, wd):
     both = dot(da, wd)
     dawd = both[:, :HD] + both[:, HD:]
-    mean = jnp.sum(dawd * da.astype(F32), axis=1, keepdims=True) * (1.0 / D)
-    return dawd, lax.rsqrt(mean + EPS)
+    return dawd, lax.rsqrt(row_sum(dawd * da.astype(F32)) * (1.0 / D) + EPS)
 
 
 def lanes(column):
@@ -240,7 +243,7 @@
         to = wide.chip(wide.p1, wide.p2, wide.p3 + o)
         pl.semaphore_signal(barrier, inc=1, device_id=to, device_id_type=MESH)
 
-    pl.semaphore_wait(barrier, 31 + 15 + 15 + 3)
+    return lambda: pl.semaphore_wait(barrier, 31 + 15 + 15 + 3)
 
 
 def masks(r, g, members):
@@ -302,25 +305,31 @@
     mix_q = r.mix[:, :HD]
     wd = r.wd[...]
 
-    @pl.loop(0, 16, unroll=4)
-    def _(j):
-        da = r.da[j]
+    @pl.loop(0, 4)
+    def _(n):
+        da = r.da[pl.ds(4 * n, 4)].reshape(4 * IMG, HD)
         _, inv = row_scale(da, wd)
-        kv = dot(da, mix_kv) * inv
-        cosine, sine = tables(j, r.phase, r.base)
-        rows = pl.ds(pl.multiple_of(j * IMG, IMG), IMG)
-        r.k[rows, :] = turn(kv[:, :HD], cosine, sine).astype(BF16)
-        r.v[rows, :] = kv[:, HD:].astype(BF16)
-        r.vt[:, rows] = kv[:, HD:].T.astype(BF16)
+        scaled = (da.astype(F32) * inv).astype(BF16)
+        kv = dot(scaled, mix_kv)
+        whole = pl.ds(pl.multiple_of(n * 1024, 1024), 1024)
+        r.vt[:, whole] = dot(mix_kv[:, HD:], scaled, (((0,), (1,)), ((), ()))).astype(BF16)
+        for m in range(4):
+            j = 4 * n + m
+            cosine, sine = tables(j, r.phase, r.base)
+            rows = pl.ds(pl.multiple_of(j * IMG, IMG), IMG)
+            part = kv[m * IMG : (m + 1) * IMG, :]
+            r.k[rows, :] = turn(part[:, :HD], cosine, sine).astype(BF16)
+            r.v[rows, :] = part[:, HD:].astype(BF16)
 
     for m in range(4):
-        da = r.da[members[m]]
-        r.da_own[m * IMG : (m + 1) * IMG, :] = da
-        _, inv = row_scale(da, wd)
+        r.da_own[m * IMG : (m + 1) * IMG, :] = r.da[members[m]]
+    da = r.da_own[...]
+    _, inv = row_scale(da, wd)
+    queries = dot((da.astype(F32) * inv).astype(BF16), mix_q) * (SCALE * LOG2E)
+    for m in range(4):
+        rows = slice(m * IMG, (m + 1) * IMG)
         cosine, sine = tables(members[m], r.phase, r.base)
-        r.q[m * IMG : (m + 1) * IMG, :] = (
-            turn(dot(da, mix_q) * inv, cosine, sine) * (SCALE * LOG2E)
-        ).astype(BF16)
+        r.q[rows, :] = turn(queries[rows, :], cosine, sine).astype(BF16)
 
 
 def tile_rows(j):
@@ -456,22 +465,31 @@
     mix = r.mix[...]
     r.small[...] = jnp.zeros_like(r.small)
 
-    @pl.loop(0, 16, unroll=2)
-    def _(j):
-        group, m = split_sy(j)
-        ours = (group == g).astype(F32)
-        da = r.da[j]
+    @pl.loop(0, 4)
+    def _(n):
+        da = r.da[pl.ds(4 * n, 4)].reshape(4 * IMG, HD)
         da_wide = da.astype(F32)
         dawd, inv = row_scale(da, wd)
-        cosine, sine = tables(j, r.phase, r.base)
-        at = pl.ds(pl.multiple_of(j * IMG, IMG), IMG)
-        gq = turn(r.dq[m] * (ours * SCALE), cosine, -sine)
-        gk = turn(r.dk[at, :] * (1.0 / LOG2E), cosine, -sine)
-        grads = jnp.concatenate([gq, gk, r.dv[at, :]], axis=1).astype(BF16)
+        extra = []
+        for k in range(4):
+            j = 4 * n + k
+            group, m = split_sy(j)
+            ours = (group == g).astype(F32)
+            cosine, sine = tables(j, r.phase, r.base)
+            at = pl.ds(pl.multiple_of(j * IMG, IMG), IMG)
+            rows = slice(k * IMG, (k + 1) * IMG)
+            gq = turn(r.dq[m] * (ours * SCALE), cosine, -sine)
+            gk = turn(r.dk[at, :] * (1.0 / LOG2E), cosine, -sine)
+            r.grads[rows, :HD] = gq.astype(BF16)
+            r.grads[rows, HD : 2 * HD] = gk.astype(BF16)
+            r.grads[rows, 2 * HD :] = r.dv[at, :].astype(BF16)
+            extra.append(r.ex[m] * ours)
+        grads = r.grads[...]
         back = dot(grads, mix, NT)
-        cube = (inv * inv * inv) * (jnp.sum(back * da_wide, axis=1, keepdims=True) * (1.0 / D))
-        grad = (inv * back - cube * dawd + r.ex[m] * ours) * r.sp[j].astype(F32)
-        r.dpre[j] = grad.astype(BF16)
+        cube = (inv * inv * inv) * (row_sum(back * da_wide) * (1.0 / D))
+        slope = r.sp[pl.ds(4 * n, 4)].reshape(4 * IMG, HD).astype(F32)
+        grad = (inv * back - cube * dawd + jnp.concatenate(extra, axis=0)) * slope
+        r.dpre[pl.ds(4 * n, 4)] = grad.astype(BF16).reshape(4, IMG, HD)
         r.small[:, :384] += dot((da_wide * inv).astype(BF16), grads, TN)
         r.small[:, 384:] += dot((da_wide * cube).astype(BF16), da, TN)
 
@@ -488,30 +506,27 @@
 
 
 def block_of(group, e):
-    i = div(e, 8)
-    sx = mod(e, 8)
-    sy = sy_of(group, i)
-    x = div(sx, 2)
-    y = div(sy, 4)
-    z = 2 * mod(div(sy, 2), 2) + mod(sx, 2)
-    core = mod(i, 2)
-    return core, jnp.where(core == 0, (z * 4 + y) * 4 + x, (y * 4 + x) * 4 + z)
+    sx = e % 8
+    sy = sy_of(group, e // 8)
+    x = sx // 2
+    y = sy // 4
+    z = 2 * ((sy // 2) % 2) + sx % 2
+    core = sy % 2
+    return core, (z * 4 + y) * 4 + x if core == 0 else (y * 4 + x) * 4 + z
 
 
 def lay_up(r):
-    @pl.loop(0, 32, unroll=2)
-    def _(e):
+    for e in range(32):
         cols = [r.every_u[block_of(group, e)].astype(F32) for group in range(4)]
-        at = pl.ds(pl.multiple_of(e * HD, HD), HD)
-        r.grad_up[at, :] = jnp.concatenate(cols, axis=0).T.astype(BF16)
+        r.grad_up[e * HD : (e + 1) * HD, :] = jnp.concatenate(cols, axis=0).T.astype(BF16)
 
 
 def lay_down(r):
-    @pl.loop(0, 32, unroll=2)
-    def _(e):
-        at = pl.ds(pl.multiple_of(e * HD, HD), HD)
+    for e in range(32):
         for group in range(4):
-            r.grad_down[32 * group : 32 * group + 32, at] = r.every_d[block_of(group, e)]
+            r.grad_down[32 * group : 32 * group + 32, e * HD : (e + 1) * HD] = r.every_d[
+                block_of(group, e)
+            ]
 
 
 def whole_kernel(names, *refs):
@@ -537,31 +552,15 @@
         loads.append(copy)
     wide_u = Spread(r.every_u, r.s_wide_u)
     wide_d = Spread(r.every_d, r.s_wide_d)
-    greet(wide_u)
-
-    lat = Fan("sx", r.lat, r.lat_in, r.s_lat)
+    all_here = greet(wide_u)
     r.own_off[...] = jnp.full((8, HD), r.offset[0].astype(F32))
+    r.pad_lat[...] = jnp.zeros_like(r.pad_lat)
     for k in range(2):
         row = r.pgrad[...].astype(F32)[k : k + 1, :]
         for c in range(PW):
             r.pg[k * PW + c : k * PW + c + 1, :] = row[:, c * CH : c * CH + CH]
-    offs = Fan("sy", r.own_off, r.offs, r.s_off)
-    text = Fan("sx", r.text, r.text_in, r.s_text)
-    tgrad = Fan("sx", r.tgrad, r.tgrad_in, r.s_tgrad)
-    r.lat_in[sx] = r.lat[...]
-    r.offs[sy] = r.own_off[...]
-    r.text_in[sx] = r.text[...]
-    r.tgrad_in[sx] = r.tgrad[...]
-
-    r.pad_lat[...] = jnp.zeros_like(r.pad_lat)
-    lat.arrived()
-    for n in range(8):
-        r.rows_lat[2 * n : 2 * n + 2, :] = r.lat_in[n].astype(F32)
-    r.pad_lat[:, CH : CH + PW * CH] = r.rows_lat[...].astype(BF16)
-    lats = Fan("sy", r.pad_lat, r.lat_all, r.s_lats)
-    r.lat_all[sy] = r.pad_lat[...]
-
-    gain = r.gain[...].astype(F32)
+    gain = r.gain[...].astype(F32).reshape(1, D)
+    r.gain_row[...] = gain
     loads[0].wait()
     loads[1].wait()
     down = r.dn[...]
@@ -571,11 +570,32 @@
     r.wd[:, HD:] = (both - high.astype(F32)).astype(BF16)
     r.wu[...] = dot(down, r.up[...]).astype(BF16)
     scaled = (down.astype(F32) * gain).astype(BF16)
+    all_here()
+
+    lat = Fan("sx", r.lat, r.lat_in, r.s_lat)
+    r.lat_in[sx] = r.lat[...]
+
+    lat.arrived()
+    for n in range(8):
+        r.rows_lat[2 * n : 2 * n + 2, :] = r.lat_in[n].astype(F32)
+    r.pad_lat[:, CH : CH + PW * CH] = r.rows_lat[...].astype(BF16)
+    lats = Fan("sy", r.pad_lat, r.lat_all, r.s_lats)
+    r.lat_all[sy] = r.pad_lat[...]
+    offs = Fan("sy", r.own_off, r.offs, r.s_off)
+    r.offs[sy] = r.own_off[...]
+    text = Fan("sx", r.text, r.text_in, r.s_text)
+    tgrad = Fan("sx", r.tgrad, r.tgrad_in, r.s_tgrad)
+    r.text_in[sx] = r.text[...]
+    r.tgrad_in[sx] = r.tgrad[...]
+
     for n, weight in enumerate([r.wq, r.wk, r.wv]):
         loads[2 + n].wait()
         r.mix[:, n * HD : (n + 1) * HD] = dot(scaled, weight[:, mine]).astype(BF16)
     loads[5].wait()
     r.nt[...] = dot(r.up[...], r.wo[mine, :], (((0,), (1,)), ((), ()))).astype(BF16)
+
+    lats.arrived()
+    down_block(r)
 
     text.arrived()
     tgrad.arrived()
@@ -607,8 +627,6 @@
     offs.arrived()
     masks(r, g, members)
 
-    lats.arrived()
-    down_block(r)
     project(r, members)
 
     def text_ready():
@@ -677,6 +695,21 @@
     def _(j):
         normalise(r.e_q.at[j], r.m_q.at[j], r.lse[2, :1, :HD])
 
+    backward_text(r, 8 - g)
+
+    atx.arrived()
+    joined = jnp.concatenate([r.atx[h] for h in range(4)], axis=1)
+
+    @pl.loop(0, 8)
+    def _(c):
+        at = pl.ds(pl.multiple_of(c * 512, 512), 512)
+        out = dot(joined, r.wo[:, at])
+        for n in range(8):
+            r.mixed[n, :, at] = out[4 * n : 4 * n + 4, :].astype(BF16)
+
+    mixes = Fan("sx", r.mixed, r.mixed_in, r.s_mix, lambda ty, to: to)
+    r.mixed_in[sx] = r.mixed[sx]
+
     ups.arrived()
     for m in range(4):
         for n in range(8):
@@ -701,7 +734,7 @@
     heads_u = Fan("head", r.low_u, r.low_u_in, r.s_hu, lambda ty, to: to)
     r.low_u_in[g] = r.low_u[g]
 
-    backward_images(r, 1, 7 - g, members)
+    backward_images(r, 0, g, members)
 
     heads_u.arrived()
     low_u = jnp.sum(r.low_u_in[...].astype(F32), axis=0).astype(BF16)
@@ -716,22 +749,7 @@
     sums_u = Fan("team", r.wide_u, r.wide_u_in, r.s_su, lambda ty, to: to)
     r.wide_u_in[e] = r.wide_u[e]
 
-    backward_images(r, 0, g, members)
-
-    atx.arrived()
-    joined = jnp.concatenate([r.atx[h] for h in range(4)], axis=1)
-
-    @pl.loop(0, 8)
-    def _(c):
-        at = pl.ds(pl.multiple_of(c * 512, 512), 512)
-        out = dot(joined, r.wo[:, at])
-        for n in range(8):
-            r.mixed[n, :, at] = out[4 * n : 4 * n + 4, :].astype(BF16)
-
-    mixes = Fan("sx", r.mixed, r.mixed_in, r.s_mix, lambda ty, to: to)
-    r.mixed_in[sx] = r.mixed[sx]
-
-    backward_text(r, 8 - g)
+    backward_images(r, 1, 7 - g, members)
 
     sums_u.arrived()
     wide_u.plane(jnp.sum(r.wide_u_in[...].astype(F32), axis=0).astype(BF16))
@@ -741,7 +759,6 @@
         r.low_d[n] = r.small[32 * n : 32 * n + 32, :].astype(BF16)
     heads_d = Fan("head", r.low_d, r.low_d_in, r.s_hd, lambda ty, to: to)
     r.low_d_in[g] = r.low_d[g]
-    wide_u.slabs()
     conv_grad(r)
     convs = Fan("head", r.conv, r.conv_in, r.s_c1, lambda ty, to: to)
     r.conv_in[g] = r.conv[g]
@@ -754,7 +771,7 @@
         grad = dot(low[:, :HD], r.wq[at, mine], NT)
         grad = grad + dot(low[:, HD : 2 * HD], r.wk[at, mine], NT)
         grad = grad + dot(low[:, 2 * HD : 3 * HD], r.wv[at, mine], NT)
-        grad = grad * r.gain[:, at].astype(F32)
+        grad = grad * r.gain_row[:, at]
         grad = grad + dot(low_u[:, 2 * HD :], r.up[at, :], NT)
         grad = grad - dot(low[:, 3 * HD :], r.dn[:, at])
         for k in range(4):
@@ -762,31 +779,37 @@
 
     sums_d = Fan("team", r.wide_d, r.wide_d_in, r.s_sd, lambda ty, to: to)
     r.wide_d_in[e] = r.wide_d[e]
+    wide_u.slabs()
     convs.arrived()
     r.conv_a[...] = jnp.sum(r.conv_in[...].astype(F32), axis=0).astype(BF16)
     beside = Fan("sx", r.conv_a, r.conv_sx, r.s_c2)
     r.conv_sx[sx] = r.conv_a[...]
-    wide_u.pass_on()
     mixes.arrived()
     total = r.text[...].astype(F32)
     for n in range(8):
         total = total + r.mixed_in[n].astype(F32)
     r.text_out[...] = total.astype(BF16)
+    sums_d.arrived()
+    wide_d.plane(jnp.sum(r.wide_d_in[...].astype(F32), axis=0).astype(BF16))
     beside.arrived()
     r.conv_b[...] = jnp.sum(r.conv_sx[...].astype(F32), axis=0).astype(BF16)
     along = Fan("group", r.conv_b, r.conv_gr, r.s_c3)
     r.conv_gr[head] = r.conv_b[...]
-    sums_d.arrived()
-    wide_d.plane(jnp.sum(r.wide_d_in[...].astype(F32), axis=0).astype(BF16))
+    wide_u.pass_on()
+    wide_d.slabs()
     along.arrived()
     r.conv_c[...] = jnp.sum(r.conv_gr[...].astype(F32), axis=0).astype(BF16)
     across = Fan("head", r.conv_c, r.conv_all, r.s_c4)
     r.conv_all[g] = r.conv_c[...]
-    wide_d.slabs()
     wide_u.arrived()
     lay_up(r)
     wide_d.pass_on()
     across.arrived()
+    for n in range(3):
+        r.grad_conv[80 * n : 80 * n + 80, :] = r.conv_all[n].astype(F32)
+    rest = r.conv_all[3].astype(F32)
+    r.grad_conv[240:, :] = rest[:48, :]
+    r.grad_out[...] = rest[48:, :]
     wide_d.arrived()
     lay_down(r)
     for fan in (
@@ -824,9 +847,12 @@
         "text_out": ((4, D), BF16),
         "grad_down": ((HD, D), BF16),
         "grad_up": ((D, HD), BF16),
-        "conv_all": ((4, 80, HD), BF16),
+        "grad_conv": ((288, HD), F32),
+        "grad_out": ((CH, HD), F32),
     }
     scratch = {
+        "conv_all": ((4, 80, HD), BF16),
+        "gain_row": ((1, D), F32),
         "pg": ((32, CH), F32),
         "pred_rows": ((2, PW * CH), F32),
         "every_u": ((2, 64, 32, HD), BF16),
@@ -897,6 +923,7 @@
         "dqs": ((512, HD), F32),
         "ex": ((4, IMG, HD), F32),
         "dpre": ((16, IMG, HD), BF16),
+        "grads": ((1024, 384), BF16),
         "small_u": ((HD, 384), F32),
         "low_u": ((4, 32, 384), BF16),
         "low_u_in": ((4, 32, 384), BF16),
@@ -936,9 +963,36 @@
         out_specs=vmem(len(outs)),
         scratch_shapes=[space(*v) for v in scratch.values()] + [dma(v) for v in sems.values()],
         compiler_params=pltpu.CompilerParams(
-            collective_id=cid, has_side_effects=True, vmem_limit_bytes=60 * 2**20
+            collective_id=cid, has_side_effects=True, vmem_limit_bytes=61 * 2**20
         ),
     )(*inputs.values())
+
+
+def results_kernel(pred, text, down, up, conv, out, *results):
+    for src, dst in zip((pred, text), results[:2]):
+        dst[0] = src[...]
+    for src, dst in zip((down, up, conv), results[2:5]):
+        dst[...] = src[...].astype(F32)
+    results[5][...] = out[...]
+
+
+def results(*arrays):
+    sds = jax.ShapeDtypeStruct
+    shapes = [
+        sds((1, 2, PW * CH), BF16),
+        sds((1, 4, D), BF16),
+        sds((HD, D), F32),
+        sds((D, HD), F32),
+        sds((288, HD), F32),
+        sds((CH, HD), F32),
+    ]
+    return pl.pallas_call(
+        results_kernel,
+        out_shape=shapes,
+        in_specs=vmem(6),
+        out_specs=vmem(6),
+        compiler_params=pltpu.CompilerParams(vmem_limit_bytes=32 * 2**20),
+    )(*arrays)
 
 
 def rope_base():
@@ -968,13 +1022,13 @@
     pred_grad,
     text_grad,
 ):
-    pred, text_out, grad_down_proj, grad_up_proj, conv = whole(
+    pred, text_out, grad_down_proj, grad_up_proj, grad_conv, grad_out = whole(
         {
             "offset": image_offset,
             "text": text_tokens[0],
             "tgrad": text_grad[0],
             "lat": latent[0],
-            "gain": norm_gain[None],
+            "gain": norm_gain,
             "pgrad": pred_grad[0],
             "wconv": w_down_conv,
             "w_uo": w_up_out.T,
@@ -988,15 +1042,10 @@
         },
         1,
     )
-    conv = conv.reshape(320, HD).astype(F32)
-    return (
-        pred[None],
-        text_out[None],
-        conv[:288],
-        grad_down_proj.astype(F32),
-        grad_up_proj.astype(F32),
-        conv[288:].T,
+    pred, text_out, grad_down_proj, grad_up_proj, grad_conv, grad_out = results(
+        pred, text_out, grad_down_proj, grad_up_proj, grad_conv, grad_out
     )
+    return pred, text_out, grad_conv, grad_down_proj, grad_up_proj, grad_out.T
 
 
 def solution(mesh):

time: 124 us -> 118 us (0.952)
  other arithmetic: 5.19 us -> 0 us
  Pallas kernels: 114 us -> 111 us
  local copies, waits for them, and re-layouts: 3.8 us -> 5.5 us
    pallas_call x1, Pallas kernels: 114 us -> 109 us  [whole(): pl.pallas_call(functools.partial(whole_kernel, names), out_shape=[sds(*v)...]
    convert_element_type x3 -> x0, other arithmetic: 5.19 us -> none  [the longest x1 2.76 us: shards(): grad_down_proj.astype(F32)]
    unnamed x8 -> x12, local copies, waits for them, and re-layouts: 1.21 us -> 5.5 us
    pallas_call x0 -> x1, Pallas kernels: none -> 2.26 us  [results(): pl.pallas_call(results_kernel, out_shape=shapes, in_specs=vmem(6), out_sp...]
    broadcast_in_dim x1 -> x0, local copies, waits for them, and re-layouts: 1.31 us -> none  [shards(): norm_gain[None]]
where the time goes in v4:
time: 118 us
  Pallas kernels  111 us (94%)
  local copies, waits for them, and re-layouts  5.5 us (5%)
  between operations  1.3 us (1%)
    pallas_call x1, Pallas kernels, whole(): pl.pallas_call(functools.partial(whole_kernel, names), out_shape=[sds(*v)...  109 us
    unnamed x12, local copies, waits for them, and re-layouts  5.5 us

profile of v4, /device:TPU:1, one launch (start us, length us, event | category | flops | bytes accessed | tf_op | source)
XLA Modules:
  0.0 117.6 jit_solution(6609834699477291319)
XLA Ops:
  1.3 108.5 %shard_map.190 = (bf16[2,512]{1,0:T(2,128)(2,1)}, bf16[4,4096]{1,0:T(4,128)(2,1)}, bf16[128,4096]{1,0:T(8,128)(2,1)}, bf16[4096,128]{1,0:T(8,128)(2,1)}, f32[288,128]{1,0:T(8,128)}, /*index=5*/f32[32,128]{1,0:T(8,128)}) custom-call(s32[1]{0:T(128)S(6)} %copy.21.refs_0_, bf16[4,4096]{1,0:T(4,128)(2,1)} %bitcast.6, bf16[4,4096]{1,0:T(4,128)(2,1)} %bitcast.7, ...), custom_call_target="tpu_custom_call" | custom-call | tf_op jit(solution)/shard_map/pallas_call | solution.py:959
  109.8 0.0 copy-start
  109.8 1.2 %copy-done = bf16[128,4096]{1,0:T(8,128)(2,1)S(1)} copy-done((bf16[128,4096]{1,0:T(8,128)(2,1)S(1)}, bf16[128,4096]{1,0:T(8,128)(2,1)}, u32[]{:S(2)}) %copy-start) | copy-done | bytes 1048600
  111.0 0.0 copy-start.1
  111.0 1.2 %copy-done.1 = bf16[4096,128]{1,0:T(8,128)(2,1)S(1)} copy-done((bf16[4096,128]{1,0:T(8,128)(2,1)S(1)}, bf16[4096,128]{1,0:T(8,128)(2,1)}, u32[]{:S(2)}) %copy-start.1) | copy-done | bytes 1048600
  112.2 0.0 copy-start.2
  112.2 0.9 copy-done.2
  113.2 0.0 copy-start.3
  113.2 0.8 copy-done.3
  113.9 0.0 copy-start.4
  113.9 0.7 copy-done.4
  114.6 0.0 copy-start.5
  114.6 0.7 copy-done.5
  115.3 2.3 %shard_map.191 = (bf16[1,2,512]{2,1,0:T(2,128)(2,1)}, bf16[1,4,4096]{2,1,0:T(4,128)(2,1)}, f32[128,4096]{1,0:T(8,128)}, f32[4096,128]{1,0:T(8,128)}, f32[288,128]{1,0:T(8,128)}, /*index=5*/f32[32,128]{1,0:T(8,128)}) custom-call(bf16[2,512]{1,0:T(2,128)(2,1)S(1)} %copy-done.5, bf16[4,4096]{1,0:T(4,128)(2,1)S(1)} %copy-done.3, bf16[128,4096]{1,0:T(8,128)(2,1)S(1)} %copy-done, ...), custom_call_target="tpu_custom_call" | custom-call | tf_op jit(solution)/shard_map/pallas_call | solution.py:989
Async XLA Ops:
  109.8 1.2 %copy-start = (bf16[128,4096]{1,0:T(8,128)(2,1)S(1)}, bf16[128,4096]{1,0:T(8,128)(2,1)}, u32[]{:S(2)}) copy-start(bf16[128,4096]{1,0:T(8,128)(2,1)} %get-tuple-element.20.down) | copy-start | bytes 3145732
  111.0 1.2 %copy-start.1 = (bf16[4096,128]{1,0:T(8,128)(2,1)S(1)}, bf16[4096,128]{1,0:T(8,128)(2,1)}, u32[]{:S(2)}) copy-start(bf16[4096,128]{1,0:T(8,128)(2,1)} %get-tuple-element.21.up) | copy-start | bytes 3145732
  112.2 0.9 copy-start.2
  113.2 0.8 copy-start.3
  113.9 0.7 copy-start.4
  114.6 0.7 copy-start.5

commit v5 on v4

--- a/solution.py
+++ b/solution.py
@@ -111,6 +111,31 @@
 
     def sent(self):
         pltpu.make_async_copy(self.land, self.land, self.sems.at[0]).wait()
+
+
+class Team:
+    def __init__(self, source, land, sems):
+        sy = lax.axis_index("sy")
+        self.g, i = split_sy(sy)
+        self.own = i * 8 + lax.axis_index("sx")
+        self.source = source
+        self.slots = land
+        self.land = land.at[pl.ds(0, 31)]
+        self.sems = sems
+
+    def push(self, f):
+        @pl.when(f != self.own)
+        def _():
+            to = (mod(f, 8), sy_of(self.g, div(f, 8)))
+            remote(
+                self.source.at[f], self.slots.at[self.own], self.sems.at[0], self.sems.at[1], to
+            )
+
+    def keep(self):
+        self.slots[self.own] = self.source[self.own]
+
+    arrived = Fan.arrived
+    sent = Fan.sent
 
 
 def sigmoid(v):
@@ -281,7 +306,8 @@
     r.wpad[...] = jnp.zeros_like(r.wpad)
     for tap in range(3):
         r.wpad[tap * 128 : tap * 128 + 96, :] = r.wconv[tap * 96 : tap * 96 + 96, :].astype(F32)
-    mid = r.lat_all[...].reshape(256, 640).astype(F32)
+    mid = r.lat_all[...].reshape(256, PW * CH).astype(F32)
+    mid = pltpu.roll(jnp.concatenate([mid, jnp.zeros((256, HD), F32)], axis=1), CH, 1)
     row = lax.broadcasted_iota(jnp.int32, mid.shape, 0) % PH
     r.wide[0] = jnp.where(row == 0, 0.0, pltpu.roll(mid, 1, 0))
     r.wide[1] = mid
@@ -554,7 +580,6 @@
     wide_d = Spread(r.every_d, r.s_wide_d)
     all_here = greet(wide_u)
     r.own_off[...] = jnp.full((8, HD), r.offset[0].astype(F32))
-    r.pad_lat[...] = jnp.zeros_like(r.pad_lat)
     for k in range(2):
         row = r.pgrad[...].astype(F32)[k : k + 1, :]
         for c in range(PW):
@@ -573,20 +598,18 @@
     all_here()
 
     lat = Fan("sx", r.lat, r.lat_in, r.s_lat)
+    text = Fan("sx", r.text, r.text_in, r.s_text)
     r.lat_in[sx] = r.lat[...]
+    r.text_in[sx] = r.text[...]
 
     lat.arrived()
     for n in range(8):
         r.rows_lat[2 * n : 2 * n + 2, :] = r.lat_in[n].astype(F32)
-    r.pad_lat[:, CH : CH + PW * CH] = r.rows_lat[...].astype(BF16)
-    lats = Fan("sy", r.pad_lat, r.lat_all, r.s_lats)
-    r.lat_all[sy] = r.pad_lat[...]
+    r.row_lat[...] = r.rows_lat[...].astype(BF16)
+    lats = Fan("sy", r.row_lat, r.lat_all, r.s_lats)
+    r.lat_all[sy] = r.row_lat[...]
     offs = Fan("sy", r.own_off, r.offs, r.s_off)
     r.offs[sy] = r.own_off[...]
-    text = Fan("sx", r.text, r.text_in, r.s_text)
-    tgrad = Fan("sx", r.tgrad, r.tgrad_in, r.s_tgrad)
-    r.text_in[sx] = r.text[...]
-    r.tgrad_in[sx] = r.tgrad[...]
 
     for n, weight in enumerate([r.wq, r.wk, r.wv]):
         loads[2 + n].wait()
@@ -594,14 +617,9 @@
     loads[5].wait()
     r.nt[...] = dot(r.up[...], r.wo[mine, :], (((0,), (1,)), ((), ()))).astype(BF16)
 
-    lats.arrived()
-    down_block(r)
-
     text.arrived()
-    tgrad.arrived()
     for n in range(8):
         r.rows_text[4 * n : 4 * n + 4, :] = r.text_in[n].astype(F32)
-        r.rows_grad[4 * n : 4 * n + 4, :] = r.tgrad_in[n].astype(F32)
     wide = r.rows_text[...]
     inverse = lax.rsqrt(jnp.mean(wide * wide, axis=1, keepdims=True) + EPS)
     normed = (wide * inverse * gain).astype(BF16)
@@ -611,14 +629,12 @@
     query = dot(normed, r.wq[...])
     key = dot(normed, r.wk[...])
     value = dot(normed, r.wv[...])
-    outer = dot(r.rows_grad[...].astype(BF16), r.wo[...], NT)
     for h in range(4):
         at = slice(h * HD, (h + 1) * HD)
         r.kv_out[h, :, :HD] = turn(key[:, at], cosine, sine).astype(BF16)
         r.kv_out[h, :, HD:] = value[:, at].astype(BF16)
         turned = turn(query[:, at], cosine, sine)
-        r.qd_out[h, :, :HD] = (turned * (SCALE * LOG2E)).astype(BF16)
-        r.qd_out[h, :, HD:] = outer[:, at].astype(BF16)
+        r.qd_out[h] = (turned * (SCALE * LOG2E)).astype(BF16)
     kvs = Fan("sy", r.kv_out, r.kv_in, r.s_kv, lambda ty, to: split_sy(ty)[1])
     qds = Fan("group", r.qd_out, r.qd_in, r.s_qd, lambda ty, to: to)
     r.kv_in[sy] = r.kv_out[head]
@@ -627,18 +643,21 @@
     offs.arrived()
     masks(r, g, members)
 
+    lats.arrived()
+    tgrad = Fan("sx", r.tgrad, r.tgrad_in, r.s_tgrad)
+    r.tgrad_in[sx] = r.tgrad[...]
+    down_block(r)
+
     project(r, members)
 
     def text_ready():
         kvs.arrived()
         qds.arrived()
         kv = r.kv_in[...].reshape(512, 256)
-        qd = r.qd_in[...].reshape(128, 256)
         r.kt[...] = kv[:, :HD]
         r.vtx[...] = kv[:, HD:]
         r.vtt[...] = kv[:, HD:].astype(F32).T.astype(BF16)
-        r.q[1024:, :] = qd[:, :HD]
-        r.do[1024:, :] = qd[:, HD:]
+        r.q[1024:, :] = r.qd_in[...].reshape(128, HD)
 
     def add_part(m):
         r.reorder[...] = dot(r.att[m * IMG : (m + 1) * IMG, :], r.nt[...], NT) + dot(
@@ -650,16 +669,34 @@
                     pl.ds(2 * n + k, PW, stride=PH), :
                 ].astype(BF16)
 
+    parts = Team(r.part, r.part_in, r.s_part)
+    e = parts.own
     attend_images(r, 1, 7 - g, text_ready)
     add_part(2)
     add_part(3)
+
+    @pl.loop(0, 16)
+    def _(o):
+        parts.push(16 + mod(e + o, 16))
+
     attend_images(r, 0, g, lambda: None)
     add_part(0)
     add_part(1)
 
-    e, _ = ring("team")
-    parts = Fan("team", r.part, r.part_in, r.s_part, lambda ty, to: to)
-    r.part_in[e] = r.part[e]
+    @pl.loop(0, 16)
+    def _(o):
+        parts.push(mod(e + o, 16))
+
+    parts.keep()
+
+    tgrad.arrived()
+    for n in range(8):
+        r.rows_grad[4 * n : 4 * n + 4, :] = r.tgrad_in[n].astype(F32)
+    outer = dot(r.rows_grad[...].astype(BF16), r.wo[...], NT)
+    for h in range(4):
+        r.d_out[h] = outer[:, h * HD : (h + 1) * HD].astype(BF16)
+    outers = Fan("group", r.d_out, r.d_in, r.s_do, lambda ty, to: to)
+    r.d_in[head] = r.d_out[head]
     attend_text(r, 8 - g, None)
     for m in range(4):
         r.att_txt[m] = r.att[1024 + m * TXT : 1024 + (m + 1) * TXT, :]
@@ -695,6 +732,8 @@
     def _(j):
         normalise(r.e_q.at[j], r.m_q.at[j], r.lse[2, :1, :HD])
 
+    outers.arrived()
+    r.do[1024:, :] = r.d_in[...].reshape(128, HD)
     backward_text(r, 8 - g)
 
     atx.arrived()
@@ -739,15 +778,18 @@
     heads_u.arrived()
     low_u = jnp.sum(r.low_u_in[...].astype(F32), axis=0).astype(BF16)
 
+    sums_u = Team(r.wide_u, r.wide_u_in, r.s_su)
+
     @pl.loop(0, 8)
-    def _(c):
+    def _(n):
+        c = mod(n + div(e, 4), 8)
         at = pl.ds(pl.multiple_of(c * 512, 512), 512)
         grad = dot(low_u[:, :HD], r.wo[mine, at]) + dot(low_u[:, HD : 2 * HD], r.dn[:, at])
         for k in range(4):
             r.wide_u[4 * c + k] = grad[:, k * HD : (k + 1) * HD].astype(BF16)
-
-    sums_u = Fan("team", r.wide_u, r.wide_u_in, r.s_su, lambda ty, to: to)
-    r.wide_u_in[e] = r.wide_u[e]
+            sums_u.push(4 * c + k)
+
+    sums_u.keep()
 
     backward_images(r, 1, 7 - g, members)
 
@@ -762,23 +804,32 @@
     conv_grad(r)
     convs = Fan("head", r.conv, r.conv_in, r.s_c1, lambda ty, to: to)
     r.conv_in[g] = r.conv[g]
+
+    @pl.loop(0, 8)
+    def _(c):
+        at = pl.ds(pl.multiple_of(c * 512, 512), 512)
+        r.base_d[:, at] = dot(low_u[:, 2 * HD :], r.up[at, :], NT)
+
     heads_d.arrived()
     low = jnp.sum(r.low_d_in[...].astype(F32), axis=0).astype(BF16)
 
+    sums_d = Team(r.wide_d, r.wide_d_in, r.s_sd)
+
     @pl.loop(0, 8)
-    def _(c):
+    def _(n):
+        c = mod(n + div(e, 4), 8)
         at = pl.ds(pl.multiple_of(c * 512, 512), 512)
         grad = dot(low[:, :HD], r.wq[at, mine], NT)
         grad = grad + dot(low[:, HD : 2 * HD], r.wk[at, mine], NT)
         grad = grad + dot(low[:, 2 * HD : 3 * HD], r.wv[at, mine], NT)
         grad = grad * r.gain_row[:, at]
-        grad = grad + dot(low_u[:, 2 * HD :], r.up[at, :], NT)
+        grad = grad + r.base_d[:, at]
         grad = grad - dot(low[:, 3 * HD :], r.dn[:, at])
         for k in range(4):
             r.wide_d[4 * c + k] = grad[:, k * HD : (k + 1) * HD].astype(BF16)
-
-    sums_d = Fan("team", r.wide_d, r.wide_d_in, r.s_sd, lambda ty, to: to)
-    r.wide_d_in[e] = r.wide_d[e]
+            sums_d.push(4 * c + k)
+
+    sums_d.keep()
     wide_u.slabs()
     convs.arrived()
     r.conv_a[...] = jnp.sum(r.conv_in[...].astype(F32), axis=0).astype(BF16)
@@ -820,6 +871,7 @@
         lats,
         kvs,
         qds,
+        outers,
         parts,
         atx,
         ups,
@@ -868,9 +920,9 @@
         "tgrad_in": ((8, 4, D), BF16),
         "own_off": ((8, HD), F32),
         "offs": ((16, 8, HD), F32),
-        "pad_lat": ((PH, 640), BF16),
+        "row_lat": ((PH, PW * CH), BF16),
         "rows_lat": ((PH, PW * CH), F32),
-        "lat_all": ((16, PH, 640), BF16),
+        "lat_all": ((16, PH, PW * CH), BF16),
         "rows_text": ((TXT, D), F32),
         "rows_grad": ((TXT, D), F32),
         "wd": ((HD, 256), BF16),
@@ -878,9 +930,11 @@
         "mix": ((HD, 384), BF16),
         "nt": ((HD, HD), BF16),
         "kv_out": ((4, TXT, 256), BF16),
-        "qd_out": ((4, TXT, 256), BF16),
+        "qd_out": ((4, TXT, HD), BF16),
         "kv_in": ((16, TXT, 256), BF16),
-        "qd_in": ((4, TXT, 256), BF16),
+        "qd_in": ((4, TXT, HD), BF16),
+        "d_out": ((4, TXT, HD), BF16),
+        "d_in": ((4, TXT, HD), BF16),
         "phase": ((2, 16, HD), F32),
         "bias_tt": ((512, 128), F32),
         "bias_ti": ((512, HD), F32),
@@ -932,6 +986,7 @@
         "low_d_in": ((4, 32, 512), BF16),
         "wide_u": ((32, 32, HD), BF16),
         "wide_u_in": ((32, 32, HD), BF16),
+        "base_d": ((32, D), F32),
         "wide_d": ((32, 32, HD), BF16),
         "wide_d_in": ((32, 32, HD), BF16),
         "mixed": ((8, 4, D), BF16),
@@ -946,7 +1001,7 @@
     }
     sems = {"local": (6,), "s_wide_u": (2, 8), "s_wide_d": (2, 8)}
     for name in (
-        ("lat", "off", "text", "tgrad", "lats", "kv", "qd", "part", "atx", "up", "hu", "su")
+        ("lat", "off", "text", "do", "tgrad", "lats", "kv", "qd", "part", "atx", "up", "hu", "su")
         + ("mix", "hd", "sd", "c1", "c2", "c3", "c4")
     ):
         sems["s_" + name] = (2,)

time: 118 us -> 108 us (0.915)
  Pallas kernels: 111 us -> 101 us
    pallas_call x1, Pallas kernels: 109 us -> 98.8 us  [whole(): pl.pallas_call(functools.partial(whole_kernel, names), out_shape=[sds(*v)...]
where the time goes in v5:
time: 108 us
  Pallas kernels  101 us (94%)
  local copies, waits for them, and re-layouts  5.5 us (5%)
  between operations  1.3 us (1%)
    pallas_call x1, Pallas kernels, whole(): pl.pallas_call(functools.partial(whole_kernel, names), out_shape=[sds(*v)...  98.8 us
    unnamed x12, local copies, waits for them, and re-layouts  5.5 us
    pallas_call x1, Pallas kernels, results(): pl.pallas_call(results_kernel, out_shape=shapes, in_specs=vmem(6), out_sp...  2.26 us

profile of v5, /device:TPU:1, one launch (start us, length us, event | category | flops | bytes accessed | tf_op | source)
XLA Modules:
  0.0 107.8 jit_solution(16530688800451918685)
XLA Ops:
  1.3 98.8 %shard_map.190 = (bf16[2,512]{1,0:T(2,128)(2,1)}, bf16[4,4096]{1,0:T(4,128)(2,1)}, bf16[128,4096]{1,0:T(8,128)(2,1)}, bf16[4096,128]{1,0:T(8,128)(2,1)}, f32[288,128]{1,0:T(8,128)}, /*index=5*/f32[32,128]{1,0:T(8,128)}) custom-call(s32[1]{0:T(128)S(6)} %copy.21.refs_0_, bf16[4,4096]{1,0:T(4,128)(2,1)} %bitcast.6, bf16[4,4096]{1,0:T(4,128)(2,1)} %bitcast.7, ...), custom_call_target="tpu_custom_call" | custom-call | tf_op jit(solution)/shard_map/pallas_call | solution.py:1014
  100.0 0.0 copy-start
  100.1 1.2 %copy-done = bf16[128,4096]{1,0:T(8,128)(2,1)S(1)} copy-done((bf16[128,4096]{1,0:T(8,128)(2,1)S(1)}, bf16[128,4096]{1,0:T(8,128)(2,1)}, u32[]{:S(2)}) %copy-start) | copy-done | bytes 1048600
  101.3 0.0 copy-start.1
  101.3 1.2 %copy-done.1 = bf16[4096,128]{1,0:T(8,128)(2,1)S(1)} copy-done((bf16[4096,128]{1,0:T(8,128)(2,1)S(1)}, bf16[4096,128]{1,0:T(8,128)(2,1)}, u32[]{:S(2)}) %copy-start.1) | copy-done | bytes 1048600
  102.5 0.0 copy-start.2
  102.5 0.9 copy-done.2
  103.4 0.0 copy-start.3
  103.4 0.8 copy-done.3
  104.2 0.0 copy-start.4
  104.2 0.7 copy-done.4
  104.9 0.0 copy-start.5
  104.9 0.7 copy-done.5
  105.6 2.3 %shard_map.191 = (bf16[1,2,512]{2,1,0:T(2,128)(2,1)}, bf16[1,4,4096]{2,1,0:T(4,128)(2,1)}, f32[128,4096]{1,0:T(8,128)}, f32[4096,128]{1,0:T(8,128)}, f32[288,128]{1,0:T(8,128)}, /*index=5*/f32[32,128]{1,0:T(8,128)}) custom-call(bf16[2,512]{1,0:T(2,128)(2,1)S(1)} %copy-done.5, bf16[4,4096]{1,0:T(4,128)(2,1)S(1)} %copy-done.3, bf16[128,4096]{1,0:T(8,128)(2,1)S(1)} %copy-done, ...), custom_call_target="tpu_custom_call" | custom-call | tf_op jit(solution)/shard_map/pallas_call | solution.py:1044
Async XLA Ops:
  100.0 1.2 %copy-start = (bf16[128,4096]{1,0:T(8,128)(2,1)S(1)}, bf16[128,4096]{1,0:T(8,128)(2,1)}, u32[]{:S(2)}) copy-start(bf16[128,4096]{1,0:T(8,128)(2,1)} %get-tuple-element.20.down) | copy-start | bytes 3145732
  101.3 1.2 %copy-start.1 = (bf16[4096,128]{1,0:T(8,128)(2,1)S(1)}, bf16[4096,128]{1,0:T(8,128)(2,1)}, u32[]{:S(2)}) copy-start(bf16[4096,128]{1,0:T(8,128)(2,1)} %get-tuple-element.21.up) | copy-start | bytes 3145732
  102.5 0.9 copy-start.2
  103.4 0.8 copy-start.3
  104.2 0.7 copy-start.4
  104.9 0.7 copy-start.5

commit v6 on v5

--- a/solution.py
+++ b/solution.py
@@ -599,6 +599,8 @@
 
     lat = Fan("sx", r.lat, r.lat_in, r.s_lat)
     text = Fan("sx", r.text, r.text_in, r.s_text)
+    offs = Fan("sy", r.own_off, r.offs, r.s_off)
+    r.offs[sy] = r.own_off[...]
     r.lat_in[sx] = r.lat[...]
     r.text_in[sx] = r.text[...]
 
@@ -608,9 +610,6 @@
     r.row_lat[...] = r.rows_lat[...].astype(BF16)
     lats = Fan("sy", r.row_lat, r.lat_all, r.s_lats)
     r.lat_all[sy] = r.row_lat[...]
-    offs = Fan("sy", r.own_off, r.offs, r.s_off)
-    r.offs[sy] = r.own_off[...]
-
     for n, weight in enumerate([r.wq, r.wk, r.wv]):
         loads[2 + n].wait()
         r.mix[:, n * HD : (n + 1) * HD] = dot(scaled, weight[:, mine]).astype(BF16)
@@ -736,19 +735,6 @@
     r.do[1024:, :] = r.d_in[...].reshape(128, HD)
     backward_text(r, 8 - g)
 
-    atx.arrived()
-    joined = jnp.concatenate([r.atx[h] for h in range(4)], axis=1)
-
-    @pl.loop(0, 8)
-    def _(c):
-        at = pl.ds(pl.multiple_of(c * 512, 512), 512)
-        out = dot(joined, r.wo[:, at])
-        for n in range(8):
-            r.mixed[n, :, at] = out[4 * n : 4 * n + 4, :].astype(BF16)
-
-    mixes = Fan("sx", r.mixed, r.mixed_in, r.s_mix, lambda ty, to: to)
-    r.mixed_in[sx] = r.mixed[sx]
-
     ups.arrived()
     for m in range(4):
         for n in range(8):
@@ -775,6 +761,16 @@
 
     backward_images(r, 0, g, members)
 
+    atx.arrived()
+    joined = jnp.concatenate([r.atx[h] for h in range(4)], axis=1)
+
+    @pl.loop(0, 8)
+    def _(c):
+        at = pl.ds(pl.multiple_of(c * 512, 512), 512)
+        out = dot(joined, r.wo[:, at])
+        for n in range(8):
+            r.mixed[n, :, at] = out[4 * n : 4 * n + 4, :].astype(BF16)
+
     heads_u.arrived()
     low_u = jnp.sum(r.low_u_in[...].astype(F32), axis=0).astype(BF16)
 
@@ -790,6 +786,8 @@
             sums_u.push(4 * c + k)
 
     sums_u.keep()
+    mixes = Fan("sx", r.mixed, r.mixed_in, r.s_mix, lambda ty, to: to)
+    r.mixed_in[sx] = r.mixed[sx]
 
     backward_images(r, 1, 7 - g, members)
 
@@ -1046,7 +1044,7 @@
         out_shape=shapes,
         in_specs=vmem(6),
         out_specs=vmem(6),
-        compiler_params=pltpu.CompilerParams(vmem_limit_bytes=32 * 2**20),
+        compiler_params=pltpu.CompilerParams(vmem_limit_bytes=60 * 2**20),
     )(*arrays)
 
 

time: 108 us -> 103 us (0.954)
  local copies, waits for them, and re-layouts: 5.5 us -> 0 us
    unnamed x12 -> x0, local copies, waits for them, and re-layouts: 5.5 us -> none
    pallas_call x1, Pallas kernels: 2.26 us -> 3.78 us  [results(): pl.pallas_call(results_kernel, out_shape=shapes, in_specs=vmem(6), out_sp...]
    pallas_call x1, Pallas kernels: 98.8 us -> 97.6 us  [whole(): pl.pallas_call(functools.partial(whole_kernel, names), out_shape=[sds(*v)...]
where the time goes in v6:
time: 103 us
  Pallas kernels  101 us (98%)
  between operations  1.29 us (1%)
    pallas_call x1, Pallas kernels, whole(): pl.pallas_call(functools.partial(whole_kernel, names), out_shape=[sds(*v)...  97.6 us
    pallas_call x1, Pallas kernels, results(): pl.pallas_call(results_kernel, out_shape=shapes, in_specs=vmem(6), out_sp...  3.78 us

profile of v6, /device:TPU:1, one launch (start us, length us, event | category | flops | bytes accessed | tf_op | source)
XLA Modules:
  0.0 102.6 jit_solution(12262691035070184813)
XLA Ops:
  1.3 97.6 %shard_map.190 = (bf16[2,512]{1,0:T(2,128)(2,1)}, bf16[4,4096]{1,0:T(4,128)(2,1)}, bf16[128,4096]{1,0:T(8,128)(2,1)}, bf16[4096,128]{1,0:T(8,128)(2,1)}, f32[288,128]{1,0:T(8,128)}, /*index=5*/f32[32,128]{1,0:T(8,128)}) custom-call(s32[1]{0:T(128)S(6)} %copy.21.refs_0_, bf16[4,4096]{1,0:T(4,128)(2,1)} %bitcast.6, bf16[4,4096]{1,0:T(4,128)(2,1)} %bitcast.7, ...), custom_call_target="tpu_custom_call" | custom-call | tf_op jit(solution)/shard_map/pallas_call | solution.py:1012
  98.9 3.8 %shard_map.191 = (bf16[1,2,512]{2,1,0:T(2,128)(2,1)}, bf16[1,4,4096]{2,1,0:T(4,128)(2,1)}, f32[128,4096]{1,0:T(8,128)}, f32[4096,128]{1,0:T(8,128)}, f32[288,128]{1,0:T(8,128)}, /*index=5*/f32[32,128]{1,0:T(8,128)}) custom-call(bf16[2,512]{1,0:T(2,128)(2,1)} %get-tuple-element.18.pred, bf16[4,4096]{1,0:T(4,128)(2,1)} %get-tuple-element.19.text, ...), custom_call_target="tpu_custom_call" | custom-call | tf_op jit(solution)/shard_map/pallas_call | solution.py:1042

commit v7 on v6

--- a/solution.py
+++ b/solution.py
@@ -799,6 +799,7 @@
         r.low_d[n] = r.small[32 * n : 32 * n + 32, :].astype(BF16)
     heads_d = Fan("head", r.low_d, r.low_d_in, r.s_hd, lambda ty, to: to)
     r.low_d_in[g] = r.low_d[g]
+    wide_u.slabs()
     conv_grad(r)
     convs = Fan("head", r.conv, r.conv_in, r.s_c1, lambda ty, to: to)
     r.conv_in[g] = r.conv[g]
@@ -828,7 +829,6 @@
             sums_d.push(4 * c + k)
 
     sums_d.keep()
-    wide_u.slabs()
     convs.arrived()
     r.conv_a[...] = jnp.sum(r.conv_in[...].astype(F32), axis=0).astype(BF16)
     beside = Fan("sx", r.conv_a, r.conv_sx, r.s_c2)
@@ -844,8 +844,8 @@
     r.conv_b[...] = jnp.sum(r.conv_sx[...].astype(F32), axis=0).astype(BF16)
     along = Fan("group", r.conv_b, r.conv_gr, r.s_c3)
     r.conv_gr[head] = r.conv_b[...]
+    wide_d.slabs()
     wide_u.pass_on()
-    wide_d.slabs()
     along.arrived()
     r.conv_c[...] = jnp.sum(r.conv_gr[...].astype(F32), axis=0).astype(BF16)
     across = Fan("head", r.conv_c, r.conv_all, r.s_c4)

time: 103 us -> 101 us (0.981)
  Pallas kernels: 101 us -> 99.8 us
    pallas_call x1, Pallas kernels: 97.6 us -> 96 us  [whole(): pl.pallas_call(functools.partial(whole_kernel, names), out_shape=[sds(*v)...]
where the time goes in v7:
time: 101 us
  Pallas kernels  99.8 us (99%)
  between operations  1.29 us (1%)
    pallas_call x1, Pallas kernels, whole(): pl.pallas_call(functools.partial(whole_kernel, names), out_shape=[sds(*v)...  96 us
    pallas_call x1, Pallas kernels, results(): pl.pallas_call(results_kernel, out_shape=shapes, in_specs=vmem(6), out_sp...  3.78 us

profile of v7, /device:TPU:1, one launch (start us, length us, event | category | flops | bytes accessed | tf_op | source)
XLA Modules:
  0.0 101.0 jit_solution(16007956208931761984)
XLA Ops:
  1.3 96.0 %shard_map.190 = (bf16[2,512]{1,0:T(2,128)(2,1)}, bf16[4,4096]{1,0:T(4,128)(2,1)}, bf16[128,4096]{1,0:T(8,128)(2,1)}, bf16[4096,128]{1,0:T(8,128)(2,1)}, f32[288,128]{1,0:T(8,128)}, /*index=5*/f32[32,128]{1,0:T(8,128)}) custom-call(s32[1]{0:T(128)S(6)} %copy.21.refs_0_, bf16[4,4096]{1,0:T(4,128)(2,1)} %bitcast.6, bf16[4,4096]{1,0:T(4,128)(2,1)} %bitcast.7, ...), custom_call_target="tpu_custom_call" | custom-call | tf_op jit(solution)/shard_map/pallas_call | solution.py:1012
  97.3 3.8 %shard_map.191 = (bf16[1,2,512]{2,1,0:T(2,128)(2,1)}, bf16[1,4,4096]{2,1,0:T(4,128)(2,1)}, f32[128,4096]{1,0:T(8,128)}, f32[4096,128]{1,0:T(8,128)}, f32[288,128]{1,0:T(8,128)}, /*index=5*/f32[32,128]{1,0:T(8,128)}) custom-call(bf16[2,512]{1,0:T(2,128)(2,1)} %get-tuple-element.18.pred, bf16[4,4096]{1,0:T(4,128)(2,1)} %get-tuple-element.19.text, ...), custom_call_target="tpu_custom_call" | custom-call | tf_op jit(solution)/shard_map/pallas_call | solution.py:1042
